TPU v7x, 256 devices: a whole 4x4x8 slice. The times are simulated.
256 devices in a mesh: dom: 16 (over z, core), st: 16 (over x, y).
Axes of the slice: x: 4, y: 4, z: 8, core: 2. Of those that a mesh axis runs over, the one named last changes fastest.
Arguments:
- inv_sqrt_blocks: bfloat16 [1024, 8, 128, 128], P('dom'), may hold values from -0.1875 to 0.1875
- waves: bfloat16 [512, 131072], P('st', 'dom'), may hold values from -0.59765625 to 0.59765625
- occupation: float32 [512], P('st'), may hold values from 0 to 2
- block_ref: int32 [1024, 8], P('dom'), may hold values from 0 to 127, as said below
- row_count: int32 [1024], P('dom'), may hold values from 2 to 8
- send_list: int32 [16, 4, 16], P('dom'), may hold values from 0 to 63
Outputs:
- density: float32 [1024, 8, 128, 128], P('dom', None, 'st')
Inputs may be any that keep to these rules, and one draw needn't show every extreme that they name: `block_ref`: slot 0 names the row's own block, slot 1 another block of the same domain, slots 2 and on codes 64 and above of blocks received from neighbouring domains.
All inputs are finite; a program needn't handle non-finite values.
Results may differ from a plain program's by a relative error of at most 0.0037.
Values may be sent and summed in bfloat16 or wider, within the bound.
No kernel may reach another device: no remote copies, remote signals or barrier semaphores. Data moves between devices by JAX's collectives and lax.ppermute only.
A program may use at most 192 MiB of HBM per device.

v0:
```python
import jax
import jax.numpy as jnp
from jax import lax
from jax.experimental import pallas as pl
from jax.experimental.pallas import tpu as pltpu
from jax.sharding import PartitionSpec as P

LIST = 144
PAIRS = 32 + LIST // 2
OFFSETS = (-2, -1, 1, 2)
SIDE = 4
BF16, F32 = jnp.bfloat16, jnp.float32


def params(mib=32):
    return pltpu.CompilerParams(vmem_limit_bytes=mib * 1024 * 1024)


def cost(flops, moved):
    return pl.CostEstimate(flops=flops, bytes_accessed=moved, transcendentals=0)


def along_dom(value, by):
    return lax.ppermute(value, "dom", [(i, (i + by) % 16) for i in range(16)])


def along_x(value, by):
    pairs = [(SIDE * x + y, SIDE * ((x + by) % SIDE) + y) for x in range(SIDE) for y in range(SIDE)]
    return lax.ppermute(value, "st", pairs)


def along_y(value, by):
    pairs = [(SIDE * x + y, SIDE * x + (y + by) % SIDE) for x in range(SIDE) for y in range(SIDE)]
    return lax.ppermute(value, "st", pairs)


def pick_waves(waves, send_list):
    def kernel(send_ref, waves_ref, *outs):
        for n in range(4):
            for j in range(16):
                block = send_ref[n, j]
                outs[n][j] = waves_ref[:, pl.ds(pl.multiple_of(block * 128, 128), 128)]

    piece = jax.ShapeDtypeStruct((16, 32, 128), BF16)
    return pl.pallas_call(
        kernel,
        out_shape=[piece] * 4,
        in_specs=[
            pl.BlockSpec(memory_space=pltpu.SMEM),
            pl.BlockSpec(memory_space=pltpu.VMEM),
        ],
        out_specs=[pl.BlockSpec(memory_space=pltpu.VMEM)] * 4,
        compiler_params=params(16),
        name="pick_waves",
    )(send_list, waves)


NT = (((1,), (1,)), ((), ()))
ROWS = 16
OWN_ROWS = 32


def coef_own(inv_sqrt_blocks, waves, block_ref):
    def kernel(ref_ref, blocks_ref, waves_ref, out_ref):
        step = pl.program_id(0)
        for b in range(OWN_ROWS):
            i = step * OWN_ROWS + b
            operand = jnp.concatenate(
                [
                    waves_ref[:, pl.ds(pl.multiple_of(ref_ref[i, k] * 128, 128), 128)]
                    for k in range(2)
                ],
                axis=1,
            )
            factor = jnp.concatenate([blocks_ref[b, 0], blocks_ref[b, 1]], axis=1)
            out_ref[b] = lax.dot_general(operand, factor, NT, preferred_element_type=F32)

    return pl.pallas_call(
        kernel,
        grid=(64 // OWN_ROWS,),
        out_shape=jax.ShapeDtypeStruct((64, 32, 128), F32),
        in_specs=[
            pl.BlockSpec(memory_space=pltpu.SMEM),
            pl.BlockSpec((OWN_ROWS, 2, 128, 128), lambda i: (i, 0, 0, 0)),
            pl.BlockSpec((32, 8192), lambda i: (0, 0)),
        ],
        out_specs=pl.BlockSpec((OWN_ROWS, 32, 128), lambda i: (i, 0, 0)),
        compiler_params=params(48),
        cost_estimate=cost(2 * 64 * 2 * 32 * 128 * 128, 6 * 1024 * 1024),
        name="coef_own",
    )(block_ref, inv_sqrt_blocks, waves)


def coef_all(inv_sqrt_blocks, first, pieces, block_ref, row_count, send_list, occupation):
    def kernel(
        ref_ref, count_ref, send_ref, blocks_1, blocks_2, blocks_3, first_ref, occ_ref,
        p0, p1, p2, p3, coef_ref, o0, o1, o2, o3, table,
    ):
        step = pl.program_id(0)

        @pl.when(step == 0)
        def _():
            for n, piece in enumerate((p0, p1, p2, p3)):
                table[16 * n : 16 * n + 16] = piece[...]
            lane = lax.broadcasted_iota(jnp.int32, (32, 128), 1)
            occ = jnp.broadcast_to(occ_ref[...], (32, 128))
            high = occ.astype(BF16).astype(F32)
            middle = (occ - high).astype(BF16).astype(F32)
            low = occ - high - middle
            parts = jnp.where(lane == 0, high, jnp.where(lane == 1, middle, low))
            coef_ref[64] = jnp.where(lane < 3, parts, 0.0).astype(BF16)

        for b in range(ROWS):
            i = step * ROWS + b
            operands, factors = [], []
            for slot in range(2, 8):
                block = table[jnp.clip(ref_ref[i, slot] - 64, 0, 63)]
                operands.append(jnp.where(slot < count_ref[0, i], block, jnp.zeros_like(block)))
                factors.append((blocks_1, blocks_2, blocks_3)[slot // 2 - 1][b, slot % 2])
            term = lax.dot_general(
                jnp.concatenate(factors, axis=1),
                jnp.concatenate(operands, axis=1),
                NT,
                preferred_element_type=F32,
            )
            coef_ref[i] = (first_ref[b] + term.T).astype(BF16)

        @pl.when(step == 64 // ROWS - 1)
        def _():
            for n, out in enumerate((o0, o1, o2, o3)):
                for j in range(16):
                    out[j] = coef_ref[send_ref[n, j]]

    piece = jax.ShapeDtypeStruct((16, 32, 128), BF16)
    whole = pl.BlockSpec((16, 32, 128), lambda i: (0, 0, 0))
    smem = pl.BlockSpec(memory_space=pltpu.SMEM)
    return pl.pallas_call(
        kernel,
        grid=(64 // ROWS,),
        out_shape=[jax.ShapeDtypeStruct((65, 32, 128), BF16)] + [piece] * 4,
        in_specs=[smem, smem, smem]
        + [pl.BlockSpec((ROWS, 2, 128, 128), lambda i, k=k: (i, k, 0, 0)) for k in (1, 2, 3)]
        + [
            pl.BlockSpec((ROWS, 32, 128), lambda i: (i, 0, 0)),
            pl.BlockSpec((32, 1), lambda i: (0, 0)),
        ]
        + [whole] * 4,
        out_specs=[pl.BlockSpec((65, 32, 128), lambda i: (0, 0, 0))] + [whole] * 4,
        scratch_shapes=[pltpu.VMEM((64, 32, 128), BF16)],
        compiler_params=params(48),
        cost_estimate=cost(2 * 64 * 6 * 32 * 128 * 128, 14 * 1024 * 1024),
        name="coef_all",
    )(
        block_ref, row_count, send_list, inv_sqrt_blocks, inv_sqrt_blocks, inv_sqrt_blocks,
        first, occupation, *pieces,
    )


def from_beside(value):
    return along_y(value, 1), along_y(value, -1), along_x(value, 1), along_x(value, -1)


def from_far(beside):
    lower_y, higher_y, lower_x, higher_x = beside
    far_y = along_y(lower_y[:32], 1), along_y(higher_y[32:], -1)
    far_x = along_x(lower_x[:32], 1), along_x(higher_x[32:], -1)
    return (lower_y, higher_y, *far_y), (lower_x, higher_x, *far_x)


def unite(table, pieces):
    own, lower, higher, far_0, far_1 = pieces
    for n, piece in enumerate((own, lower, higher)):
        table[:, 32 * n : 32 * n + 32] = piece[...]
    table[0:32, 96:128] = far_0[...]
    table[32 : table.shape[0], 96:128] = far_1[...]


HALF = jax.ShapeDtypeStruct((4, 32, 16, 128), BF16)
KEPT = jax.ShapeDtypeStruct((4, 32, 16, 128), F32)
PARTS = [KEPT, HALF, HALF, HALF]


def product(weighted, low, high):
    both = jnp.dot(weighted, jnp.concatenate([low, high], axis=1), preferred_element_type=F32)
    for t in range(4):
        rows = both[8 * t : 8 * t + 8]
        yield jnp.concatenate([rows[:, :128], rows[:, 128:]], axis=0)


def density_own(here, coef, gathered_y, gathered_x, block_ref):
    def kernel(here_ref, ref_ref, own, ly, hy, fy0, fy1, lx, hx, fx0, fx1, w_ref, *rest):
        outs, tables, turned = rest[:8], rest[8:10], rest[10]
        x, y = here_ref[0], here_ref[1]
        for v, pieces in enumerate(((own, ly, hy, fy0, fy1), (own, lx, hx, fx0, fx1))):
            table = tables[v]
            unite(table, pieces)
            split = table[64].astype(F32)
            occ = split[:, 0:1] + split[:, 1:2] + split[:, 2:3]

            for i in range(32):
                mine = table[32 * v + i]
                weighted = (occ * mine.astype(F32)).astype(BF16).astype(F32)
                turned[32 * v + i] = weighted.T

            for i in range(32):
                groups = []
                for t in range(4):
                    group = SIDE * lax.rem(x + t, SIDE) + y if v == 0 else SIDE * x + lax.rem(y + t, SIDE)
                    groups.append(turned[32 * v + i, pl.ds(pl.multiple_of(group * 8, 8), 8)])
                lhs = jnp.concatenate(groups, axis=0).astype(BF16)
                w_ref[32 * v + i] = lhs
                both = [table[jnp.clip(ref_ref[32 * v + i, k], 0, 63)] for k in range(2)]
                for t, part in enumerate(product(lhs, *both)):
                    outs[4 * v + t][0, i] = part.astype(outs[4 * v + t].dtype)

    smem, vmem = pl.BlockSpec(memory_space=pltpu.SMEM), pl.BlockSpec(memory_space=pltpu.VMEM)
    full = pl.BlockSpec((65, 32, 128), lambda i: (0, 0, 0))
    lower = pl.BlockSpec((32, 32, 128), lambda i: (0, 0, 0))
    upper = pl.BlockSpec((33, 32, 128), lambda i: (0, 0, 0))
    return pl.pallas_call(
        kernel,
        grid=(1,),
        out_shape=[jax.ShapeDtypeStruct((64, 32, 128), BF16)] + PARTS * 2,
        in_specs=[smem, smem, full] + [full, full, lower, upper] * 2,
        out_specs=[pl.BlockSpec((64, 32, 128), lambda i: (0, 0, 0))]
        + [pl.BlockSpec((1, 32, 16, 128), lambda i: (0, 0, 0, 0))] * 8,
        scratch_shapes=[
            pltpu.VMEM((65, 128, 128), BF16),
            pltpu.VMEM((65, 128, 128), BF16),
            pltpu.VMEM((64, 128, 128), F32),
        ],
        compiler_params=params(),
        cost_estimate=cost(2 * 64 * 2 * 128 * 32 * 128, 7 * 1024 * 1024),
        name="density_own",
    )(here, block_ref, coef, *gathered_y, *gathered_x)


def density_rest(weighted, halo, halo_y, halo_x, block_ref, begun):
    def kernel(ref_ref, w_ref, own, ly, hy, fy0, fy1, lx, hx, fx0, fx1, *rest):
        outs, tables = rest[8:16], rest[16:]
        pair = pl.program_id(0)

        @pl.when(pair == 0)
        def _():
            unite(tables[0], (own, ly, hy, fy0, fy1))
            unite(tables[1], (own, lx, hx, fx0, fx1))

        for v, table in enumerate(tables):
            for i in range(32):
                codes = [ref_ref[32 * v + i, 2 + 2 * pair + k] - 64 for k in range(2)]
                both = [table[jnp.clip(code, 0, 63)] for code in codes]
                for t, part in enumerate(product(w_ref[32 * v + i], *both)):
                    outs[4 * v + t][0, i] = part.astype(outs[4 * v + t].dtype)

    smem = pl.BlockSpec(memory_space=pltpu.SMEM)
    full = pl.BlockSpec((64, 32, 128), lambda i: (0, 0, 0))
    lower = pl.BlockSpec((32, 32, 128), lambda i: (0, 0, 0))
    return pl.pallas_call(
        kernel,
        grid=(3,),
        out_shape=PARTS * 2,
        in_specs=[smem, full, full] + [full, full, lower, lower] * 2 + [pl.BlockSpec(memory_space=pl.ANY)] * 8,
        out_specs=[pl.BlockSpec((1, 32, 16, 128), lambda i: (i + 1, 0, 0, 0))] * 8,
        scratch_shapes=[pltpu.VMEM((64, 128, 128), BF16)] * 2,
        input_output_aliases={11 + n: n for n in range(8)},
        compiler_params=params(),
        cost_estimate=cost(2 * 64 * 6 * 128 * 32 * 128, 10 * 1024 * 1024),
        name="density_rest",
    )(block_ref, weighted, halo, *halo_y, *halo_x, *begun)


def finish(parts, row_count):
    rows = 16

    def kernel(count_ref, *refs):
        ins, out_ref = refs[:8], refs[8]
        step = pl.program_id(0)
        for v in range(2):

            @pl.when(step // (32 // rows) == v)
            def _():
                for pair in range(4):
                    value = ins[4 * v][pair]
                    for t in range(1, 4):
                        value = value + ins[4 * v + t][pair].astype(F32)
                    for b in range(rows):
                        count = count_ref[0, step * rows + b]
                        for k in range(2):
                            part = value[b, 8 * k : 8 * k + 8]
                            out_ref[b, 2 * pair + k] = jnp.where(2 * pair + k < count, part, jnp.zeros_like(part))

    per = 32 // rows
    low = pl.BlockSpec((4, rows, 16, 128), lambda i: (0, jnp.minimum(i, per - 1), 0, 0))
    high = pl.BlockSpec((4, rows, 16, 128), lambda i: (0, jnp.maximum(i - per, 0), 0, 0))
    return pl.pallas_call(
        kernel,
        grid=(64 // rows,),
        out_shape=jax.ShapeDtypeStruct((64, 8, 8, 128), F32),
        in_specs=[pl.BlockSpec(memory_space=pltpu.SMEM)] + [low] * 4 + [high] * 4,
        out_specs=pl.BlockSpec((rows, 8, 8, 128), lambda i: (i, 0, 0, 0)),
        compiler_params=params(),
        cost_estimate=cost(0, 7 * 1024 * 1024),
        name="finish",
    )(row_count, *parts)


def plan(block_ref, row_count):
    room, none = 2 * PAIRS, 4 * PAIRS

    def kernel(ref_ref, count_ref, entry_ref, place_ref, over_ref):
        def clear(p, carry):
            entry_ref[0, p] = 0
            entry_ref[1, p] = 0
            return carry

        lax.fori_loop(0, LIST + 1, clear, 0, unroll=5)

        def row(i, lengths):
            count = count_ref[0, i]
            for k in range(2, 8):
                block = jnp.clip(ref_ref[i, k] - 64, 0, 63)
                which = block // 32
                long = jnp.where(which == 0, lengths[0], lengths[1])
                p = jnp.minimum(long, LIST)
                alive = (k < count).astype(jnp.int32)
                entry_ref[which, p] = i * 64 + block
                placed = (k < count) & (p < LIST)
                place_ref[i, k] = jnp.where(placed, which * room + 64 + p, none)
                lengths = (lengths[0] + alive * (1 - which), lengths[1] + alive * which)
            return lengths

        lengths = lax.fori_loop(0, 64, row, (jnp.int32(0), jnp.int32(0)), unroll=2)
        over_ref[0, 0] = (jnp.maximum(*lengths) > LIST).astype(jnp.int32)

    smem = pl.BlockSpec(memory_space=pltpu.SMEM)
    return pl.pallas_call(
        kernel,
        out_shape=[
            jax.ShapeDtypeStruct((2, LIST + 1), jnp.int32),
            jax.ShapeDtypeStruct((64, 8), jnp.int32),
            jax.ShapeDtypeStruct((1, 1), jnp.int32),
        ],
        in_specs=[smem, smem],
        out_specs=[smem] * 3,
        compiler_params=params(16),
        cost_estimate=cost(0, 24 * 1024 * 1024),
        name="plan",
    )(block_ref, row_count)


def targets(here_ref, v):
    x, y = here_ref[0], here_ref[1]
    for t in range(4):
        yield SIDE * lax.rem(x + t, SIDE) + y if v == 0 else SIDE * x + lax.rem(y + t, SIDE)


def weigh(v, here, shards, block_ref):
    def kernel(here_ref, ref_ref, own, lower, higher, far_0, far_1, w_ref, *rest):
        outs, table, turned = rest[:4], rest[4], rest[5]
        unite(table, (own, lower, higher, far_0, far_1))
        split = table[64].astype(F32)
        occ = split[:, 0:1] + split[:, 1:2] + split[:, 2:3]
        for i in range(64):
            turned[i] = (occ * table[i].astype(F32)).astype(BF16).astype(F32).T
        starts = [pl.multiple_of(group * 8, 8) for group in targets(here_ref, v)]
        for i in range(64):
            groups = [turned[i, pl.ds(start, 8)] for start in starts]
            w_ref[i] = jnp.concatenate(groups, axis=0).astype(BF16)
        for i in range(32):
            both = [table[jnp.clip(ref_ref[32 * v + i, k], 0, 63)] for k in range(2)]
            for t, part in enumerate(product(w_ref[32 * v + i], *both)):
                outs[t][i] = part.astype(outs[t].dtype)

    smem, vmem = pl.BlockSpec(memory_space=pltpu.SMEM), pl.BlockSpec(memory_space=pltpu.VMEM)
    part = (32, 16, 128)
    return pl.pallas_call(
        kernel,
        out_shape=[jax.ShapeDtypeStruct((64, 32, 128), BF16), jax.ShapeDtypeStruct(part, F32)]
        + [jax.ShapeDtypeStruct(part, BF16)] * 3,
        in_specs=[smem, smem] + [vmem] * 5,
        out_specs=[vmem] * 5,
        scratch_shapes=[pltpu.VMEM((65, 128, 128), BF16), pltpu.VMEM((64, 128, 128), F32)],
        compiler_params=params(16),
        cost_estimate=cost(64 * 2 * 128 * 32 * 128, 4 * 1024 * 1024),
        name=f"weigh_{v}",
    )(here, block_ref, *shards)


def density_list(v, entries, weighted, shards, begun):
    def kernel(entry_ref, w_ref, own, lower, higher, far, *rest):
        begun_refs, outs, table = rest[:4], rest[4:8], rest[8]
        for n, piece in enumerate((own, lower, higher, far)):
            table[:, 32 * n : 32 * n + 32] = piece[...]
        for begun_ref, out in zip(begun_refs, outs):
            out[0:32] = begun_ref[...]
        for p in range(0, LIST, 2):
            halves = []
            for q in range(2):
                entry = entry_ref[v, p + q]
                weight, block = w_ref[lax.shift_right_logical(entry, 6)], table[entry & 31]
                halves.append(jnp.dot(weight, block, preferred_element_type=F32))
            for t, out in enumerate(outs):
                pair = jnp.concatenate([half[8 * t : 8 * t + 8] for half in halves], axis=0)
                out[32 + p // 2] = pair.astype(out.dtype)

    smem, vmem = pl.BlockSpec(memory_space=pltpu.SMEM), pl.BlockSpec(memory_space=pltpu.VMEM)
    part = (PAIRS, 16, 128)
    return pl.pallas_call(
        kernel,
        out_shape=[jax.ShapeDtypeStruct(part, F32)] + [jax.ShapeDtypeStruct(part, BF16)] * 3,
        in_specs=[smem] + [vmem] * 9,
        out_specs=[vmem] * 4,
        scratch_shapes=[pltpu.VMEM((32, 128, 128), BF16)],
        compiler_params=params(16),
        cost_estimate=cost(LIST * 2 * 128 * 32 * 128, 4 * 1024 * 1024),
        name=f"density_list_{v}",
    )(entries, weighted, *shards, *begun)


def gather_up(parts, places):
    def kernel(place_ref, *refs):
        ins, out_ref, sums = refs[:8], refs[8], refs[9]
        for v in range(2):
            value = ins[4 * v][...]
            for t in range(1, 4):
                value = value + ins[4 * v + t][...].astype(F32)
            sums[2 * PAIRS * v : 2 * PAIRS * v + 2 * PAIRS] = value.reshape(2 * PAIRS, 8, 128)
        sums[4 * PAIRS] = jnp.zeros((8, 128), F32)
        for i in range(64):
            for k in range(2):
                out_ref[i, k] = sums[2 * PAIRS * (i // 32) + 2 * (i % 32) + k]
            for k in range(2, 8):
                out_ref[i, k] = sums[place_ref[i, k]]

    smem, vmem = pl.BlockSpec(memory_space=pltpu.SMEM), pl.BlockSpec(memory_space=pltpu.VMEM)
    return pl.pallas_call(
        kernel,
        out_shape=jax.ShapeDtypeStruct((64, 8, 8, 128), F32),
        in_specs=[smem] + [vmem] * 8,
        out_specs=vmem,
        scratch_shapes=[pltpu.VMEM((4 * PAIRS + 1, 8, 128), F32)],
        compiler_params=params(16),
        cost_estimate=cost(0, 7 * 1024 * 1024),
        name="gather_up",
    )(places, *parts)


def scattered(parts_x, parts_y):
    arrived = []
    for parts, along in ((parts_x, along_x), (parts_y, along_y)):
        arrived.append(parts[0])
        arrived += [along(parts[t], t) for t in range(1, 4)]
    return arrived


def any_way(coef, halo, here, block_ref, count):
    own_y, own_x = from_far(from_beside(coef))
    halo_y, halo_x = from_far(from_beside(halo))
    weighted, *begun = density_own(here, coef, own_y, own_x, block_ref)
    parts = density_rest(weighted, halo, halo_y, halo_x, block_ref, begun)
    return finish(scattered(parts[:4], parts[4:]), count)


def body(inv_sqrt_blocks, waves, occupation, block_ref, row_count, send_list):
    send = send_list[0]
    count = row_count.reshape(1, 64)
    st = lax.axis_index("st")
    here = jnp.stack([st // SIDE, st % SIDE]).astype(jnp.int32)

    picked = pick_waves(waves, send)
    pieces = [along_dom(p, offset) for p, offset in zip(picked, OFFSETS)]
    first = coef_own(inv_sqrt_blocks, waves, block_ref)
    entries, places, over = plan(block_ref, count)
    coef, *outgoing = coef_all(
        inv_sqrt_blocks, first, pieces, block_ref, count, send, occupation.reshape(32, 1)
    )
    beside = from_beside(coef)
    halos = [along_dom(p, offset) for p, offset in zip(outgoing, OFFSETS)]
    *beside, h0, h1, h2, h3 = lax.optimization_barrier((*beside, *halos))
    far_y, far_x = from_far(beside)
    own_y, own_x = [coef, *far_y], [coef, *far_x]
    half_y = jnp.concatenate([h0, h1], axis=0)
    half_x = jnp.concatenate([h2, h3], axis=0)
    half_y, half_x, *far = lax.optimization_barrier((half_y, half_x, *far_y, *far_x))
    own_y, own_x = [coef, *far[:4]], [coef, *far[4:]]
    halo_y = [half_y] + [along_y(half_y, by) for by in (1, -1, 2)]
    halo_x = [half_x] + [along_x(half_x, by) for by in (1, -1, 2)]
    weighted_y, *begun_y = weigh(0, here, own_y, block_ref)
    weighted_x, *begun_x = weigh(1, here, own_x, block_ref)
    *shards, entries, weighted_y, weighted_x = lax.optimization_barrier(
        (*halo_y[1:], *halo_x[1:], entries, weighted_y, weighted_x)
    )
    halo_y, halo_x = [half_y, *shards[:3]], [half_x, *shards[3:]]
    parts_x = density_list(0, entries, weighted_y, halo_y, begun_y)
    parts_y = density_list(1, entries, weighted_x, halo_x, begun_x)
    density = gather_up(scattered(parts_x, parts_y), places)

    def again(density, coef, halo, *rest):
        return any_way(coef, halo, *rest)

    def keep(density, *rest):
        return density

    halo = jnp.concatenate([half_y, half_x], axis=0)
    return lax.cond(over[0, 0] > 0, again, keep, density, coef, halo, here, block_ref, count)


def solution(mesh):
    in_specs = (
        P("dom", None, None, None),
        P("st", "dom"),
        P("st"),
        P("dom", None),
        P("dom"),
        P("dom", None, None),
    )
    out_specs = P("dom", None, "st", None)
    return jax.shard_map(body, mesh=mesh, in_specs=in_specs, out_specs=out_specs, check_vma=False)
```

profile of v0, /device:TPU:6, one launch (start us, length us, event | category | flops | bytes accessed | tf_op | source)
XLA Modules:
  0.0 134.6 jit_solution(14545419608986383879)
XLA Ops:
  2.4 5.9 %collective-permute-start.22 = (bf16[16,32,128]{2,1,0:T(8,128)(2,1)S(1)}, bf16[16,32,128]{2,1,0:T(8,128)(2,1)S(1)}, u32[]{:S(2)}, u32[]{:S(2)}) collective-permute-start(bf16[16,32,128]{2,1,0:T(8,128)(2,1)S(1)} %get-tuple-element.100), channel_id=1, source_target_pairs={{0,224},{16,240},{32,0},{48,16},{64,32},{80,48},{96,64},{112,80},{... | collective-permute-start | bytes 393224 | tf_op jit(solution)/shard_map/ppermute | solution.py:24
  12.1 3.3 %coef_own.1.first_ref = f32[64,32,128]{2,1,0:T(8,128)S(1)} custom-call(s32[64,8]{1,0:T(8,128)S(1)} %copy.17.ref_ref, bf16[64,8,128,128]{3,2,1,0:T(8,128)(2,1)} %blocks_3.1, bf16[32,8192]{1,0:T(8,128)(2,1)S(1)} %copy-done.1), custom_call_target="tpu_custom_call" | custom-call | flops 134217728 | bytes 6291456 | tf_op jit(solution)/shard_map/coef_own/pallas_call | solution.py:78
  16.5 7.2 %coef_all.1 = (bf16[65,32,128]{2,1,0:T(8,128)(2,1)S(1)}, bf16[16,32,128]{2,1,0:T(8,128)(2,1)S(1)}, bf16[16,32,128]{2,1,0:T(8,128)(2,1)S(1)}, bf16[16,32,128]{2,1,0:T(8,128)(2,1)S(1)}, bf16[16,32,128]{2,1,0:T(8,128)(2,1)S(1)}) custom-call(s32[64,8]{1,0:T(8,128)S(1)} %copy.17.ref_ref, s32[1,64]{1,0:T(1,128)S(1)} %bitcast.8, s32[4,16]{1,0:T(4,128)S(1)} %bitcast.7, ...), custom_call_target="tpu_custom_call" | custom-call | flops 402653184 | bytes 14680064 | tf_op jit(solution)/shard_map/coef_all/pallas_call | solution.py:137
  24.6 2.4 %collective-permute-start.28 = (bf16[65,32,128]{2,1,0:T(8,128)(2,1)S(1)}, bf16[65,32,128]{2,1,0:T(8,128)(2,1)S(1)}, u32[]{:S(2)}, u32[]{:S(2)}) collective-permute-start(bf16[65,32,128]{2,1,0:T(8,128)(2,1)S(1)} %get-tuple-element.104.own), channel_id=1, source_target_pairs={{0,4},{1,5},{2,6},{3,7},{4,8},{5,9},{6,10},{7,11},{8,12},{9,13},{1... | collective-permute-start | bytes 1597448 | tf_op jit(solution)/shard_map/ppermute | solution.py:29
  27.0 3.0 %collective-permute-start.27 = (bf16[65,32,128]{2,1,0:T(8,128)(2,1)S(1)}, bf16[65,32,128]{2,1,0:T(8,128)(2,1)S(1)}, u32[]{:S(2)}, u32[]{:S(2)}) collective-permute-start(bf16[65,32,128]{2,1,0:T(8,128)(2,1)S(1)} %get-tuple-element.104.own), channel_id=1, source_target_pairs={{0,3},{1,0},{2,1},{3,2},{4,7},{5,4},{6,5},{7,6},{8,11},{9,8},{10,9... | collective-permute-start | bytes 1597448 | tf_op jit(solution)/shard_map/ppermute | solution.py:34
  31.6 3.4 %collective-permute-done.30 = bf16[16,32,128]{2,1,0:T(8,128)(2,1)S(1)} collective-permute-done((bf16[16,32,128]{2,1,0:T(8,128)(2,1)S(1)}, bf16[16,32,128]{2,1,0:T(8,128)(2,1)S(1)}, u32[]{:S(2)}, u32[]{:S(2)}) %collective-permute-start.30) | collective-permute-done | bytes 131104 | tf_op jit(solution)/shard_map/ppermute | solution.py:24
  36.3 2.5 %collective-permute-done.31 = bf16[16,32,128]{2,1,0:T(8,128)(2,1)S(1)} collective-permute-done((bf16[16,32,128]{2,1,0:T(8,128)(2,1)S(1)}, bf16[16,32,128]{2,1,0:T(8,128)(2,1)S(1)}, u32[]{:S(2)}, u32[]{:S(2)}) %collective-permute-start.31) | collective-permute-done | bytes 131104 | tf_op jit(solution)/shard_map/ppermute | solution.py:24
  38.8 6.0 %collective-permute-done.32 = bf16[16,32,128]{2,1,0:T(8,128)(2,1)S(1)} collective-permute-done((bf16[16,32,128]{2,1,0:T(8,128)(2,1)S(1)}, bf16[16,32,128]{2,1,0:T(8,128)(2,1)S(1)}, u32[]{:S(2)}, u32[]{:S(2)}) %collective-permute-start.32) | collective-permute-done | bytes 131104 | tf_op jit(solution)/shard_map/ppermute | solution.py:24
  44.9 6.2 %collective-permute-done.33 = bf16[16,32,128]{2,1,0:T(8,128)(2,1)S(1)} collective-permute-done((bf16[16,32,128]{2,1,0:T(8,128)(2,1)S(1)}, bf16[16,32,128]{2,1,0:T(8,128)(2,1)S(1)}, u32[]{:S(2)}, u32[]{:S(2)}) %collective-permute-start.33) | collective-permute-done | bytes 131104 | tf_op jit(solution)/shard_map/ppermute | solution.py:24
  51.2 3.0 %collective-permute-start.35 = (bf16[33,32,128]{2,1,0:T(8,128)(2,1)S(1)}, bf16[33,32,128]{2,1,0:T(8,128)(2,1)S(1)}, u32[]{:S(2)}, u32[]{:S(2)}) collective-permute-start(bf16[33,32,128]{2,1,0:T(8,128)(2,1)S(1)} %slice.37), channel_id=1, source_target_pairs={{0,3},{1,0},{2,1},{3,2},{4,7},{5,4},{6,5},{7,6},{8,11},{9,8},{10,9... | collective-permute-start | bytes 811016 | tf_op jit(solution)/shard_map/ppermute | solution.py:34
  54.2 3.2 %collective-permute-start.36 = (bf16[32,32,128]{2,1,0:T(8,128)(2,1)S(1)}, bf16[32,32,128]{2,1,0:T(8,128)(2,1)S(1)}, u32[]{:S(2)}, u32[]{:S(2)}) collective-permute-start(bf16[32,32,128]{2,1,0:T(8,128)(2,1)S(1)} %slice.38), channel_id=1, source_target_pairs={{0,4},{1,5},{2,6},{3,7},{4,8},{5,9},{6,10},{7,11},{8,12},{9,13},{1... | collective-permute-start | bytes 786440 | tf_op jit(solution)/shard_map/ppermute | solution.py:29
  57.5 3.8 %collective-permute-done.36.far_0 = bf16[32,32,128]{2,1,0:T(8,128)(2,1)S(1)} collective-permute-done((bf16[32,32,128]{2,1,0:T(8,128)(2,1)S(1)}, bf16[32,32,128]{2,1,0:T(8,128)(2,1)S(1)}, u32[]{:S(2)}, u32[]{:S(2)}) %collective-permute-start.36) | collective-permute-done | bytes 262176 | tf_op jit(solution)/shard_map/ppermute | solution.py:29
  62.0 6.9 %collective-permute-done.34.far_0 = bf16[32,32,128]{2,1,0:T(8,128)(2,1)S(1)} collective-permute-done((bf16[32,32,128]{2,1,0:T(8,128)(2,1)S(1)}, bf16[32,32,128]{2,1,0:T(8,128)(2,1)S(1)}, u32[]{:S(2)}, u32[]{:S(2)}) %collective-permute-start.34) | collective-permute-done | bytes 262176 | tf_op jit(solution)/shard_map/ppermute | solution.py:34
  72.4 5.3 %collective-permute-done.40.far = bf16[32,32,128]{2,1,0:T(8,128)(2,1)S(1)} collective-permute-done((bf16[32,32,128]{2,1,0:T(8,128)(2,1)S(1)}, bf16[32,32,128]{2,1,0:T(8,128)(2,1)S(1)}, u32[]{:S(2)}, u32[]{:S(2)}) %collective-permute-start.40) | collective-permute-done | bytes 262176 | tf_op jit(solution)/shard_map/ppermute | solution.py:34
  77.7 7.9 %plan.1 = (s32[2,145]{1,0:T(2,128)S(1)}, s32[64,8]{1,0:T(8,128)S(1)}, s32[1,1]{1,0:T(1,128)}) custom-call(s32[64,8]{1,0:T(8,128)S(1)} %copy.17.ref_ref, s32[1,64]{1,0:T(1,128)S(1)} %bitcast.9), custom_call_target="tpu_custom_call" | custom-call | bytes 25165824 | tf_op jit(solution)/shard_map/plan/pallas_call | solution.py:336
  86.7 2.4 %weigh_0.1 = (bf16[64,32,128]{2,1,0:T(8,128)(2,1)S(1)}, f32[32,16,128]{2,1,0:T(8,128)S(1)}, bf16[32,16,128]{2,1,0:T(8,128)(2,1)S(1)}, bf16[32,16,128]{2,1,0:T(8,128)(2,1)S(1)}, bf16[32,16,128]{2,1,0:T(8,128)(2,1)S(1)}) custom-call(s32[2]{0:T(128)S(1)} %pad_add_fusion.here_ref, s32[64,8]{1,0:T(8,128)S(1)} %copy.17.ref_ref, bf16[65,32,128]{2,1,0:T(8,128)(2,1)} %copy-done.16, ...), custom_call_target="tpu_custom_call" | custom-call | flops 67108864 | bytes 4194304 | tf_op jit(solution)/shard_map/weigh_0/pallas_call | solution.py:376
  91.5 2.6 %density_list_1.1 = (f32[104,16,128]{2,1,0:T(8,128)S(1)}, bf16[104,16,128]{2,1,0:T(8,128)(2,1)S(1)}, bf16[104,16,128]{2,1,0:T(8,128)(2,1)S(1)}, bf16[104,16,128]{2,1,0:T(8,128)(2,1)S(1)}) custom-call(s32[2,145]{1,0:T(2,128)S(1)} %get-tuple-element.130.entry_ref, bf16[64,32,128]{2,1,0:T(8,128)(2,1)S(1)} %get-tuple-element.143.w_ref, ...), custom_call_target="tpu_custom_call" | custom-call | flops 150994944 | bytes 4194304 | tf_op jit(solution)/shard_map/density_list_1/pallas_call | solution.py:408
  95.3 2.5 %collective-permute-start.49 = (bf16[104,16,128]{2,1,0:T(8,128)(2,1)S(1)}, bf16[104,16,128]{2,1,0:T(8,128)(2,1)S(1)}, u32[]{:S(2)}, u32[]{:S(2)}) collective-permute-start(bf16[104,16,128]{2,1,0:T(8,128)(2,1)S(1)} %get-tuple-element.154), channel_id=1, source_target_pairs={{0,3},{1,0},{2,1},{3,2},{4,7},{5,4},{6,5},{7,6},{8,11},{9,8},{10,9... | collective-permute-start | bytes 1277960 | tf_op jit(solution)/shard_map/ppermute | solution.py:34
  97.9 2.5 %density_list_0.1 = (f32[104,16,128]{2,1,0:T(8,128)S(1)}, bf16[104,16,128]{2,1,0:T(8,128)(2,1)S(1)}, bf16[104,16,128]{2,1,0:T(8,128)(2,1)S(1)}, bf16[104,16,128]{2,1,0:T(8,128)(2,1)S(1)}) custom-call(s32[2,145]{1,0:T(2,128)S(1)} %get-tuple-element.130.entry_ref, bf16[64,32,128]{2,1,0:T(8,128)(2,1)S(1)} %get-tuple-element.131.w_ref, ...), custom_call_target="tpu_custom_call" | custom-call | flops 150994944 | bytes 4194304 | tf_op jit(solution)/shard_map/density_list_0/pallas_call | solution.py:408
  101.4 2.7 %collective-permute-start.45 = (bf16[104,16,128]{2,1,0:T(8,128)(2,1)S(1)}, bf16[104,16,128]{2,1,0:T(8,128)(2,1)S(1)}, u32[]{:S(2)}, u32[]{:S(2)}) collective-permute-start(bf16[104,16,128]{2,1,0:T(8,128)(2,1)S(1)} %get-tuple-element.141), channel_id=1, source_target_pairs={{0,8},{1,9},{2,10},{3,11},{4,12},{5,13},{6,14},{7,15},{8,0},{9,1},... | collective-permute-start | bytes 1277960 | tf_op jit(solution)/shard_map/ppermute | solution.py:29
  104.1 4.0 %collective-permute-done.47.refs_5_ = bf16[104,16,128]{2,1,0:T(8,128)(2,1)S(1)} collective-permute-done((bf16[104,16,128]{2,1,0:T(8,128)(2,1)S(1)}, bf16[104,16,128]{2,1,0:T(8,128)(2,1)S(1)}, u32[]{:S(2)}, u32[]{:S(2)}) %collective-permute-start.47) | collective-permute-done | bytes 426016 | tf_op jit(solution)/shard_map/ppermute | solution.py:34
  108.1 15.7 %collective-permute-start.46 = (bf16[104,16,128]{2,1,0:T(8,128)(2,1)S(1)}, bf16[104,16,128]{2,1,0:T(8,128)(2,1)S(1)}, u32[]{:S(2)}, u32[]{:S(2)}) collective-permute-start(bf16[104,16,128]{2,1,0:T(8,128)(2,1)S(1)} %get-tuple-element.142), channel_id=1, source_target_pairs={{0,12},{1,13},{2,14},{3,15},{4,0},{5,1},{6,2},{7,3},{8,4},{9,5},{1... | collective-permute-start | bytes 1277960 | tf_op jit(solution)/shard_map/ppermute | solution.py:29
  124.6 6.5 %collective-permute-done.46.refs_3_ = bf16[104,16,128]{2,1,0:T(8,128)(2,1)S(1)} collective-permute-done((bf16[104,16,128]{2,1,0:T(8,128)(2,1)S(1)}, bf16[104,16,128]{2,1,0:T(8,128)(2,1)S(1)}, u32[]{:S(2)}, u32[]{:S(2)}) %collective-permute-start.46) | collective-permute-done | bytes 426016 | tf_op jit(solution)/shard_map/ppermute | solution.py:29
  131.1 3.3 %gather_up.1 = f32[64,8,8,128]{3,2,1,0:T(8,128)} custom-call(s32[64,8]{1,0:T(8,128)S(1)} %get-tuple-element.99.place_ref, f32[104,16,128]{2,1,0:T(8,128)S(1)} %get-tuple-element.139.refs_0_, bf16[104,16,128]{2,1,0:T(8,128)(2,1)S(1)} %collective-permute-done.44.refs_1_, bf16[104,16,128]{2,1,0:T(8,128)(2,1)S(1)} %collective-permute-done.45.refs_2_, ...), custom_call_target="tpu_custom_call" | custom-call | bytes 7340032 | tf_op jit(solution)/shard_map/gather_up/pallas_call | solution.py:436
  (75 shorter events, 21.1 us)
Async XLA Ops:
  2.4 13.0 %collective-permute-start.22 = (bf16[16,32,128]{2,1,0:T(8,128)(2,1)S(1)}, bf16[16,32,128]{2,1,0:T(8,128)(2,1)S(1)}, u32[]{:S(2)}, u32[]{:S(2)}) collective-permute-start(bf16[16,32,128]{2,1,0:T(8,128)(2,1)S(1)} %get-tuple-element.100), channel_id=1, source_target_pairs={{0,224},{16,240},{32,0},{48,16},{64,32},{80,48},{96,64},{112,80},{... | collective-permute-start | bytes 393224 | tf_op jit(solution)/shard_map/ppermute | solution.py:24
  8.4 7.1 %collective-permute-start.23 = (bf16[16,32,128]{2,1,0:T(8,128)(2,1)S(1)}, bf16[16,32,128]{2,1,0:T(8,128)(2,1)S(1)}, u32[]{:S(2)}, u32[]{:S(2)}) collective-permute-start(bf16[16,32,128]{2,1,0:T(8,128)(2,1)S(1)} %get-tuple-element.101), channel_id=1, source_target_pairs={{0,240},{16,0},{32,16},{48,32},{64,48},{80,64},{96,80},{112,96},{1... | collective-permute-start | bytes 393224 | tf_op jit(solution)/shard_map/ppermute | solution.py:24
  8.5 6.9 %collective-permute-start.24 = (bf16[16,32,128]{2,1,0:T(8,128)(2,1)S(1)}, bf16[16,32,128]{2,1,0:T(8,128)(2,1)S(1)}, u32[]{:S(2)}, u32[]{:S(2)}) collective-permute-start(bf16[16,32,128]{2,1,0:T(8,128)(2,1)S(1)} %get-tuple-element.102), channel_id=1, source_target_pairs={{0,16},{16,32},{32,48},{48,64},{64,80},{80,96},{96,112},{112,128},... | collective-permute-start | bytes 393224 | tf_op jit(solution)/shard_map/ppermute | solution.py:24
  8.9 7.6 %collective-permute-start.25 = (bf16[16,32,128]{2,1,0:T(8,128)(2,1)S(1)}, bf16[16,32,128]{2,1,0:T(8,128)(2,1)S(1)}, u32[]{:S(2)}, u32[]{:S(2)}) collective-permute-start(bf16[16,32,128]{2,1,0:T(8,128)(2,1)S(1)} %get-tuple-element.103), channel_id=1, source_target_pairs={{0,32},{16,48},{32,64},{48,80},{64,96},{80,112},{96,128},{112,144}... | collective-permute-start | bytes 393224 | tf_op jit(solution)/shard_map/ppermute | solution.py:24
  23.7 27.3 %collective-permute-start.29 = (bf16[65,32,128]{2,1,0:T(8,128)(2,1)S(1)}, bf16[65,32,128]{2,1,0:T(8,128)(2,1)S(1)}, u32[]{:S(2)}, u32[]{:S(2)}) collective-permute-start(bf16[65,32,128]{2,1,0:T(8,128)(2,1)S(1)} %get-tuple-element.104.own), channel_id=1, source_target_pairs={{0,12},{1,13},{2,14},{3,15},{4,0},{5,1},{6,2},{7,3},{8,4},{9,5},{1... | collective-permute-start | bytes 1597448 | tf_op jit(solution)/shard_map/ppermute | solution.py:29
  24.6 26.4 %collective-permute-start.28 = (bf16[65,32,128]{2,1,0:T(8,128)(2,1)S(1)}, bf16[65,32,128]{2,1,0:T(8,128)(2,1)S(1)}, u32[]{:S(2)}, u32[]{:S(2)}) collective-permute-start(bf16[65,32,128]{2,1,0:T(8,128)(2,1)S(1)} %get-tuple-element.104.own), channel_id=1, source_target_pairs={{0,4},{1,5},{2,6},{3,7},{4,8},{5,9},{6,10},{7,11},{8,12},{9,13},{1... | collective-permute-start | bytes 1597448 | tf_op jit(solution)/shard_map/ppermute | solution.py:29
  27.0 24.0 %collective-permute-start.27 = (bf16[65,32,128]{2,1,0:T(8,128)(2,1)S(1)}, bf16[65,32,128]{2,1,0:T(8,128)(2,1)S(1)}, u32[]{:S(2)}, u32[]{:S(2)}) collective-permute-start(bf16[65,32,128]{2,1,0:T(8,128)(2,1)S(1)} %get-tuple-element.104.own), channel_id=1, source_target_pairs={{0,3},{1,0},{2,1},{3,2},{4,7},{5,4},{6,5},{7,6},{8,11},{9,8},{10,9... | collective-permute-start | bytes 1597448 | tf_op jit(solution)/shard_map/ppermute | solution.py:34
  30.0 21.0 %collective-permute-start.26 = (bf16[65,32,128]{2,1,0:T(8,128)(2,1)S(1)}, bf16[65,32,128]{2,1,0:T(8,128)(2,1)S(1)}, u32[]{:S(2)}, u32[]{:S(2)}) collective-permute-start(bf16[65,32,128]{2,1,0:T(8,128)(2,1)S(1)} %get-tuple-element.104.own), channel_id=1, source_target_pairs={{0,1},{1,2},{2,3},{3,0},{4,5},{5,6},{6,7},{7,4},{8,9},{9,10},{10,1... | collective-permute-start | bytes 1597448 | tf_op jit(solution)/shard_map/ppermute | solution.py:34
  51.1 18.5 %collective-permute-start.37 = (bf16[33,32,128]{2,1,0:T(8,128)(2,1)S(1)}, bf16[33,32,128]{2,1,0:T(8,128)(2,1)S(1)}, u32[]{:S(2)}, u32[]{:S(2)}) collective-permute-start(bf16[33,32,128]{2,1,0:T(8,128)(2,1)S(1)} %slice.39), channel_id=1, source_target_pairs={{0,12},{1,13},{2,14},{3,15},{4,0},{5,1},{6,2},{7,3},{8,4},{9,5},{1... | collective-permute-start | bytes 811016 | tf_op jit(solution)/shard_map/ppermute | solution.py:29
  51.2 18.5 %collective-permute-start.35 = (bf16[33,32,128]{2,1,0:T(8,128)(2,1)S(1)}, bf16[33,32,128]{2,1,0:T(8,128)(2,1)S(1)}, u32[]{:S(2)}, u32[]{:S(2)}) collective-permute-start(bf16[33,32,128]{2,1,0:T(8,128)(2,1)S(1)} %slice.37), channel_id=1, source_target_pairs={{0,3},{1,0},{2,1},{3,2},{4,7},{5,4},{6,5},{7,6},{8,11},{9,8},{10,9... | collective-permute-start | bytes 811016 | tf_op jit(solution)/shard_map/ppermute | solution.py:34
  54.2 7.1 %collective-permute-start.36 = (bf16[32,32,128]{2,1,0:T(8,128)(2,1)S(1)}, bf16[32,32,128]{2,1,0:T(8,128)(2,1)S(1)}, u32[]{:S(2)}, u32[]{:S(2)}) collective-permute-start(bf16[32,32,128]{2,1,0:T(8,128)(2,1)S(1)} %slice.38), channel_id=1, source_target_pairs={{0,4},{1,5},{2,6},{3,7},{4,8},{5,9},{6,10},{7,11},{8,12},{9,13},{1... | collective-permute-start | bytes 786440 | tf_op jit(solution)/shard_map/ppermute | solution.py:29
  57.4 11.5 %collective-permute-start.34 = (bf16[32,32,128]{2,1,0:T(8,128)(2,1)S(1)}, bf16[32,32,128]{2,1,0:T(8,128)(2,1)S(1)}, u32[]{:S(2)}, u32[]{:S(2)}) collective-permute-start(bf16[32,32,128]{2,1,0:T(8,128)(2,1)S(1)} %slice.36), channel_id=1, source_target_pairs={{0,1},{1,2},{2,3},{3,0},{4,5},{5,6},{6,7},{7,4},{8,9},{9,10},{10,1... | collective-permute-start | bytes 786440 | tf_op jit(solution)/shard_map/ppermute | solution.py:34
  69.7 8.0 %collective-permute-start.40 = (bf16[32,32,128]{2,1,0:T(8,128)(2,1)S(1)}, bf16[32,32,128]{2,1,0:T(8,128)(2,1)S(1)}, u32[]{:S(2)}, u32[]{:S(2)}) collective-permute-start(bf16[32,32,128]{2,1,0:T(8,128)(2,1)S(1)} %get-tuple-element.117.own), channel_id=1, source_target_pairs={{0,2},{1,3},{2,0},{3,1},{4,6},{5,7},{6,4},{7,5},{8,10},{9,11},{10,... | collective-permute-start | bytes 786440 | tf_op jit(solution)/shard_map/ppermute | solution.py:34
  69.7 21.8 %collective-permute-start.39 = (bf16[32,32,128]{2,1,0:T(8,128)(2,1)S(1)}, bf16[32,32,128]{2,1,0:T(8,128)(2,1)}, u32[]{:S(2)}, u32[]{:S(2)}) collective-permute-start(bf16[32,32,128]{2,1,0:T(8,128)(2,1)S(1)} %get-tuple-element.117.own), channel_id=1, source_target_pairs={{0,3},{1,0},{2,1},{3,2},{4,7},{5,4},{6,5},{7,6},{8,11},{9,8},{10,9... | collective-permute-start | bytes 786440 | tf_op jit(solution)/shard_map/ppermute | solution.py:34
  70.0 21.4 %collective-permute-start.38 = (bf16[32,32,128]{2,1,0:T(8,128)(2,1)S(1)}, bf16[32,32,128]{2,1,0:T(8,128)(2,1)}, u32[]{:S(2)}, u32[]{:S(2)}) collective-permute-start(bf16[32,32,128]{2,1,0:T(8,128)(2,1)S(1)} %get-tuple-element.117.own), channel_id=1, source_target_pairs={{0,1},{1,2},{2,3},{3,0},{4,5},{5,6},{6,7},{7,4},{8,9},{9,10},{10,1... | collective-permute-start | bytes 786440 | tf_op jit(solution)/shard_map/ppermute | solution.py:34
  72.0 19.4 %collective-permute-start.43 = (bf16[32,32,128]{2,1,0:T(8,128)(2,1)S(1)}, bf16[32,32,128]{2,1,0:T(8,128)(2,1)}, u32[]{:S(2)}, u32[]{:S(2)}) collective-permute-start(bf16[32,32,128]{2,1,0:T(8,128)(2,1)S(1)} %get-tuple-element.118.own), channel_id=1, source_target_pairs={{0,8},{1,9},{2,10},{3,11},{4,12},{5,13},{6,14},{7,15},{8,0},{9,1},... | collective-permute-start | bytes 786440 | tf_op jit(solution)/shard_map/ppermute | solution.py:29
  72.0 19.4 %collective-permute-start.42 = (bf16[32,32,128]{2,1,0:T(8,128)(2,1)S(1)}, bf16[32,32,128]{2,1,0:T(8,128)(2,1)}, u32[]{:S(2)}, u32[]{:S(2)}) collective-permute-start(bf16[32,32,128]{2,1,0:T(8,128)(2,1)S(1)} %get-tuple-element.118.own), channel_id=1, source_target_pairs={{0,12},{1,13},{2,14},{3,15},{4,0},{5,1},{6,2},{7,3},{8,4},{9,5},{1... | collective-permute-start | bytes 786440 | tf_op jit(solution)/shard_map/ppermute | solution.py:29
  77.7 13.8 %collective-permute-start.41 = (bf16[32,32,128]{2,1,0:T(8,128)(2,1)S(1)}, bf16[32,32,128]{2,1,0:T(8,128)(2,1)}, u32[]{:S(2)}, u32[]{:S(2)}) collective-permute-start(bf16[32,32,128]{2,1,0:T(8,128)(2,1)S(1)} %get-tuple-element.118.own), channel_id=1, source_target_pairs={{0,4},{1,5},{2,6},{3,7},{4,8},{5,9},{6,10},{7,11},{8,12},{9,13},{1... | collective-permute-start | bytes 786440 | tf_op jit(solution)/shard_map/ppermute | solution.py:29
  94.1 14.0 %collective-permute-start.47 = (bf16[104,16,128]{2,1,0:T(8,128)(2,1)S(1)}, bf16[104,16,128]{2,1,0:T(8,128)(2,1)S(1)}, u32[]{:S(2)}, u32[]{:S(2)}) collective-permute-start(bf16[104,16,128]{2,1,0:T(8,128)(2,1)S(1)} %get-tuple-element.152), channel_id=1, source_target_pairs={{0,1},{1,2},{2,3},{3,0},{4,5},{5,6},{6,7},{7,4},{8,9},{9,10},{10,1... | collective-permute-start | bytes 1277960 | tf_op jit(solution)/shard_map/ppermute | solution.py:34
  94.2 30.4 %collective-permute-start.48 = (bf16[104,16,128]{2,1,0:T(8,128)(2,1)S(1)}, bf16[104,16,128]{2,1,0:T(8,128)(2,1)S(1)}, u32[]{:S(2)}, u32[]{:S(2)}) collective-permute-start(bf16[104,16,128]{2,1,0:T(8,128)(2,1)S(1)} %get-tuple-element.153), channel_id=1, source_target_pairs={{0,2},{1,3},{2,0},{3,1},{4,6},{5,7},{6,4},{7,5},{8,10},{9,11},{10,... | collective-permute-start | bytes 1277960 | tf_op jit(solution)/shard_map/ppermute | solution.py:34
  95.3 29.2 %collective-permute-start.49 = (bf16[104,16,128]{2,1,0:T(8,128)(2,1)S(1)}, bf16[104,16,128]{2,1,0:T(8,128)(2,1)S(1)}, u32[]{:S(2)}, u32[]{:S(2)}) collective-permute-start(bf16[104,16,128]{2,1,0:T(8,128)(2,1)S(1)} %get-tuple-element.154), channel_id=1, source_target_pairs={{0,3},{1,0},{2,1},{3,2},{4,7},{5,4},{6,5},{7,6},{8,11},{9,8},{10,9... | collective-permute-start | bytes 1277960 | tf_op jit(solution)/shard_map/ppermute | solution.py:34
  100.3 24.2 %collective-permute-start.44 = (bf16[104,16,128]{2,1,0:T(8,128)(2,1)S(1)}, bf16[104,16,128]{2,1,0:T(8,128)(2,1)S(1)}, u32[]{:S(2)}, u32[]{:S(2)}) collective-permute-start(bf16[104,16,128]{2,1,0:T(8,128)(2,1)S(1)} %get-tuple-element.140), channel_id=1, source_target_pairs={{0,4},{1,5},{2,6},{3,7},{4,8},{5,9},{6,10},{7,11},{8,12},{9,13},{1... | collective-permute-start | bytes 1277960 | tf_op jit(solution)/shard_map/ppermute | solution.py:29
  101.4 23.2 %collective-permute-start.45 = (bf16[104,16,128]{2,1,0:T(8,128)(2,1)S(1)}, bf16[104,16,128]{2,1,0:T(8,128)(2,1)S(1)}, u32[]{:S(2)}, u32[]{:S(2)}) collective-permute-start(bf16[104,16,128]{2,1,0:T(8,128)(2,1)S(1)} %get-tuple-element.141), channel_id=1, source_target_pairs={{0,8},{1,9},{2,10},{3,11},{4,12},{5,13},{6,14},{7,15},{8,0},{9,1},... | collective-permute-start | bytes 1277960 | tf_op jit(solution)/shard_map/ppermute | solution.py:29
  108.1 23.1 %collective-permute-start.46 = (bf16[104,16,128]{2,1,0:T(8,128)(2,1)S(1)}, bf16[104,16,128]{2,1,0:T(8,128)(2,1)S(1)}, u32[]{:S(2)}, u32[]{:S(2)}) collective-permute-start(bf16[104,16,128]{2,1,0:T(8,128)(2,1)S(1)} %get-tuple-element.142), channel_id=1, source_target_pairs={{0,12},{1,13},{2,14},{3,15},{4,0},{5,1},{6,2},{7,3},{8,4},{9,5},{1... | collective-permute-start | bytes 1277960 | tf_op jit(solution)/shard_map/ppermute | solution.py:29
  (16 other events, 97.8 us)
where the time goes:
time: 137 us; the launch traced here: 135 us
  starting transfers between devices  48.5 us (35%)
  waiting for transfers between devices  45.7 us (33%)
  Pallas kernels  32.2 us (24%)
  local copies, waits for them, and re-layouts  6.73 us (5%)
    ppermute x10, starting transfers between devices, along_x(): return lax.ppermute(value, 'st', pairs)  26.4 us
    ppermute x8, waiting for transfers between devices, along_dom(): return lax.ppermute(value, 'dom', [(i, (i + by) % 16) for i in range(16)])  19.1 us
    ppermute x10, waiting for transfers between devices, along_y(): return lax.ppermute(value, 'st', pairs)  16.2 us
    ppermute x10, starting transfers between devices, along_y(): return lax.ppermute(value, 'st', pairs)  12.1 us
    ppermute x10, waiting for transfers between devices, along_x(): return lax.ppermute(value, 'st', pairs)  10.4 us
    ppermute x8, starting transfers between devices, along_dom(): return lax.ppermute(value, 'dom', [(i, (i + by) % 16) for i in range(16)])  10 us
    pallas_call x1, Pallas kernels, plan(): pl.pallas_call(kernel, out_shape=[jax.ShapeDtypeStruct((2, LIST + 1), jnp...  7.93 us
    pallas_call x1, Pallas kernels, coef_all(): pl.pallas_call(kernel, grid=(64 // ROWS,), out_shape=[jax.ShapeDtypeStruc...  7.25 us
  transfers between devices with their start and end apart: 28, of which 10 were waited for; matrix products, arithmetic and copies ran while one was open for 1% of the time, Pallas kernels for 14%

commit v1 on v0

--- a/solution.py
+++ b/solution.py
@@ -355,9 +355,10 @@
 
 
 def weigh(v, here, shards, block_ref):
-    def kernel(here_ref, ref_ref, own, lower, higher, far_0, far_1, w_ref, *rest):
+    def kernel(here_ref, ref_ref, own, lower, higher, far, w_ref, *rest):
         outs, table, turned = rest[:4], rest[4], rest[5]
-        unite(table, (own, lower, higher, far_0, far_1))
+        for n, piece in enumerate((own, lower, higher, far)):
+            table[:, 32 * n : 32 * n + 32] = piece[...]
         split = table[64].astype(F32)
         occ = split[:, 0:1] + split[:, 1:2] + split[:, 2:3]
         for i in range(64):
@@ -377,7 +378,7 @@
         kernel,
         out_shape=[jax.ShapeDtypeStruct((64, 32, 128), BF16), jax.ShapeDtypeStruct(part, F32)]
         + [jax.ShapeDtypeStruct(part, BF16)] * 3,
-        in_specs=[smem, smem] + [vmem] * 5,
+        in_specs=[smem, smem] + [vmem] * 4,
         out_specs=[vmem] * 5,
         scratch_shapes=[pltpu.VMEM((65, 128, 128), BF16), pltpu.VMEM((64, 128, 128), F32)],
         compiler_params=params(16),
@@ -474,15 +475,15 @@
     coef, *outgoing = coef_all(
         inv_sqrt_blocks, first, pieces, block_ref, count, send, occupation.reshape(32, 1)
     )
-    beside = from_beside(coef)
     halos = [along_dom(p, offset) for p, offset in zip(outgoing, OFFSETS)]
-    *beside, h0, h1, h2, h3 = lax.optimization_barrier((*beside, *halos))
-    far_y, far_x = from_far(beside)
-    own_y, own_x = [coef, *far_y], [coef, *far_x]
-    half_y = jnp.concatenate([h0, h1], axis=0)
-    half_x = jnp.concatenate([h2, h3], axis=0)
-    half_y, half_x, *far = lax.optimization_barrier((half_y, half_x, *far_y, *far_x))
-    own_y, own_x = [coef, *far[:4]], [coef, *far[4:]]
+    ready = [lax.optimization_barrier((coef, h)) for h in halos]
+    own_x = [coef, along_x(ready[2][0], 1), along_x(ready[3][0], -1), along_x(coef, 2)]
+    own_y = [coef, along_y(ready[1][0], 1), along_y(ready[3][0], -1), along_y(ready[0][0], 2)]
+    halos = [h for _, h in ready]
+    half_y, half_x, entries, *own = lax.optimization_barrier(
+        (jnp.concatenate(halos[:2], axis=0), jnp.concatenate(halos[2:], axis=0), entries, *own_y[1:], *own_x[1:])
+    )
+    own_y, own_x = [coef, *own[:3]], [coef, *own[3:]]
     halo_y = [half_y] + [along_y(half_y, by) for by in (1, -1, 2)]
     halo_x = [half_x] + [along_x(half_x, by) for by in (1, -1, 2)]
     weighted_y, *begun_y = weigh(0, here, own_y, block_ref)

time: 137 us -> 114 us (0.83)
  the two profiles are of different devices: /device:TPU:6 before, /device:TPU:107 now
where the time goes in v1:
time: 114 us
  waiting for transfers between devices  40.5 us (36%)
  starting transfers between devices  34.2 us (30%)
  Pallas kernels  32.2 us (28%)
  local copies, waits for them, and re-layouts  5.84 us (5%)
    ppermute x9, waiting for transfers between devices, along_x(): return lax.ppermute(value, 'st', pairs)  23.4 us
    ppermute x9, waiting for transfers between devices, along_y(): return lax.ppermute(value, 'st', pairs)  14 us
    ppermute x9, starting transfers between devices, along_y(): return lax.ppermute(value, 'st', pairs)  12.5 us
    ppermute x9, starting transfers between devices, along_x(): return lax.ppermute(value, 'st', pairs)  12.1 us
    ppermute x8, starting transfers between devices, along_dom(): return lax.ppermute(value, 'dom', [(i, (i + by) % 16) for i in range(16)])  9.65 us
    pallas_call x1, Pallas kernels, plan(): pl.pallas_call(kernel, out_shape=[jax.ShapeDtypeStruct((2, LIST + 1), jnp...  7.93 us
    pallas_call x1, Pallas kernels, coef_all(): pl.pallas_call(kernel, grid=(64 // ROWS,), out_shape=[jax.ShapeDtypeStruc...  7.26 us
    unnamed x25, local copies, waits for them, and re-layouts  5.11 us
  transfers between devices with their start and end apart: 26, of which 11 were waited for; matrix products, arithmetic and copies ran while one was open for 1% of the time, Pallas kernels for 16%

profile of v1, /device:TPU:107, one launch (start us, length us, event | category | flops | bytes accessed | tf_op | source)
XLA Modules:
  0.0 113.7 jit_solution(3512359665089254213)
XLA Ops:
  3.3 2.7 %collective-permute-start.24 = (bf16[16,32,128]{2,1,0:T(8,128)(2,1)S(1)}, bf16[16,32,128]{2,1,0:T(8,128)(2,1)S(1)}, u32[]{:S(2)}, u32[]{:S(2)}) collective-permute-start(bf16[16,32,128]{2,1,0:T(8,128)(2,1)S(1)} %get-tuple-element.101), channel_id=1, source_target_pairs={{0,16},{16,32},{32,48},{48,64},{64,80},{80,96},{96,112},{112,128},... | collective-permute-start | bytes 393224 | tf_op jit(solution)/shard_map/ppermute | solution.py:24
  6.0 1.6 %collective-permute-start.25 = (bf16[16,32,128]{2,1,0:T(8,128)(2,1)S(1)}, bf16[16,32,128]{2,1,0:T(8,128)(2,1)S(1)}, u32[]{:S(2)}, u32[]{:S(2)}) collective-permute-start(bf16[16,32,128]{2,1,0:T(8,128)(2,1)S(1)} %get-tuple-element.102), channel_id=1, source_target_pairs={{0,32},{16,48},{32,64},{48,80},{64,96},{80,112},{96,128},{112,144}... | collective-permute-start | bytes 393224 | tf_op jit(solution)/shard_map/ppermute | solution.py:24
  10.2 3.3 %coef_own.1.first_ref = f32[64,32,128]{2,1,0:T(8,128)S(1)} custom-call(s32[64,8]{1,0:T(8,128)S(1)} %copy.17.ref_ref, bf16[64,8,128,128]{3,2,1,0:T(8,128)(2,1)} %blocks_3.1, bf16[32,8192]{1,0:T(8,128)(2,1)S(1)} %copy-done.1), custom_call_target="tpu_custom_call" | custom-call | flops 134217728 | bytes 6291456 | tf_op jit(solution)/shard_map/coef_own/pallas_call | solution.py:78
  13.6 7.3 %coef_all.1 = (bf16[65,32,128]{2,1,0:T(8,128)(2,1)S(1)}, bf16[16,32,128]{2,1,0:T(8,128)(2,1)S(1)}, bf16[16,32,128]{2,1,0:T(8,128)(2,1)S(1)}, bf16[16,32,128]{2,1,0:T(8,128)(2,1)S(1)}, bf16[16,32,128]{2,1,0:T(8,128)(2,1)S(1)}) custom-call(s32[64,8]{1,0:T(8,128)S(1)} %copy.17.ref_ref, s32[1,64]{1,0:T(1,128)S(1)} %bitcast.8, s32[4,16]{1,0:T(4,128)S(1)} %bitcast.7, ...), custom_call_target="tpu_custom_call" | custom-call | flops 402653184 | bytes 14680064 | tf_op jit(solution)/shard_map/coef_all/pallas_call | solution.py:137
  20.8 1.9 %collective-permute-start.35 = (bf16[65,32,128]{2,1,0:T(8,128)(2,1)S(1)}, bf16[65,32,128]{2,1,0:T(8,128)(2,1)S(1)}, u32[]{:S(2)}, u32[]{:S(2)}) collective-permute-start(bf16[65,32,128]{2,1,0:T(8,128)(2,1)S(1)} %get-tuple-element.116.own), channel_id=1, source_target_pairs={{0,8},{1,9},{2,10},{3,11},{4,12},{5,13},{6,14},{7,15},{8,0},{9,1},... | collective-permute-start | bytes 1597448 | tf_op jit(solution)/shard_map/ppermute | solution.py:29
  24.4 2.8 %collective-permute-start.28 = (bf16[16,32,128]{2,1,0:T(8,128)(2,1)S(1)}, bf16[16,32,128]{2,1,0:T(8,128)(2,1)S(1)}, u32[]{:S(2)}, u32[]{:S(2)}) collective-permute-start(bf16[16,32,128]{2,1,0:T(8,128)(2,1)S(1)} %get-tuple-element.108), channel_id=1, source_target_pairs={{0,16},{16,32},{32,48},{48,64},{64,80},{80,96},{96,112},{112,128},... | collective-permute-start | bytes 393224 | tf_op jit(solution)/shard_map/ppermute | solution.py:24
  29.6 2.0 %collective-permute-done.27 = bf16[16,32,128]{2,1,0:T(8,128)(2,1)S(1)} collective-permute-done((bf16[16,32,128]{2,1,0:T(8,128)(2,1)S(1)}, bf16[16,32,128]{2,1,0:T(8,128)(2,1)S(1)}, u32[]{:S(2)}, u32[]{:S(2)}) %collective-permute-start.27) | collective-permute-done | bytes 131104 | tf_op jit(solution)/shard_map/ppermute | solution.py:24
  33.0 3.3 %collective-permute-done.35.far = bf16[65,32,128]{2,1,0:T(8,128)(2,1)S(1)} collective-permute-done((bf16[65,32,128]{2,1,0:T(8,128)(2,1)S(1)}, bf16[65,32,128]{2,1,0:T(8,128)(2,1)S(1)}, u32[]{:S(2)}, u32[]{:S(2)}) %collective-permute-start.35) | collective-permute-done | bytes 532512 | tf_op jit(solution)/shard_map/ppermute | solution.py:29
  36.3 2.3 %collective-permute-start.32 = (bf16[65,32,128]{2,1,0:T(8,128)(2,1)S(1)}, bf16[65,32,128]{2,1,0:T(8,128)(2,1)S(1)}, u32[]{:S(2)}, u32[]{:S(2)}) collective-permute-start(bf16[65,32,128]{2,1,0:T(8,128)(2,1)S(1)} %get-tuple-element.116.own), channel_id=1, source_target_pairs={{0,2},{1,3},{2,0},{3,1},{4,6},{5,7},{6,4},{7,5},{8,10},{9,11},{10,... | collective-permute-start | bytes 1597448 | tf_op jit(solution)/shard_map/ppermute | solution.py:34
  38.6 7.9 %plan.1 = (s32[2,145]{1,0:T(2,128)S(1)}, s32[64,8]{1,0:T(8,128)S(1)}, s32[1,1]{1,0:T(1,128)}) custom-call(s32[64,8]{1,0:T(8,128)S(1)} %copy.17.ref_ref, s32[1,64]{1,0:T(1,128)S(1)} %bitcast.9), custom_call_target="tpu_custom_call" | custom-call | bytes 25165824 | tf_op jit(solution)/shard_map/plan/pallas_call | solution.py:336
  47.8 6.3 %collective-permute-done.32.far = bf16[65,32,128]{2,1,0:T(8,128)(2,1)S(1)} collective-permute-done((bf16[65,32,128]{2,1,0:T(8,128)(2,1)S(1)}, bf16[65,32,128]{2,1,0:T(8,128)(2,1)S(1)}, u32[]{:S(2)}, u32[]{:S(2)}) %collective-permute-start.32) | collective-permute-done | bytes 532512 | tf_op jit(solution)/shard_map/ppermute | solution.py:34
  55.6 4.7 %collective-permute-start.37 = (bf16[32,32,128]{2,1,0:T(8,128)(2,1)S(1)}, bf16[32,32,128]{2,1,0:T(8,128)(2,1)}, u32[]{:S(2)}, u32[]{:S(2)}) collective-permute-start(bf16[32,32,128]{2,1,0:T(8,128)(2,1)S(1)} %get-tuple-element.117.own), channel_id=1, source_target_pairs={{0,3},{1,0},{2,1},{3,2},{4,7},{5,4},{6,5},{7,6},{8,11},{9,8},{10,9... | collective-permute-start | bytes 786440 | tf_op jit(solution)/shard_map/ppermute | solution.py:34
  61.5 3.0 %collective-permute-start.41 = (bf16[32,32,128]{2,1,0:T(8,128)(2,1)S(1)}, bf16[32,32,128]{2,1,0:T(8,128)(2,1)S(1)}, u32[]{:S(2)}, u32[]{:S(2)}) collective-permute-start(bf16[32,32,128]{2,1,0:T(8,128)(2,1)S(1)} %get-tuple-element.118.own), channel_id=1, source_target_pairs={{0,8},{1,9},{2,10},{3,11},{4,12},{5,13},{6,14},{7,15},{8,0},{9,1},... | collective-permute-start | bytes 786440 | tf_op jit(solution)/shard_map/ppermute | solution.py:29
  66.8 2.4 %weigh_1.1 = (bf16[64,32,128]{2,1,0:T(8,128)(2,1)S(1)}, f32[32,16,128]{2,1,0:T(8,128)S(1)}, bf16[32,16,128]{2,1,0:T(8,128)(2,1)S(1)}, bf16[32,16,128]{2,1,0:T(8,128)(2,1)S(1)}, bf16[32,16,128]{2,1,0:T(8,128)(2,1)S(1)}) custom-call(s32[2]{0:T(128)S(1)} %pad_add_fusion.here_ref, s32[64,8]{1,0:T(8,128)S(1)} %copy.17.ref_ref, bf16[65,32,128]{2,1,0:T(8,128)(2,1)} %copy-done.16, ...), custom_call_target="tpu_custom_call" | custom-call | flops 67108864 | bytes 4194304 | tf_op jit(solution)/shard_map/weigh_1/pallas_call | solution.py:377
  69.3 2.4 %weigh_0.1 = (bf16[64,32,128]{2,1,0:T(8,128)(2,1)S(1)}, f32[32,16,128]{2,1,0:T(8,128)S(1)}, bf16[32,16,128]{2,1,0:T(8,128)(2,1)S(1)}, bf16[32,16,128]{2,1,0:T(8,128)(2,1)S(1)}, bf16[32,16,128]{2,1,0:T(8,128)(2,1)S(1)}) custom-call(s32[2]{0:T(128)S(1)} %pad_add_fusion.here_ref, s32[64,8]{1,0:T(8,128)S(1)} %copy.17.ref_ref, ...), custom_call_target="tpu_custom_call" | custom-call | flops 67108864 | bytes 4194304 | tf_op jit(solution)/shard_map/weigh_0/pallas_call | solution.py:377
  71.7 5.3 %collective-permute-done.40.higher = bf16[32,32,128]{2,1,0:T(8,128)(2,1)} collective-permute-done((bf16[32,32,128]{2,1,0:T(8,128)(2,1)S(1)}, bf16[32,32,128]{2,1,0:T(8,128)(2,1)}, u32[]{:S(2)}, u32[]{:S(2)}) %collective-permute-start.40) | collective-permute-done | bytes 262176 | tf_op jit(solution)/shard_map/ppermute | solution.py:29
  77.0 2.5 %density_list_0.1 = (f32[104,16,128]{2,1,0:T(8,128)S(1)}, bf16[104,16,128]{2,1,0:T(8,128)(2,1)S(1)}, bf16[104,16,128]{2,1,0:T(8,128)(2,1)S(1)}, bf16[104,16,128]{2,1,0:T(8,128)(2,1)S(1)}) custom-call(s32[2,145]{1,0:T(2,128)S(1)} %get-tuple-element.128.entry_ref, bf16[64,32,128]{2,1,0:T(8,128)(2,1)S(1)} %get-tuple-element.129.w_ref, ...), custom_call_target="tpu_custom_call" | custom-call | flops 150994944 | bytes 4194304 | tf_op jit(solution)/shard_map/density_list_0/pallas_call | solution.py:409
  82.0 2.0 %collective-permute-start.44 = (bf16[104,16,128]{2,1,0:T(8,128)(2,1)S(1)}, bf16[104,16,128]{2,1,0:T(8,128)(2,1)S(1)}, u32[]{:S(2)}, u32[]{:S(2)}) collective-permute-start(bf16[104,16,128]{2,1,0:T(8,128)(2,1)S(1)} %get-tuple-element.140), channel_id=1, source_target_pairs={{0,12},{1,13},{2,14},{3,15},{4,0},{5,1},{6,2},{7,3},{8,4},{9,5},{1... | collective-permute-start | bytes 1277960 | tf_op jit(solution)/shard_map/ppermute | solution.py:29
  84.0 2.5 %density_list_1.1 = (f32[104,16,128]{2,1,0:T(8,128)S(1)}, bf16[104,16,128]{2,1,0:T(8,128)(2,1)S(1)}, bf16[104,16,128]{2,1,0:T(8,128)(2,1)S(1)}, bf16[104,16,128]{2,1,0:T(8,128)(2,1)S(1)}) custom-call(s32[2,145]{1,0:T(2,128)S(1)} %get-tuple-element.128.entry_ref, bf16[64,32,128]{2,1,0:T(8,128)(2,1)S(1)} %get-tuple-element.141.w_ref, ...), custom_call_target="tpu_custom_call" | custom-call | flops 150994944 | bytes 4194304 | tf_op jit(solution)/shard_map/density_list_1/pallas_call | solution.py:409
  88.6 1.6 %collective-permute-done.42.refs_1_ = bf16[104,16,128]{2,1,0:T(8,128)(2,1)S(1)} collective-permute-done((bf16[104,16,128]{2,1,0:T(8,128)(2,1)S(1)}, bf16[104,16,128]{2,1,0:T(8,128)(2,1)S(1)}, u32[]{:S(2)}, u32[]{:S(2)}) %collective-permute-start.42) | collective-permute-done | bytes 426016 | tf_op jit(solution)/shard_map/ppermute | solution.py:29
  90.8 1.5 %collective-permute-done.43.refs_2_ = bf16[104,16,128]{2,1,0:T(8,128)(2,1)S(1)} collective-permute-done((bf16[104,16,128]{2,1,0:T(8,128)(2,1)S(1)}, bf16[104,16,128]{2,1,0:T(8,128)(2,1)S(1)}, u32[]{:S(2)}, u32[]{:S(2)}) %collective-permute-start.43) | collective-permute-done | bytes 426016 | tf_op jit(solution)/shard_map/ppermute | solution.py:29
  92.3 10.4 %collective-permute-done.44.refs_3_ = bf16[104,16,128]{2,1,0:T(8,128)(2,1)S(1)} collective-permute-done((bf16[104,16,128]{2,1,0:T(8,128)(2,1)S(1)}, bf16[104,16,128]{2,1,0:T(8,128)(2,1)S(1)}, u32[]{:S(2)}, u32[]{:S(2)}) %collective-permute-start.44) | collective-permute-done | bytes 426016 | tf_op jit(solution)/shard_map/ppermute | solution.py:29
  102.8 7.6 %collective-permute-done.47.refs_7_ = bf16[104,16,128]{2,1,0:T(8,128)(2,1)S(1)} collective-permute-done((bf16[104,16,128]{2,1,0:T(8,128)(2,1)S(1)}, bf16[104,16,128]{2,1,0:T(8,128)(2,1)S(1)}, u32[]{:S(2)}, u32[]{:S(2)}) %collective-permute-start.47) | collective-permute-done | bytes 426016 | tf_op jit(solution)/shard_map/ppermute | solution.py:34
  110.4 3.3 %gather_up.1 = f32[64,8,8,128]{3,2,1,0:T(8,128)} custom-call(s32[64,8]{1,0:T(8,128)S(1)} %get-tuple-element.98.place_ref, f32[104,16,128]{2,1,0:T(8,128)S(1)} %get-tuple-element.137.refs_0_, bf16[104,16,128]{2,1,0:T(8,128)(2,1)S(1)} %collective-permute-done.42.refs_1_, bf16[104,16,128]{2,1,0:T(8,128)(2,1)S(1)} %collective-permute-done.43.refs_2_, ...), custom_call_target="tpu_custom_call" | custom-call | bytes 7340032 | tf_op jit(solution)/shard_map/gather_up/pallas_call | solution.py:437
  (67 shorter events, 22.1 us)
Async XLA Ops:
  2.4 11.1 %collective-permute-start.22 = (bf16[16,32,128]{2,1,0:T(8,128)(2,1)S(1)}, bf16[16,32,128]{2,1,0:T(8,128)(2,1)S(1)}, u32[]{:S(2)}, u32[]{:S(2)}) collective-permute-start(bf16[16,32,128]{2,1,0:T(8,128)(2,1)S(1)} %get-tuple-element.99), channel_id=1, source_target_pairs={{0,224},{16,240},{32,0},{48,16},{64,32},{80,48},{96,64},{112,80},{... | collective-permute-start | bytes 393224 | tf_op jit(solution)/shard_map/ppermute | solution.py:24
  2.5 11.0 %collective-permute-start.23 = (bf16[16,32,128]{2,1,0:T(8,128)(2,1)S(1)}, bf16[16,32,128]{2,1,0:T(8,128)(2,1)S(1)}, u32[]{:S(2)}, u32[]{:S(2)}) collective-permute-start(bf16[16,32,128]{2,1,0:T(8,128)(2,1)S(1)} %get-tuple-element.100), channel_id=1, source_target_pairs={{0,240},{16,0},{32,16},{48,32},{64,48},{80,64},{96,80},{112,96},{1... | collective-permute-start | bytes 393224 | tf_op jit(solution)/shard_map/ppermute | solution.py:24
  3.3 10.2 %collective-permute-start.24 = (bf16[16,32,128]{2,1,0:T(8,128)(2,1)S(1)}, bf16[16,32,128]{2,1,0:T(8,128)(2,1)S(1)}, u32[]{:S(2)}, u32[]{:S(2)}) collective-permute-start(bf16[16,32,128]{2,1,0:T(8,128)(2,1)S(1)} %get-tuple-element.101), channel_id=1, source_target_pairs={{0,16},{16,32},{32,48},{48,64},{64,80},{80,96},{96,112},{112,128},... | collective-permute-start | bytes 393224 | tf_op jit(solution)/shard_map/ppermute | solution.py:24
  6.0 7.5 %collective-permute-start.25 = (bf16[16,32,128]{2,1,0:T(8,128)(2,1)S(1)}, bf16[16,32,128]{2,1,0:T(8,128)(2,1)S(1)}, u32[]{:S(2)}, u32[]{:S(2)}) collective-permute-start(bf16[16,32,128]{2,1,0:T(8,128)(2,1)S(1)} %get-tuple-element.102), channel_id=1, source_target_pairs={{0,32},{16,48},{32,64},{48,80},{64,96},{80,112},{96,128},{112,144}... | collective-permute-start | bytes 393224 | tf_op jit(solution)/shard_map/ppermute | solution.py:24
  20.8 15.5 %collective-permute-start.35 = (bf16[65,32,128]{2,1,0:T(8,128)(2,1)S(1)}, bf16[65,32,128]{2,1,0:T(8,128)(2,1)S(1)}, u32[]{:S(2)}, u32[]{:S(2)}) collective-permute-start(bf16[65,32,128]{2,1,0:T(8,128)(2,1)S(1)} %get-tuple-element.116.own), channel_id=1, source_target_pairs={{0,8},{1,9},{2,10},{3,11},{4,12},{5,13},{6,14},{7,15},{8,0},{9,1},... | collective-permute-start | bytes 1597448 | tf_op jit(solution)/shard_map/ppermute | solution.py:29
  24.2 7.4 %collective-permute-start.27 = (bf16[16,32,128]{2,1,0:T(8,128)(2,1)S(1)}, bf16[16,32,128]{2,1,0:T(8,128)(2,1)S(1)}, u32[]{:S(2)}, u32[]{:S(2)}) collective-permute-start(bf16[16,32,128]{2,1,0:T(8,128)(2,1)S(1)} %get-tuple-element.106), channel_id=1, source_target_pairs={{0,240},{16,0},{32,16},{48,32},{64,48},{80,64},{96,80},{112,96},{1... | collective-permute-start | bytes 393224 | tf_op jit(solution)/shard_map/ppermute | solution.py:24
  24.4 7.3 %collective-permute-start.28 = (bf16[16,32,128]{2,1,0:T(8,128)(2,1)S(1)}, bf16[16,32,128]{2,1,0:T(8,128)(2,1)S(1)}, u32[]{:S(2)}, u32[]{:S(2)}) collective-permute-start(bf16[16,32,128]{2,1,0:T(8,128)(2,1)S(1)} %get-tuple-element.108), channel_id=1, source_target_pairs={{0,16},{16,32},{32,48},{48,64},{64,80},{80,96},{96,112},{112,128},... | collective-permute-start | bytes 393224 | tf_op jit(solution)/shard_map/ppermute | solution.py:24
  28.3 19.3 %collective-permute-start.34 = (bf16[65,32,128]{2,1,0:T(8,128)(2,1)S(1)}, bf16[65,32,128]{2,1,0:T(8,128)(2,1)S(1)}, u32[]{:S(2)}, u32[]{:S(2)}) collective-permute-start(bf16[65,32,128]{2,1,0:T(8,128)(2,1)S(1)} %get-tuple-element.116.own), channel_id=1, source_target_pairs={{0,12},{1,13},{2,14},{3,15},{4,0},{5,1},{6,2},{7,3},{8,4},{9,5},{1... | collective-permute-start | bytes 1597448 | tf_op jit(solution)/shard_map/ppermute | solution.py:29
  29.5 18.2 %collective-permute-start.31 = (bf16[65,32,128]{2,1,0:T(8,128)(2,1)S(1)}, bf16[65,32,128]{2,1,0:T(8,128)(2,1)S(1)}, u32[]{:S(2)}, u32[]{:S(2)}) collective-permute-start(bf16[65,32,128]{2,1,0:T(8,128)(2,1)S(1)} %get-tuple-element.116.own), channel_id=1, source_target_pairs={{0,3},{1,0},{2,1},{3,2},{4,7},{5,4},{6,5},{7,6},{8,11},{9,8},{10,9... | collective-permute-start | bytes 1597448 | tf_op jit(solution)/shard_map/ppermute | solution.py:34
  31.7 16.1 %collective-permute-start.33 = (bf16[65,32,128]{2,1,0:T(8,128)(2,1)S(1)}, bf16[65,32,128]{2,1,0:T(8,128)(2,1)S(1)}, u32[]{:S(2)}, u32[]{:S(2)}) collective-permute-start(bf16[65,32,128]{2,1,0:T(8,128)(2,1)S(1)} %get-tuple-element.116.own), channel_id=1, source_target_pairs={{0,4},{1,5},{2,6},{3,7},{4,8},{5,9},{6,10},{7,11},{8,12},{9,13},{1... | collective-permute-start | bytes 1597448 | tf_op jit(solution)/shard_map/ppermute | solution.py:29
  31.7 16.1 %collective-permute-start.30 = (bf16[65,32,128]{2,1,0:T(8,128)(2,1)S(1)}, bf16[65,32,128]{2,1,0:T(8,128)(2,1)S(1)}, u32[]{:S(2)}, u32[]{:S(2)}) collective-permute-start(bf16[65,32,128]{2,1,0:T(8,128)(2,1)S(1)} %get-tuple-element.116.own), channel_id=1, source_target_pairs={{0,1},{1,2},{2,3},{3,0},{4,5},{5,6},{6,7},{7,4},{8,9},{9,10},{10,1... | collective-permute-start | bytes 1597448 | tf_op jit(solution)/shard_map/ppermute | solution.py:34
  36.3 17.8 %collective-permute-start.32 = (bf16[65,32,128]{2,1,0:T(8,128)(2,1)S(1)}, bf16[65,32,128]{2,1,0:T(8,128)(2,1)S(1)}, u32[]{:S(2)}, u32[]{:S(2)}) collective-permute-start(bf16[65,32,128]{2,1,0:T(8,128)(2,1)S(1)} %get-tuple-element.116.own), channel_id=1, source_target_pairs={{0,2},{1,3},{2,0},{3,1},{4,6},{5,7},{6,4},{7,5},{8,10},{9,11},{10,... | collective-permute-start | bytes 1597448 | tf_op jit(solution)/shard_map/ppermute | solution.py:34
  54.9 9.9 %collective-permute-start.38 = (bf16[32,32,128]{2,1,0:T(8,128)(2,1)S(1)}, bf16[32,32,128]{2,1,0:T(8,128)(2,1)S(1)}, u32[]{:S(2)}, u32[]{:S(2)}) collective-permute-start(bf16[32,32,128]{2,1,0:T(8,128)(2,1)S(1)} %get-tuple-element.117.own), channel_id=1, source_target_pairs={{0,2},{1,3},{2,0},{3,1},{4,6},{5,7},{6,4},{7,5},{8,10},{9,11},{10,... | collective-permute-start | bytes 786440 | tf_op jit(solution)/shard_map/ppermute | solution.py:34
  55.6 16.0 %collective-permute-start.37 = (bf16[32,32,128]{2,1,0:T(8,128)(2,1)S(1)}, bf16[32,32,128]{2,1,0:T(8,128)(2,1)}, u32[]{:S(2)}, u32[]{:S(2)}) collective-permute-start(bf16[32,32,128]{2,1,0:T(8,128)(2,1)S(1)} %get-tuple-element.117.own), channel_id=1, source_target_pairs={{0,3},{1,0},{2,1},{3,2},{4,7},{5,4},{6,5},{7,6},{8,11},{9,8},{10,9... | collective-permute-start | bytes 786440 | tf_op jit(solution)/shard_map/ppermute | solution.py:34
  60.3 11.4 %collective-permute-start.36 = (bf16[32,32,128]{2,1,0:T(8,128)(2,1)S(1)}, bf16[32,32,128]{2,1,0:T(8,128)(2,1)}, u32[]{:S(2)}, u32[]{:S(2)}) collective-permute-start(bf16[32,32,128]{2,1,0:T(8,128)(2,1)S(1)} %get-tuple-element.117.own), channel_id=1, source_target_pairs={{0,1},{1,2},{2,3},{3,0},{4,5},{5,6},{6,7},{7,4},{8,9},{9,10},{10,1... | collective-permute-start | bytes 786440 | tf_op jit(solution)/shard_map/ppermute | solution.py:34
  61.5 10.2 %collective-permute-start.41 = (bf16[32,32,128]{2,1,0:T(8,128)(2,1)S(1)}, bf16[32,32,128]{2,1,0:T(8,128)(2,1)S(1)}, u32[]{:S(2)}, u32[]{:S(2)}) collective-permute-start(bf16[32,32,128]{2,1,0:T(8,128)(2,1)S(1)} %get-tuple-element.118.own), channel_id=1, source_target_pairs={{0,8},{1,9},{2,10},{3,11},{4,12},{5,13},{6,14},{7,15},{8,0},{9,1},... | collective-permute-start | bytes 786440 | tf_op jit(solution)/shard_map/ppermute | solution.py:29
  64.5 12.5 %collective-permute-start.40 = (bf16[32,32,128]{2,1,0:T(8,128)(2,1)S(1)}, bf16[32,32,128]{2,1,0:T(8,128)(2,1)}, u32[]{:S(2)}, u32[]{:S(2)}) collective-permute-start(bf16[32,32,128]{2,1,0:T(8,128)(2,1)S(1)} %get-tuple-element.118.own), channel_id=1, source_target_pairs={{0,12},{1,13},{2,14},{3,15},{4,0},{5,1},{6,2},{7,3},{8,4},{9,5},{1... | collective-permute-start | bytes 786440 | tf_op jit(solution)/shard_map/ppermute | solution.py:29
  65.5 11.5 %collective-permute-start.39 = (bf16[32,32,128]{2,1,0:T(8,128)(2,1)S(1)}, bf16[32,32,128]{2,1,0:T(8,128)(2,1)}, u32[]{:S(2)}, u32[]{:S(2)}) collective-permute-start(bf16[32,32,128]{2,1,0:T(8,128)(2,1)S(1)} %get-tuple-element.118.own), channel_id=1, source_target_pairs={{0,4},{1,5},{2,6},{3,7},{4,8},{5,9},{6,10},{7,11},{8,12},{9,13},{1... | collective-permute-start | bytes 786440 | tf_op jit(solution)/shard_map/ppermute | solution.py:29
  79.5 10.7 %collective-permute-start.42 = (bf16[104,16,128]{2,1,0:T(8,128)(2,1)S(1)}, bf16[104,16,128]{2,1,0:T(8,128)(2,1)S(1)}, u32[]{:S(2)}, u32[]{:S(2)}) collective-permute-start(bf16[104,16,128]{2,1,0:T(8,128)(2,1)S(1)} %get-tuple-element.138), channel_id=1, source_target_pairs={{0,4},{1,5},{2,6},{3,7},{4,8},{5,9},{6,10},{7,11},{8,12},{9,13},{1... | collective-permute-start | bytes 1277960 | tf_op jit(solution)/shard_map/ppermute | solution.py:29
  80.6 11.7 %collective-permute-start.43 = (bf16[104,16,128]{2,1,0:T(8,128)(2,1)S(1)}, bf16[104,16,128]{2,1,0:T(8,128)(2,1)S(1)}, u32[]{:S(2)}, u32[]{:S(2)}) collective-permute-start(bf16[104,16,128]{2,1,0:T(8,128)(2,1)S(1)} %get-tuple-element.139), channel_id=1, source_target_pairs={{0,8},{1,9},{2,10},{3,11},{4,12},{5,13},{6,14},{7,15},{8,0},{9,1},... | collective-permute-start | bytes 1277960 | tf_op jit(solution)/shard_map/ppermute | solution.py:29
  82.0 20.8 %collective-permute-start.44 = (bf16[104,16,128]{2,1,0:T(8,128)(2,1)S(1)}, bf16[104,16,128]{2,1,0:T(8,128)(2,1)S(1)}, u32[]{:S(2)}, u32[]{:S(2)}) collective-permute-start(bf16[104,16,128]{2,1,0:T(8,128)(2,1)S(1)} %get-tuple-element.140), channel_id=1, source_target_pairs={{0,12},{1,13},{2,14},{3,15},{4,0},{5,1},{6,2},{7,3},{8,4},{9,5},{1... | collective-permute-start | bytes 1277960 | tf_op jit(solution)/shard_map/ppermute | solution.py:29
  86.5 16.3 %collective-permute-start.45 = (bf16[104,16,128]{2,1,0:T(8,128)(2,1)S(1)}, bf16[104,16,128]{2,1,0:T(8,128)(2,1)S(1)}, u32[]{:S(2)}, u32[]{:S(2)}) collective-permute-start(bf16[104,16,128]{2,1,0:T(8,128)(2,1)S(1)} %get-tuple-element.150), channel_id=1, source_target_pairs={{0,1},{1,2},{2,3},{3,0},{4,5},{5,6},{6,7},{7,4},{8,9},{9,10},{10,1... | collective-permute-start | bytes 1277960 | tf_op jit(solution)/shard_map/ppermute | solution.py:34
  88.0 14.8 %collective-permute-start.46 = (bf16[104,16,128]{2,1,0:T(8,128)(2,1)S(1)}, bf16[104,16,128]{2,1,0:T(8,128)(2,1)S(1)}, u32[]{:S(2)}, u32[]{:S(2)}) collective-permute-start(bf16[104,16,128]{2,1,0:T(8,128)(2,1)S(1)} %get-tuple-element.151), channel_id=1, source_target_pairs={{0,2},{1,3},{2,0},{3,1},{4,6},{5,7},{6,4},{7,5},{8,10},{9,11},{10,... | collective-permute-start | bytes 1277960 | tf_op jit(solution)/shard_map/ppermute | solution.py:34
  90.2 20.2 %collective-permute-start.47 = (bf16[104,16,128]{2,1,0:T(8,128)(2,1)S(1)}, bf16[104,16,128]{2,1,0:T(8,128)(2,1)S(1)}, u32[]{:S(2)}, u32[]{:S(2)}) collective-permute-start(bf16[104,16,128]{2,1,0:T(8,128)(2,1)S(1)} %get-tuple-element.152), channel_id=1, source_target_pairs={{0,3},{1,0},{2,1},{3,2},{4,7},{5,4},{6,5},{7,6},{8,11},{9,8},{10,9... | collective-permute-start | bytes 1277960 | tf_op jit(solution)/shard_map/ppermute | solution.py:34
  (14 other events, 84.7 us)

commit v2 on v1

--- a/solution.py
+++ b/solution.py
@@ -358,7 +358,7 @@
     def kernel(here_ref, ref_ref, own, lower, higher, far, w_ref, *rest):
         outs, table, turned = rest[:4], rest[4], rest[5]
         for n, piece in enumerate((own, lower, higher, far)):
-            table[:, 32 * n : 32 * n + 32] = piece[...]
+            table[:, 32 * n : 32 * n + 32] = piece[0:65]
         split = table[64].astype(F32)
         occ = split[:, 0:1] + split[:, 1:2] + split[:, 2:3]
         for i in range(64):
@@ -391,7 +391,7 @@
     def kernel(entry_ref, w_ref, own, lower, higher, far, *rest):
         begun_refs, outs, table = rest[:4], rest[4:8], rest[8]
         for n, piece in enumerate((own, lower, higher, far)):
-            table[:, 32 * n : 32 * n + 32] = piece[...]
+            table[:, 32 * n : 32 * n + 32] = piece[piece.shape[0] - 32 :]
         for begun_ref, out in zip(begun_refs, outs):
             out[0:32] = begun_ref[...]
         for p in range(0, LIST, 2):
@@ -475,25 +475,20 @@
     coef, *outgoing = coef_all(
         inv_sqrt_blocks, first, pieces, block_ref, count, send, occupation.reshape(32, 1)
     )
-    halos = [along_dom(p, offset) for p, offset in zip(outgoing, OFFSETS)]
-    ready = [lax.optimization_barrier((coef, h)) for h in halos]
-    own_x = [coef, along_x(ready[2][0], 1), along_x(ready[3][0], -1), along_x(coef, 2)]
-    own_y = [coef, along_y(ready[1][0], 1), along_y(ready[3][0], -1), along_y(ready[0][0], 2)]
-    halos = [h for _, h in ready]
-    half_y, half_x, entries, *own = lax.optimization_barrier(
-        (jnp.concatenate(halos[:2], axis=0), jnp.concatenate(halos[2:], axis=0), entries, *own_y[1:], *own_x[1:])
-    )
-    own_y, own_x = [coef, *own[:3]], [coef, *own[3:]]
-    halo_y = [half_y] + [along_y(half_y, by) for by in (1, -1, 2)]
-    halo_x = [half_x] + [along_x(half_x, by) for by in (1, -1, 2)]
-    weighted_y, *begun_y = weigh(0, here, own_y, block_ref)
-    weighted_x, *begun_x = weigh(1, here, own_x, block_ref)
-    *shards, entries, weighted_y, weighted_x = lax.optimization_barrier(
-        (*halo_y[1:], *halo_x[1:], entries, weighted_y, weighted_x)
-    )
-    halo_y, halo_x = [half_y, *shards[:3]], [half_x, *shards[3:]]
-    parts_x = density_list(0, entries, weighted_y, halo_y, begun_y)
-    parts_y = density_list(1, entries, weighted_x, halo_x, begun_x)
+    halos = [along_dom(p, offset) for p, offset in zip(outgoing[:3], OFFSETS)]
+    halos[0], last = lax.optimization_barrier((halos[0], outgoing[3]))
+    halos.append(along_dom(last, OFFSETS[3]))
+    far_x = along_x(coef, 2)
+    half_y, half_x = jnp.concatenate(halos[:2], axis=0), jnp.concatenate(halos[2:], axis=0)
+    both_y, both_x = jnp.concatenate([coef, half_y], axis=0), jnp.concatenate([coef, half_x], axis=0)
+    beside = [along_y(both_y, 1), along_y(both_y, -1), along_x(both_x, 1), along_x(both_x, -1)]
+    far_y, half_far_x = along_y(both_y, 2), along_x(half_x, 2)
+    far_x, entries, *beside = lax.optimization_barrier((far_x, entries, *beside))
+    weighted_y, *begun_y = weigh(0, here, [coef, *beside[:2], far_y], block_ref)
+    weighted_x, *begun_x = weigh(1, here, [coef, *beside[2:], far_x], block_ref)
+    half_far_x, weighted_y, weighted_x = lax.optimization_barrier((half_far_x, weighted_y, weighted_x))
+    parts_x = density_list(0, entries, weighted_y, [half_y, *beside[:2], far_y], begun_y)
+    parts_y = density_list(1, entries, weighted_x, [half_x, *beside[2:], half_far_x], begun_x)
     density = gather_up(scattered(parts_x, parts_y), places)
 
     def again(density, coef, halo, *rest):

time: 114 us -> 124 us (1.088)
  the two profiles are of different devices: /device:TPU:107 before, /device:TPU:3 now
where the time goes in v2:
time: 124 us; the launch traced here: 123 us
  waiting for transfers between devices  49.1 us (40%)
  Pallas kernels  32.2 us (26%)
  starting transfers between devices  28.2 us (23%)
  local copies, waits for them, and re-layouts  12.5 us (10%)
    ppermute x6, waiting for transfers between devices, along_y(): return lax.ppermute(value, 'st', pairs)  39 us
    ppermute x8, starting transfers between devices, along_dom(): return lax.ppermute(value, 'dom', [(i, (i + by) % 16) for i in range(16)])  11 us
    ppermute x6, starting transfers between devices, along_y(): return lax.ppermute(value, 'st', pairs)  10.4 us
    unnamed x41, local copies, waits for them, and re-layouts  10.4 us
    pallas_call x1, Pallas kernels, plan(): pl.pallas_call(kernel, out_shape=[jax.ShapeDtypeStruct((2, LIST + 1), jnp...  7.93 us
    ppermute x7, waiting for transfers between devices, along_x(): return lax.ppermute(value, 'st', pairs)  7.87 us
    pallas_call x1, Pallas kernels, coef_all(): pl.pallas_call(kernel, grid=(64 // ROWS,), out_shape=[jax.ShapeDtypeStruc...  7.25 us
    ppermute x7, starting transfers between devices, along_x(): return lax.ppermute(value, 'st', pairs)  6.81 us
  transfers between devices with their start and end apart: 21, of which 7 were waited for; matrix products, arithmetic and copies ran while one was open for 6% of the time, Pallas kernels for 15%

profile of v2, /device:TPU:3, one launch (start us, length us, event | category | flops | bytes accessed | tf_op | source)
XLA Modules:
  0.0 123.1 jit_solution(15623013208662324811)
XLA Ops:
  2.4 5.7 %collective-permute-start.22 = (bf16[16,32,128]{2,1,0:T(8,128)(2,1)S(1)}, bf16[16,32,128]{2,1,0:T(8,128)(2,1)S(1)}, u32[]{:S(2)}, u32[]{:S(2)}) collective-permute-start(bf16[16,32,128]{2,1,0:T(8,128)(2,1)S(1)} %get-tuple-element.84), channel_id=1, source_target_pairs={{0,224},{16,240},{32,0},{48,16},{64,32},{80,48},{96,64},{112,80},{... | collective-permute-start | bytes 393224 | tf_op jit(solution)/shard_map/ppermute | solution.py:24
  12.4 3.3 %coef_own.1.first_ref = f32[64,32,128]{2,1,0:T(8,128)S(1)} custom-call(s32[64,8]{1,0:T(8,128)S(1)} %copy.17.ref_ref, bf16[64,8,128,128]{3,2,1,0:T(8,128)(2,1)} %blocks_3.1, bf16[32,8192]{1,0:T(8,128)(2,1)S(1)} %copy-done.1), custom_call_target="tpu_custom_call" | custom-call | flops 134217728 | bytes 6291456 | tf_op jit(solution)/shard_map/coef_own/pallas_call | solution.py:78
  15.7 1.2 collective-permute-done.25.p3
  16.9 7.3 %coef_all.1 = (bf16[65,32,128]{2,1,0:T(8,128)(2,1)S(1)}, bf16[16,32,128]{2,1,0:T(8,128)(2,1)S(1)}, bf16[16,32,128]{2,1,0:T(8,128)(2,1)S(1)}, bf16[16,32,128]{2,1,0:T(8,128)(2,1)S(1)}, bf16[16,32,128]{2,1,0:T(8,128)(2,1)S(1)}) custom-call(s32[64,8]{1,0:T(8,128)S(1)} %copy.17.ref_ref, s32[1,64]{1,0:T(1,128)S(1)} %bitcast.8, s32[4,16]{1,0:T(4,128)S(1)} %bitcast.7, ...), custom_call_target="tpu_custom_call" | custom-call | flops 402653184 | bytes 14680064 | tf_op jit(solution)/shard_map/coef_all/pallas_call | solution.py:137
  24.2 1.6 %collective-permute-start.27 = (bf16[16,32,128]{2,1,0:T(8,128)(2,1)S(1)}, bf16[16,32,128]{2,1,0:T(8,128)(2,1)S(1)}, u32[]{:S(2)}, u32[]{:S(2)}) collective-permute-start(bf16[16,32,128]{2,1,0:T(8,128)(2,1)S(1)} %get-tuple-element.90), channel_id=1, source_target_pairs={{0,224},{16,240},{32,0},{48,16},{64,32},{80,48},{96,64},{112,80},{... | collective-permute-start | bytes 393224 | tf_op jit(solution)/shard_map/ppermute | solution.py:24
  26.1 1.8 %collective-permute-start.26 = (bf16[65,32,128]{2,1,0:T(8,128)(2,1)S(1)}, bf16[65,32,128]{2,1,0:T(8,128)(2,1)S(1)}, u32[]{:S(2)}, u32[]{:S(2)}) collective-permute-start(bf16[65,32,128]{2,1,0:T(8,128)(2,1)S(1)} %get-tuple-element.88.own), channel_id=1, source_target_pairs={{0,8},{1,9},{2,10},{3,11},{4,12},{5,13},{6,14},{7,15},{8,0},{9,1},... | collective-permute-start | bytes 1597448 | tf_op jit(solution)/shard_map/ppermute | solution.py:29
  28.7 1.7 %collective-permute-start.31 = (bf16[16,32,128]{2,1,0:T(8,128)(2,1)S(1)}, bf16[16,32,128]{2,1,0:T(8,128)(2,1)S(1)}, u32[]{:S(2)}, u32[]{:S(2)}) collective-permute-start(bf16[16,32,128]{2,1,0:T(8,128)(2,1)S(1)} %get-tuple-element.94), channel_id=1, source_target_pairs={{0,16},{16,32},{32,48},{48,64},{64,80},{80,96},{96,112},{112,128},... | collective-permute-start | bytes 393224 | tf_op jit(solution)/shard_map/ppermute | solution.py:24
  30.5 2.1 %copy.34 = bf16[97,32,128]{2,1,0:T(8,128)(2,1)} copy(bf16[97,32,128]{2,1,0:T(8,128)(2,1)} %constant_dynamic-update-slice_fusion.2) | data formatting | bytes 1589248
  34.6 2.7 %collective-permute-start.30 = (bf16[97,32,128]{2,1,0:T(8,128)(2,1)}, bf16[97,32,128]{2,1,0:T(8,128)(2,1)S(1)}, u32[]{:S(2)}, u32[]{:S(2)}) collective-permute-start(bf16[97,32,128]{2,1,0:T(8,128)(2,1)} %constant_dynamic-update-slice_fusion), channel_id=1, source_target_pairs={{0,3},{1,0},{2,1},{3,2},{4,7},{5,4},{6,5},{7,6},{8,11},{9,8},{10,9... | collective-permute-start | bytes 2383880 | tf_op jit(solution)/shard_map/ppermute | solution.py:34
  39.7 1.3 %collective-permute-start.34 = (bf16[97,32,128]{2,1,0:T(8,128)(2,1)}, bf16[97,32,128]{2,1,0:T(8,128)(2,1)S(1)}, u32[]{:S(2)}, u32[]{:S(2)}) collective-permute-start(bf16[97,32,128]{2,1,0:T(8,128)(2,1)} %get-tuple-element.130), channel_id=1, source_target_pairs={{0,12},{1,13},{2,14},{3,15},{4,0},{5,1},{6,2},{7,3},{8,4},{9,5},{1... | collective-permute-start | bytes 2383880 | tf_op jit(solution)/shard_map/ppermute | solution.py:29
  42.0 2.9 %collective-permute-start.36 = (bf16[97,32,128]{2,1,0:T(8,128)(2,1)}, bf16[97,32,128]{2,1,0:T(8,128)(2,1)S(1)}, u32[]{:S(2)}, u32[]{:S(2)}) collective-permute-start(bf16[97,32,128]{2,1,0:T(8,128)(2,1)} %constant_dynamic-update-slice_fusion), channel_id=1, source_target_pairs={{0,2},{1,3},{2,0},{3,1},{4,6},{5,7},{6,4},{7,5},{8,10},{9,11},{10,... | collective-permute-start | bytes 2383880 | tf_op jit(solution)/shard_map/ppermute | solution.py:34
  44.9 26.4 %collective-permute-done.30.higher = bf16[97,32,128]{2,1,0:T(8,128)(2,1)S(1)} collective-permute-done((bf16[97,32,128]{2,1,0:T(8,128)(2,1)}, bf16[97,32,128]{2,1,0:T(8,128)(2,1)S(1)}, u32[]{:S(2)}, u32[]{:S(2)}) %collective-permute-start.30) | collective-permute-done | bytes 794656 | tf_op jit(solution)/shard_map/ppermute | solution.py:34
  71.2 1.1 collective-permute-start.35
  72.4 7.9 %plan.1 = (s32[2,145]{1,0:T(2,128)S(1)}, s32[64,8]{1,0:T(8,128)S(1)}, s32[1,1]{1,0:T(1,128)}) custom-call(s32[64,8]{1,0:T(8,128)S(1)} %copy.17.ref_ref, s32[1,64]{1,0:T(1,128)S(1)} %bitcast.9), custom_call_target="tpu_custom_call" | custom-call | bytes 25165824 | tf_op jit(solution)/shard_map/plan/pallas_call | solution.py:336
  81.5 2.7 %weigh_1.1 = (bf16[64,32,128]{2,1,0:T(8,128)(2,1)S(1)}, f32[32,16,128]{2,1,0:T(8,128)S(1)}, bf16[32,16,128]{2,1,0:T(8,128)(2,1)S(1)}, bf16[32,16,128]{2,1,0:T(8,128)(2,1)S(1)}, bf16[32,16,128]{2,1,0:T(8,128)(2,1)S(1)}) custom-call(s32[2]{0:T(128)S(1)} %pad_add_fusion.here_ref, s32[64,8]{1,0:T(8,128)S(1)} %copy.17.ref_ref, bf16[65,32,128]{2,1,0:T(8,128)(2,1)} %copy-done.14, ...), custom_call_target="tpu_custom_call" | custom-call | flops 67108864 | bytes 4194304 | tf_op jit(solution)/shard_map/weigh_1/pallas_call | solution.py:377
  84.2 2.3 %weigh_0.1 = (bf16[64,32,128]{2,1,0:T(8,128)(2,1)S(1)}, f32[32,16,128]{2,1,0:T(8,128)S(1)}, bf16[32,16,128]{2,1,0:T(8,128)(2,1)S(1)}, bf16[32,16,128]{2,1,0:T(8,128)(2,1)S(1)}, bf16[32,16,128]{2,1,0:T(8,128)(2,1)S(1)}) custom-call(s32[2]{0:T(128)S(1)} %pad_add_fusion.here_ref, s32[64,8]{1,0:T(8,128)S(1)} %copy.17.ref_ref, ...), custom_call_target="tpu_custom_call" | custom-call | flops 67108864 | bytes 4194304 | tf_op jit(solution)/shard_map/weigh_0/pallas_call | solution.py:377
  86.6 2.7 %density_list_1.1 = (f32[104,16,128]{2,1,0:T(8,128)S(1)}, bf16[104,16,128]{2,1,0:T(8,128)(2,1)S(1)}, bf16[104,16,128]{2,1,0:T(8,128)(2,1)S(1)}, bf16[104,16,128]{2,1,0:T(8,128)(2,1)S(1)}) custom-call(s32[2,145]{1,0:T(2,128)S(1)} %get-tuple-element.96.entry_ref, bf16[64,32,128]{2,1,0:T(8,128)(2,1)S(1)} %get-tuple-element.113.w_ref, ...), custom_call_target="tpu_custom_call" | custom-call | flops 150994944 | bytes 4194304 | tf_op jit(solution)/shard_map/density_list_1/pallas_call | solution.py:409
  89.4 4.7 %collective-permute-start.41 = (bf16[104,16,128]{2,1,0:T(8,128)(2,1)S(1)}, bf16[104,16,128]{2,1,0:T(8,128)(2,1)S(1)}, u32[]{:S(2)}, u32[]{:S(2)}) collective-permute-start(bf16[104,16,128]{2,1,0:T(8,128)(2,1)S(1)} %get-tuple-element.121), channel_id=1, source_target_pairs={{0,2},{1,3},{2,0},{3,1},{4,6},{5,7},{6,4},{7,5},{8,10},{9,11},{10,... | collective-permute-start | bytes 1277960 | tf_op jit(solution)/shard_map/ppermute | solution.py:34
  94.1 2.0 %density_list_0.1 = (f32[104,16,128]{2,1,0:T(8,128)S(1)}, bf16[104,16,128]{2,1,0:T(8,128)(2,1)S(1)}, bf16[104,16,128]{2,1,0:T(8,128)(2,1)S(1)}, bf16[104,16,128]{2,1,0:T(8,128)(2,1)S(1)}) custom-call(s32[2,145]{1,0:T(2,128)S(1)} %get-tuple-element.96.entry_ref, bf16[64,32,128]{2,1,0:T(8,128)(2,1)S(1)} %get-tuple-element.104.w_ref, ...), custom_call_target="tpu_custom_call" | custom-call | flops 150994944 | bytes 4194304 | tf_op jit(solution)/shard_map/density_list_0/pallas_call | solution.py:409
  96.1 1.3 %collective-permute-start.37 = (bf16[104,16,128]{2,1,0:T(8,128)(2,1)S(1)}, bf16[104,16,128]{2,1,0:T(8,128)(2,1)S(1)}, u32[]{:S(2)}, u32[]{:S(2)}) collective-permute-start(bf16[104,16,128]{2,1,0:T(8,128)(2,1)S(1)} %get-tuple-element.110), channel_id=1, source_target_pairs={{0,4},{1,5},{2,6},{3,7},{4,8},{5,9},{6,10},{7,11},{8,12},{9,13},{1... | collective-permute-start | bytes 1277960 | tf_op jit(solution)/shard_map/ppermute | solution.py:29
  98.2 3.2 %collective-permute-done.40.refs_5_ = bf16[104,16,128]{2,1,0:T(8,128)(2,1)S(1)} collective-permute-done((bf16[104,16,128]{2,1,0:T(8,128)(2,1)S(1)}, bf16[104,16,128]{2,1,0:T(8,128)(2,1)S(1)}, u32[]{:S(2)}, u32[]{:S(2)}) %collective-permute-start.40) | collective-permute-done | bytes 426016 | tf_op jit(solution)/shard_map/ppermute | solution.py:34
  102.5 9.0 %collective-permute-done.41.refs_6_ = bf16[104,16,128]{2,1,0:T(8,128)(2,1)S(1)} collective-permute-done((bf16[104,16,128]{2,1,0:T(8,128)(2,1)S(1)}, bf16[104,16,128]{2,1,0:T(8,128)(2,1)S(1)}, u32[]{:S(2)}, u32[]{:S(2)}) %collective-permute-start.41) | collective-permute-done | bytes 426016 | tf_op jit(solution)/shard_map/ppermute | solution.py:34
  111.9 7.9 %collective-permute-done.39.refs_3_ = bf16[104,16,128]{2,1,0:T(8,128)(2,1)S(1)} collective-permute-done((bf16[104,16,128]{2,1,0:T(8,128)(2,1)S(1)}, bf16[104,16,128]{2,1,0:T(8,128)(2,1)S(1)}, u32[]{:S(2)}, u32[]{:S(2)}) %collective-permute-start.39) | collective-permute-done | bytes 426016 | tf_op jit(solution)/shard_map/ppermute | solution.py:29
  119.8 3.3 %gather_up.1 = f32[64,8,8,128]{3,2,1,0:T(8,128)} custom-call(s32[64,8]{1,0:T(8,128)S(1)} %get-tuple-element.83.place_ref, f32[104,16,128]{2,1,0:T(8,128)S(1)} %get-tuple-element.109.refs_0_, bf16[104,16,128]{2,1,0:T(8,128)(2,1)S(1)} %collective-permute-done.37.refs_1_, bf16[104,16,128]{2,1,0:T(8,128)(2,1)S(1)} %collective-permute-done.38.refs_2_, ...), custom_call_target="tpu_custom_call" | custom-call | bytes 7340032 | tf_op jit(solution)/shard_map/gather_up/pallas_call | solution.py:437
  (75 shorter events, 16.1 us)
Async XLA Ops:
  2.4 13.3 %collective-permute-start.22 = (bf16[16,32,128]{2,1,0:T(8,128)(2,1)S(1)}, bf16[16,32,128]{2,1,0:T(8,128)(2,1)S(1)}, u32[]{:S(2)}, u32[]{:S(2)}) collective-permute-start(bf16[16,32,128]{2,1,0:T(8,128)(2,1)S(1)} %get-tuple-element.84), channel_id=1, source_target_pairs={{0,224},{16,240},{32,0},{48,16},{64,32},{80,48},{96,64},{112,80},{... | collective-permute-start | bytes 393224 | tf_op jit(solution)/shard_map/ppermute | solution.py:24
  8.1 7.6 %collective-permute-start.23 = (bf16[16,32,128]{2,1,0:T(8,128)(2,1)S(1)}, bf16[16,32,128]{2,1,0:T(8,128)(2,1)S(1)}, u32[]{:S(2)}, u32[]{:S(2)}) collective-permute-start(bf16[16,32,128]{2,1,0:T(8,128)(2,1)S(1)} %get-tuple-element.85), channel_id=1, source_target_pairs={{0,240},{16,0},{32,16},{48,32},{64,48},{80,64},{96,80},{112,96},{1... | collective-permute-start | bytes 393224 | tf_op jit(solution)/shard_map/ppermute | solution.py:24
  9.0 6.7 %collective-permute-start.24 = (bf16[16,32,128]{2,1,0:T(8,128)(2,1)S(1)}, bf16[16,32,128]{2,1,0:T(8,128)(2,1)S(1)}, u32[]{:S(2)}, u32[]{:S(2)}) collective-permute-start(bf16[16,32,128]{2,1,0:T(8,128)(2,1)S(1)} %get-tuple-element.86), channel_id=1, source_target_pairs={{0,16},{16,32},{32,48},{48,64},{64,80},{80,96},{96,112},{112,128},... | collective-permute-start | bytes 393224 | tf_op jit(solution)/shard_map/ppermute | solution.py:24
  9.8 7.1 %collective-permute-start.25 = (bf16[16,32,128]{2,1,0:T(8,128)(2,1)S(1)}, bf16[16,32,128]{2,1,0:T(8,128)(2,1)S(1)}, u32[]{:S(2)}, u32[]{:S(2)}) collective-permute-start(bf16[16,32,128]{2,1,0:T(8,128)(2,1)S(1)} %get-tuple-element.87), channel_id=1, source_target_pairs={{0,32},{16,48},{32,64},{48,80},{64,96},{80,112},{96,128},{112,144}... | collective-permute-start | bytes 393224 | tf_op jit(solution)/shard_map/ppermute | solution.py:24
  24.2 47.0 %copy-start.14 = (bf16[65,32,128]{2,1,0:T(8,128)(2,1)}, bf16[65,32,128]{2,1,0:T(8,128)(2,1)S(1)}, u32[]{:S(2)}) copy-start(bf16[65,32,128]{2,1,0:T(8,128)(2,1)S(1)} %get-tuple-element.88.own) | copy-start | bytes 1597444
  24.2 8.4 %collective-permute-start.27 = (bf16[16,32,128]{2,1,0:T(8,128)(2,1)S(1)}, bf16[16,32,128]{2,1,0:T(8,128)(2,1)S(1)}, u32[]{:S(2)}, u32[]{:S(2)}) collective-permute-start(bf16[16,32,128]{2,1,0:T(8,128)(2,1)S(1)} %get-tuple-element.90), channel_id=1, source_target_pairs={{0,224},{16,240},{32,0},{48,16},{64,32},{80,48},{96,64},{112,80},{... | collective-permute-start | bytes 393224 | tf_op jit(solution)/shard_map/ppermute | solution.py:24
  25.8 7.5 %collective-permute-start.28 = (bf16[16,32,128]{2,1,0:T(8,128)(2,1)S(1)}, bf16[16,32,128]{2,1,0:T(8,128)(2,1)S(1)}, u32[]{:S(2)}, u32[]{:S(2)}) collective-permute-start(bf16[16,32,128]{2,1,0:T(8,128)(2,1)S(1)} %get-tuple-element.93), channel_id=1, source_target_pairs={{0,240},{16,0},{32,16},{48,32},{64,48},{80,64},{96,80},{112,96},{1... | collective-permute-start | bytes 393224 | tf_op jit(solution)/shard_map/ppermute | solution.py:24
  26.1 15.1 %collective-permute-start.26 = (bf16[65,32,128]{2,1,0:T(8,128)(2,1)S(1)}, bf16[65,32,128]{2,1,0:T(8,128)(2,1)S(1)}, u32[]{:S(2)}, u32[]{:S(2)}) collective-permute-start(bf16[65,32,128]{2,1,0:T(8,128)(2,1)S(1)} %get-tuple-element.88.own), channel_id=1, source_target_pairs={{0,8},{1,9},{2,10},{3,11},{4,12},{5,13},{6,14},{7,15},{8,0},{9,1},... | collective-permute-start | bytes 1597448 | tf_op jit(solution)/shard_map/ppermute | solution.py:29
  28.7 8.6 %collective-permute-start.31 = (bf16[16,32,128]{2,1,0:T(8,128)(2,1)S(1)}, bf16[16,32,128]{2,1,0:T(8,128)(2,1)S(1)}, u32[]{:S(2)}, u32[]{:S(2)}) collective-permute-start(bf16[16,32,128]{2,1,0:T(8,128)(2,1)S(1)} %get-tuple-element.94), channel_id=1, source_target_pairs={{0,16},{16,32},{32,48},{48,64},{64,80},{80,96},{96,112},{112,128},... | collective-permute-start | bytes 393224 | tf_op jit(solution)/shard_map/ppermute | solution.py:24
  32.6 6.4 %collective-permute-start.32 = (bf16[16,32,128]{2,1,0:T(8,128)(2,1)S(1)}, bf16[16,32,128]{2,1,0:T(8,128)(2,1)S(1)}, u32[]{:S(2)}, u32[]{:S(2)}) collective-permute-start(bf16[16,32,128]{2,1,0:T(8,128)(2,1)S(1)} %get-tuple-element.95), channel_id=1, source_target_pairs={{0,32},{16,48},{32,64},{48,80},{64,96},{80,112},{96,128},{112,144}... | collective-permute-start | bytes 393224 | tf_op jit(solution)/shard_map/ppermute | solution.py:24
  34.6 36.6 %collective-permute-start.30 = (bf16[97,32,128]{2,1,0:T(8,128)(2,1)}, bf16[97,32,128]{2,1,0:T(8,128)(2,1)S(1)}, u32[]{:S(2)}, u32[]{:S(2)}) collective-permute-start(bf16[97,32,128]{2,1,0:T(8,128)(2,1)} %constant_dynamic-update-slice_fusion), channel_id=1, source_target_pairs={{0,3},{1,0},{2,1},{3,2},{4,7},{5,4},{6,5},{7,6},{8,11},{9,8},{10,9... | collective-permute-start | bytes 2383880 | tf_op jit(solution)/shard_map/ppermute | solution.py:34
  37.3 43.1 %collective-permute-start.29 = (bf16[97,32,128]{2,1,0:T(8,128)(2,1)}, bf16[97,32,128]{2,1,0:T(8,128)(2,1)S(1)}, u32[]{:S(2)}, u32[]{:S(2)}) collective-permute-start(bf16[97,32,128]{2,1,0:T(8,128)(2,1)} %constant_dynamic-update-slice_fusion), channel_id=1, source_target_pairs={{0,1},{1,2},{2,3},{3,0},{4,5},{5,6},{6,7},{7,4},{8,9},{9,10},{10,1... | collective-permute-start | bytes 2383880 | tf_op jit(solution)/shard_map/ppermute | solution.py:34
  37.3 33.9 %copy-start.23 = (bf16[16,32,128]{2,1,0:T(8,128)(2,1)}, bf16[16,32,128]{2,1,0:T(8,128)(2,1)S(1)}, u32[]{:S(2)}) copy-start(bf16[16,32,128]{2,1,0:T(8,128)(2,1)S(1)} %collective-permute-done.31) | copy-start | bytes 393220
  39.0 33.4 %copy-start.25 = (bf16[16,32,128]{2,1,0:T(8,128)(2,1)}, bf16[16,32,128]{2,1,0:T(8,128)(2,1)S(1)}, u32[]{:S(2)}) copy-start(bf16[16,32,128]{2,1,0:T(8,128)(2,1)S(1)} %collective-permute-done.32) | copy-start | bytes 393220
  39.7 40.7 %collective-permute-start.34 = (bf16[97,32,128]{2,1,0:T(8,128)(2,1)}, bf16[97,32,128]{2,1,0:T(8,128)(2,1)S(1)}, u32[]{:S(2)}, u32[]{:S(2)}) collective-permute-start(bf16[97,32,128]{2,1,0:T(8,128)(2,1)} %get-tuple-element.130), channel_id=1, source_target_pairs={{0,12},{1,13},{2,14},{3,15},{4,0},{5,1},{6,2},{7,3},{8,4},{9,5},{1... | collective-permute-start | bytes 2383880 | tf_op jit(solution)/shard_map/ppermute | solution.py:29
  41.0 39.4 %collective-permute-start.33 = (bf16[97,32,128]{2,1,0:T(8,128)(2,1)}, bf16[97,32,128]{2,1,0:T(8,128)(2,1)}, u32[]{:S(2)}, u32[]{:S(2)}) collective-permute-start(bf16[97,32,128]{2,1,0:T(8,128)(2,1)} %get-tuple-element.130), channel_id=1, source_target_pairs={{0,4},{1,5},{2,6},{3,7},{4,8},{5,9},{6,10},{7,11},{8,12},{9,13},{1... | collective-permute-start | bytes 2383880 | tf_op jit(solution)/shard_map/ppermute | solution.py:29
  42.0 42.2 %collective-permute-start.36 = (bf16[97,32,128]{2,1,0:T(8,128)(2,1)}, bf16[97,32,128]{2,1,0:T(8,128)(2,1)S(1)}, u32[]{:S(2)}, u32[]{:S(2)}) collective-permute-start(bf16[97,32,128]{2,1,0:T(8,128)(2,1)} %constant_dynamic-update-slice_fusion), channel_id=1, source_target_pairs={{0,2},{1,3},{2,0},{3,1},{4,6},{5,7},{6,4},{7,5},{8,10},{9,11},{10,... | collective-permute-start | bytes 2383880 | tf_op jit(solution)/shard_map/ppermute | solution.py:34
  71.2 15.3 %collective-permute-start.35 = (bf16[32,32,128]{2,1,0:T(8,128)(2,1)S(1)}, bf16[32,32,128]{2,1,0:T(8,128)(2,1)}, u32[]{:S(2)}, u32[]{:S(2)}) collective-permute-start(bf16[32,32,128]{2,1,0:T(8,128)(2,1)S(1)} %get-tuple-element.129.own), channel_id=1, source_target_pairs={{0,8},{1,9},{2,10},{3,11},{4,12},{5,13},{6,14},{7,15},{8,0},{9,1},... | collective-permute-start | bytes 786440 | tf_op jit(solution)/shard_map/ppermute | solution.py:29
  89.3 12.2 %collective-permute-start.40 = (bf16[104,16,128]{2,1,0:T(8,128)(2,1)S(1)}, bf16[104,16,128]{2,1,0:T(8,128)(2,1)S(1)}, u32[]{:S(2)}, u32[]{:S(2)}) collective-permute-start(bf16[104,16,128]{2,1,0:T(8,128)(2,1)S(1)} %get-tuple-element.120), channel_id=1, source_target_pairs={{0,1},{1,2},{2,3},{3,0},{4,5},{5,6},{6,7},{7,4},{8,9},{9,10},{10,1... | collective-permute-start | bytes 1277960 | tf_op jit(solution)/shard_map/ppermute | solution.py:34
  89.4 22.0 %collective-permute-start.41 = (bf16[104,16,128]{2,1,0:T(8,128)(2,1)S(1)}, bf16[104,16,128]{2,1,0:T(8,128)(2,1)S(1)}, u32[]{:S(2)}, u32[]{:S(2)}) collective-permute-start(bf16[104,16,128]{2,1,0:T(8,128)(2,1)S(1)} %get-tuple-element.121), channel_id=1, source_target_pairs={{0,2},{1,3},{2,0},{3,1},{4,6},{5,7},{6,4},{7,5},{8,10},{9,11},{10,... | collective-permute-start | bytes 1277960 | tf_op jit(solution)/shard_map/ppermute | solution.py:34
  94.1 17.8 %collective-permute-start.42 = (bf16[104,16,128]{2,1,0:T(8,128)(2,1)S(1)}, bf16[104,16,128]{2,1,0:T(8,128)(2,1)S(1)}, u32[]{:S(2)}, u32[]{:S(2)}) collective-permute-start(bf16[104,16,128]{2,1,0:T(8,128)(2,1)S(1)} %get-tuple-element.122), channel_id=1, source_target_pairs={{0,3},{1,0},{2,1},{3,2},{4,7},{5,4},{6,5},{7,6},{8,11},{9,8},{10,9... | collective-permute-start | bytes 1277960 | tf_op jit(solution)/shard_map/ppermute | solution.py:34
  96.1 15.8 %collective-permute-start.37 = (bf16[104,16,128]{2,1,0:T(8,128)(2,1)S(1)}, bf16[104,16,128]{2,1,0:T(8,128)(2,1)S(1)}, u32[]{:S(2)}, u32[]{:S(2)}) collective-permute-start(bf16[104,16,128]{2,1,0:T(8,128)(2,1)S(1)} %get-tuple-element.110), channel_id=1, source_target_pairs={{0,4},{1,5},{2,6},{3,7},{4,8},{5,9},{6,10},{7,11},{8,12},{9,13},{1... | collective-permute-start | bytes 1277960 | tf_op jit(solution)/shard_map/ppermute | solution.py:29
  97.4 14.5 %collective-permute-start.38 = (bf16[104,16,128]{2,1,0:T(8,128)(2,1)S(1)}, bf16[104,16,128]{2,1,0:T(8,128)(2,1)S(1)}, u32[]{:S(2)}, u32[]{:S(2)}) collective-permute-start(bf16[104,16,128]{2,1,0:T(8,128)(2,1)S(1)} %get-tuple-element.111), channel_id=1, source_target_pairs={{0,8},{1,9},{2,10},{3,11},{4,12},{5,13},{6,14},{7,15},{8,0},{9,1},... | collective-permute-start | bytes 1277960 | tf_op jit(solution)/shard_map/ppermute | solution.py:29
  101.4 18.3 %collective-permute-start.39 = (bf16[104,16,128]{2,1,0:T(8,128)(2,1)S(1)}, bf16[104,16,128]{2,1,0:T(8,128)(2,1)S(1)}, u32[]{:S(2)}, u32[]{:S(2)}) collective-permute-start(bf16[104,16,128]{2,1,0:T(8,128)(2,1)S(1)} %get-tuple-element.112), channel_id=1, source_target_pairs={{0,12},{1,13},{2,14},{3,15},{4,0},{5,1},{6,2},{7,3},{8,4},{9,5},{1... | collective-permute-start | bytes 1277960 | tf_op jit(solution)/shard_map/ppermute | solution.py:29
  (15 other events, 53.0 us)

commit v3 on v2

--- a/solution.py
+++ b/solution.py
@@ -94,7 +94,7 @@
 def coef_all(inv_sqrt_blocks, first, pieces, block_ref, row_count, send_list, occupation):
     def kernel(
         ref_ref, count_ref, send_ref, blocks_1, blocks_2, blocks_3, first_ref, occ_ref,
-        p0, p1, p2, p3, coef_ref, o0, o1, o2, o3, table,
+        p0, p1, p2, p3, coef_ref, sent_y, sent_x, o0, o1, o2, o3, table,
     ):
         step = pl.program_id(0)
 
@@ -130,6 +130,8 @@
             for n, out in enumerate((o0, o1, o2, o3)):
                 for j in range(16):
                     out[j] = coef_ref[send_ref[n, j]]
+            sent_y[0:65] = coef_ref[...]
+            sent_x[0:65] = coef_ref[...]
 
     piece = jax.ShapeDtypeStruct((16, 32, 128), BF16)
     whole = pl.BlockSpec((16, 32, 128), lambda i: (0, 0, 0))
@@ -137,7 +139,7 @@
     return pl.pallas_call(
         kernel,
         grid=(64 // ROWS,),
-        out_shape=[jax.ShapeDtypeStruct((65, 32, 128), BF16)] + [piece] * 4,
+        out_shape=[jax.ShapeDtypeStruct((n, 32, 128), BF16) for n in (65, 97, 97)] + [piece] * 4,
         in_specs=[smem, smem, smem]
         + [pl.BlockSpec((ROWS, 2, 128, 128), lambda i, k=k: (i, k, 0, 0)) for k in (1, 2, 3)]
         + [
@@ -145,7 +147,7 @@
             pl.BlockSpec((32, 1), lambda i: (0, 0)),
         ]
         + [whole] * 4,
-        out_specs=[pl.BlockSpec((65, 32, 128), lambda i: (0, 0, 0))] + [whole] * 4,
+        out_specs=[pl.BlockSpec((n, 32, 128), lambda i: (0, 0, 0)) for n in (65, 97, 97)] + [whole] * 4,
         scratch_shapes=[pltpu.VMEM((64, 32, 128), BF16)],
         compiler_params=params(48),
         cost_estimate=cost(2 * 64 * 6 * 32 * 128 * 128, 14 * 1024 * 1024),
@@ -472,22 +474,24 @@
     pieces = [along_dom(p, offset) for p, offset in zip(picked, OFFSETS)]
     first = coef_own(inv_sqrt_blocks, waves, block_ref)
     entries, places, over = plan(block_ref, count)
-    coef, *outgoing = coef_all(
+    coef, sent_y, sent_x, *outgoing = coef_all(
         inv_sqrt_blocks, first, pieces, block_ref, count, send, occupation.reshape(32, 1)
     )
-    halos = [along_dom(p, offset) for p, offset in zip(outgoing[:3], OFFSETS)]
-    halos[0], last = lax.optimization_barrier((halos[0], outgoing[3]))
-    halos.append(along_dom(last, OFFSETS[3]))
-    far_x = along_x(coef, 2)
+    halos = [along_dom(p, offset) for p, offset in zip(outgoing, OFFSETS)]
+    far_x, far_y = along_x(coef, 2), along_y(coef, 2)
+    sent_y = sent_y.at[65:81].set(halos[0]).at[81:97].set(halos[1])
+    sent_x = sent_x.at[65:81].set(halos[2]).at[81:97].set(halos[3])
+    sent_y, sent_x, far_x, far_y = lax.optimization_barrier((sent_y, sent_x, far_x, far_y))
+    beside = [along_y(sent_y, 1), along_y(sent_y, -1), along_x(sent_x, 1), along_x(sent_x, -1)]
     half_y, half_x = jnp.concatenate(halos[:2], axis=0), jnp.concatenate(halos[2:], axis=0)
-    both_y, both_x = jnp.concatenate([coef, half_y], axis=0), jnp.concatenate([coef, half_x], axis=0)
-    beside = [along_y(both_y, 1), along_y(both_y, -1), along_x(both_x, 1), along_x(both_x, -1)]
-    far_y, half_far_x = along_y(both_y, 2), along_x(half_x, 2)
-    far_x, entries, *beside = lax.optimization_barrier((far_x, entries, *beside))
+    half_y, half_x, entries = lax.optimization_barrier((half_y, half_x, entries))
+    half_far_y, half_far_x = along_y(half_y, 2), along_x(half_x, 2)
     weighted_y, *begun_y = weigh(0, here, [coef, *beside[:2], far_y], block_ref)
     weighted_x, *begun_x = weigh(1, here, [coef, *beside[2:], far_x], block_ref)
-    half_far_x, weighted_y, weighted_x = lax.optimization_barrier((half_far_x, weighted_y, weighted_x))
-    parts_x = density_list(0, entries, weighted_y, [half_y, *beside[:2], far_y], begun_y)
+    half_far_y, half_far_x, weighted_y, weighted_x = lax.optimization_barrier(
+        (half_far_y, half_far_x, weighted_y, weighted_x)
+    )
+    parts_x = density_list(0, entries, weighted_y, [half_y, *beside[:2], half_far_y], begun_y)
     parts_y = density_list(1, entries, weighted_x, [half_x, *beside[2:], half_far_x], begun_x)
     density = gather_up(scattered(parts_x, parts_y), places)
 

time: 124 us -> 109 us (0.88)
  the two profiles are of different devices: /device:TPU:3 before, /device:TPU:24 now
where the time goes in v3:
time: 109 us
  Pallas kernels  33.3 us (31%)
  waiting for transfers between devices  31.7 us (29%)
  starting transfers between devices  31.6 us (29%)
  local copies, waits for them, and re-layouts  9.58 us (9%)
  other arithmetic  1.82 us (2%)
    ppermute x7, waiting for transfers between devices, along_y(): return lax.ppermute(value, 'st', pairs)  16.9 us
    ppermute x7, starting transfers between devices, along_x(): return lax.ppermute(value, 'st', pairs)  12.3 us
    ppermute x8, starting transfers between devices, along_dom(): return lax.ppermute(value, 'dom', [(i, (i + by) % 16) for i in range(16)])  10.1 us
    ppermute x7, starting transfers between devices, along_y(): return lax.ppermute(value, 'st', pairs)  9.18 us
    ppermute x7, waiting for transfers between devices, along_x(): return lax.ppermute(value, 'st', pairs)  9.09 us
    pallas_call x1, Pallas kernels, coef_all(): pl.pallas_call(kernel, grid=(64 // ROWS,), out_shape=[jax.ShapeDtypeStruc...  8.49 us
    pallas_call x1, Pallas kernels, plan(): pl.pallas_call(kernel, out_shape=[jax.ShapeDtypeStruct((2, LIST + 1), jnp...  7.93 us
    unnamed x25, local copies, waits for them, and re-layouts  6.2 us
  transfers between devices with their start and end apart: 22, of which 12 were waited for; matrix products, arithmetic and copies ran while one was open for 5% of the time, Pallas kernels for 17%

profile of v3, /device:TPU:24, one launch (start us, length us, event | category | flops | bytes accessed | tf_op | source)
XLA Modules:
  0.0 108.8 jit_solution(11074283712404930035)
XLA Ops:
  2.4 5.9 %collective-permute-start.22 = (bf16[16,32,128]{2,1,0:T(8,128)(2,1)S(1)}, bf16[16,32,128]{2,1,0:T(8,128)(2,1)S(1)}, u32[]{:S(2)}, u32[]{:S(2)}) collective-permute-start(bf16[16,32,128]{2,1,0:T(8,128)(2,1)S(1)} %get-tuple-element.134), channel_id=1, source_target_pairs={{0,224},{16,240},{32,0},{48,16},{64,32},{80,48},{96,64},{112,80},{... | collective-permute-start | bytes 393224 | tf_op jit(solution)/shard_map/ppermute | solution.py:24
  12.1 3.3 %coef_own.1.first_ref = f32[64,32,128]{2,1,0:T(8,128)S(1)} custom-call(s32[64,8]{1,0:T(8,128)S(1)} %copy.17.ref_ref, bf16[64,8,128,128]{3,2,1,0:T(8,128)(2,1)} %blocks_3.1, bf16[32,8192]{1,0:T(8,128)(2,1)S(1)} %copy-done.1), custom_call_target="tpu_custom_call" | custom-call | flops 134217728 | bytes 6291456 | tf_op jit(solution)/shard_map/coef_own/pallas_call | solution.py:78
  16.5 8.5 %coef_all.1 = (bf16[65,32,128]{2,1,0:T(8,128)(2,1)S(1)}, bf16[97,32,128]{2,1,0:T(8,128)(2,1)}, bf16[97,32,128]{2,1,0:T(8,128)(2,1)}, bf16[16,32,128]{2,1,0:T(8,1...) custom-call(s32[64,8]{1,0:T(8,128)S(1)} %copy.17.ref_ref, ...), custom_call_target="tpu_custom_call" | custom-call | flops 402653184 | bytes 14680064 | tf_op jit(solution)/shard_map/coef_all/pallas_call | solution.py:139
  24.9 1.6 %collective-permute-start.26 = (bf16[16,32,128]{2,1,0:T(8,128)(2,1)S(1)}, bf16[16,32,128]{2,1,0:T(8,128)(2,1)S(1)}, u32[]{:S(2)}, u32[]{:S(2)}) collective-permute-start(bf16[16,32,128]{2,1,0:T(8,128)(2,1)S(1)} %get-tuple-element.138), channel_id=1, source_target_pairs={{0,224},{16,240},{32,0},{48,16},{64,32},{80,48},{96,64},{112,80},{... | collective-permute-start | bytes 393224 | tf_op jit(solution)/shard_map/ppermute | solution.py:24
  27.8 3.0 %collective-permute-start.32 = (bf16[65,32,128]{2,1,0:T(8,128)(2,1)S(1)}, bf16[65,32,128]{2,1,0:T(8,128)(2,1)S(1)}, u32[]{:S(2)}, u32[]{:S(2)}) collective-permute-start(bf16[65,32,128]{2,1,0:T(8,128)(2,1)S(1)} %get-tuple-element.146.own), channel_id=1, source_target_pairs={{0,8},{1,9},{2,10},{3,11},{4,12},{5,13},{6,14},{7,15},{8,0},{9,1},... | collective-permute-start | bytes 1597448 | tf_op jit(solution)/shard_map/ppermute | solution.py:29
  34.3 3.0 %collective-permute-done.28 = bf16[16,32,128]{2,1,0:T(8,128)(2,1)S(1)} collective-permute-done((bf16[16,32,128]{2,1,0:T(8,128)(2,1)S(1)}, bf16[16,32,128]{2,1,0:T(8,128)(2,1)S(1)}, u32[]{:S(2)}, u32[]{:S(2)}) %collective-permute-start.28) | collective-permute-done | bytes 131104 | tf_op jit(solution)/shard_map/ppermute | solution.py:24
  39.5 2.7 %collective-permute-done.33.far = bf16[65,32,128]{2,1,0:T(8,128)(2,1)S(1)} collective-permute-done((bf16[65,32,128]{2,1,0:T(8,128)(2,1)S(1)}, bf16[65,32,128]{2,1,0:T(8,128)(2,1)S(1)}, u32[]{:S(2)}, u32[]{:S(2)}) %collective-permute-start.33) | collective-permute-done | bytes 532512 | tf_op jit(solution)/shard_map/ppermute | solution.py:34
  44.6 2.7 %collective-permute-start.34 = (bf16[97,32,128]{2,1,0:T(8,128)(2,1)}, bf16[97,32,128]{2,1,0:T(8,128)(2,1)S(1)}, u32[]{:S(2)}, u32[]{:S(2)}) collective-permute-start(bf16[97,32,128]{2,1,0:T(8,128)(2,1)} %constant_dynamic-update-slice_fusion.2), channel_id=1, source_target_pairs={{0,1},{1,2},{2,3},{3,0},{4,5},{5,6},{6,7},{7,4},{8,9},{9,10},{10,1... | collective-permute-start | bytes 2383880 | tf_op jit(solution)/shard_map/ppermute | solution.py:34
  47.3 2.8 %collective-permute-start.37 = (bf16[97,32,128]{2,1,0:T(8,128)(2,1)}, bf16[97,32,128]{2,1,0:T(8,128)(2,1)S(1)}, u32[]{:S(2)}, u32[]{:S(2)}) collective-permute-start(bf16[97,32,128]{2,1,0:T(8,128)(2,1)} %constant_dynamic-update-slice_fusion), channel_id=1, source_target_pairs={{0,12},{1,13},{2,14},{3,15},{4,0},{5,1},{6,2},{7,3},{8,4},{9,5},{1... | collective-permute-start | bytes 2383880 | tf_op jit(solution)/shard_map/ppermute | solution.py:29
  50.0 7.9 %plan.1 = (s32[2,145]{1,0:T(2,128)S(1)}, s32[64,8]{1,0:T(8,128)S(1)}, s32[1,1]{1,0:T(1,128)}) custom-call(s32[64,8]{1,0:T(8,128)S(1)} %copy.17.ref_ref, s32[1,64]{1,0:T(1,128)S(1)} %bitcast.9), custom_call_target="tpu_custom_call" | custom-call | bytes 25165824 | tf_op jit(solution)/shard_map/plan/pallas_call | solution.py:338
  59.8 6.2 %collective-permute-done.35.higher = bf16[97,32,128]{2,1,0:T(8,128)(2,1)S(1)} collective-permute-done((bf16[97,32,128]{2,1,0:T(8,128)(2,1)}, bf16[97,32,128]{2,1,0:T(8,128)(2,1)S(1)}, u32[]{:S(2)}, u32[]{:S(2)}) %collective-permute-start.35) | collective-permute-done | bytes 794656 | tf_op jit(solution)/shard_map/ppermute | solution.py:34
  66.0 3.0 %collective-permute-start.31 = (bf16[32,32,128]{2,1,0:T(8,128)(2,1)}, bf16[32,32,128]{2,1,0:T(8,128)(2,1)}, u32[]{:S(2)}, u32[]{:S(2)}) collective-permute-start(bf16[32,32,128]{2,1,0:T(8,128)(2,1)} %pad_maximum_fusion.2.own), channel_id=1, source_target_pairs={{0,8},{1,9},{2,10},{3,11},{4,12},{5,13},{6,14},{7,15},{8,0},{9,1},... | collective-permute-start | bytes 786440 | tf_op jit(solution)/shard_map/ppermute | solution.py:29
  70.4 2.4 %weigh_0.1 = (bf16[64,32,128]{2,1,0:T(8,128)(2,1)S(1)}, f32[32,16,128]{2,1,0:T(8,128)S(1)}, bf16[32,16,128]{2,1,0:T(8,128)(2,1)S(1)}, bf16[32,16,128]{2,1,0:T(8,128)(2,1)S(1)}, bf16[32,16,128]{2,1,0:T(8,128)(2,1)S(1)}) custom-call(s32[2]{0:T(128)S(1)} %pad_add_fusion.here_ref, s32[64,8]{1,0:T(8,128)S(1)} %copy.17.ref_ref, bf16[65,32,128]{2,1,0:T(8,128)(2,1)} %copy-done.16, ...), custom_call_target="tpu_custom_call" | custom-call | flops 67108864 | bytes 4194304 | tf_op jit(solution)/shard_map/weigh_0/pallas_call | solution.py:379
  72.8 2.2 %collective-permute-done.36.lower = bf16[97,32,128]{2,1,0:T(8,128)(2,1)S(1)} collective-permute-done((bf16[97,32,128]{2,1,0:T(8,128)(2,1)}, bf16[97,32,128]{2,1,0:T(8,128)(2,1)S(1)}, u32[]{:S(2)}, u32[]{:S(2)}) %collective-permute-start.36) | collective-permute-done | bytes 794656 | tf_op jit(solution)/shard_map/ppermute | solution.py:29
  75.1 2.4 %weigh_1.1 = (bf16[64,32,128]{2,1,0:T(8,128)(2,1)S(1)}, f32[32,16,128]{2,1,0:T(8,128)S(1)}, bf16[32,16,128]{2,1,0:T(8,128)(2,1)S(1)}, bf16[32,16,128]{2,1,0:T(8,128)(2,1)S(1)}, bf16[32,16,128]{2,1,0:T(8,128)(2,1)S(1)}) custom-call(s32[2]{0:T(128)S(1)} %pad_add_fusion.here_ref, s32[64,8]{1,0:T(8,128)S(1)} %copy.17.ref_ref, ...), custom_call_target="tpu_custom_call" | custom-call | flops 67108864 | bytes 4194304 | tf_op jit(solution)/shard_map/weigh_1/pallas_call | solution.py:379
  77.5 2.4 %density_list_0.1 = (f32[104,16,128]{2,1,0:T(8,128)S(1)}, bf16[104,16,128]{2,1,0:T(8,128)(2,1)S(1)}, bf16[104,16,128]{2,1,0:T(8,128)(2,1)S(1)}, bf16[104,16,128]{2,1,0:T(8,128)(2,1)S(1)}) custom-call(s32[2,145]{1,0:T(2,128)S(1)} %get-tuple-element.143.entry_ref, bf16[64,32,128]{2,1,0:T(8,128)(2,1)S(1)} %get-tuple-element.155.w_ref, ...), custom_call_target="tpu_custom_call" | custom-call | flops 150994944 | bytes 4194304 | tf_op jit(solution)/shard_map/density_list_0/pallas_call | solution.py:411
  80.0 2.0 %collective-permute-start.39 = (bf16[104,16,128]{2,1,0:T(8,128)(2,1)S(1)}, bf16[104,16,128]{2,1,0:T(8,128)(2,1)S(1)}, u32[]{:S(2)}, u32[]{:S(2)}) collective-permute-start(bf16[104,16,128]{2,1,0:T(8,128)(2,1)S(1)} %get-tuple-element.163), channel_id=1, source_target_pairs={{0,8},{1,9},{2,10},{3,11},{4,12},{5,13},{6,14},{7,15},{8,0},{9,1},... | collective-permute-start | bytes 1277960 | tf_op jit(solution)/shard_map/ppermute | solution.py:29
  82.0 1.4 %collective-permute-start.40 = (bf16[104,16,128]{2,1,0:T(8,128)(2,1)S(1)}, bf16[104,16,128]{2,1,0:T(8,128)(2,1)S(1)}, u32[]{:S(2)}, u32[]{:S(2)}) collective-permute-start(bf16[104,16,128]{2,1,0:T(8,128)(2,1)S(1)} %get-tuple-element.164), channel_id=1, source_target_pairs={{0,12},{1,13},{2,14},{3,15},{4,0},{5,1},{6,2},{7,3},{8,4},{9,5},{1... | collective-permute-start | bytes 1277960 | tf_op jit(solution)/shard_map/ppermute | solution.py:29
  83.4 2.5 %density_list_1.1 = (f32[104,16,128]{2,1,0:T(8,128)S(1)}, bf16[104,16,128]{2,1,0:T(8,128)(2,1)S(1)}, bf16[104,16,128]{2,1,0:T(8,128)(2,1)S(1)}, bf16[104,16,128]{2,1,0:T(8,128)(2,1)S(1)}) custom-call(s32[2,145]{1,0:T(2,128)S(1)} %get-tuple-element.143.entry_ref, bf16[64,32,128]{2,1,0:T(8,128)(2,1)S(1)} %get-tuple-element.165.w_ref, ...), custom_call_target="tpu_custom_call" | custom-call | flops 150994944 | bytes 4194304 | tf_op jit(solution)/shard_map/density_list_1/pallas_call | solution.py:411
  85.9 3.6 %collective-permute-start.41 = (bf16[104,16,128]{2,1,0:T(8,128)(2,1)S(1)}, bf16[104,16,128]{2,1,0:T(8,128)(2,1)S(1)}, u32[]{:S(2)}, u32[]{:S(2)}) collective-permute-start(bf16[104,16,128]{2,1,0:T(8,128)(2,1)S(1)} %get-tuple-element.172), channel_id=1, source_target_pairs={{0,1},{1,2},{2,3},{3,0},{4,5},{5,6},{6,7},{7,4},{8,9},{9,10},{10,1... | collective-permute-start | bytes 1277960 | tf_op jit(solution)/shard_map/ppermute | solution.py:34
  89.5 6.7 %collective-permute-done.38.refs_1_ = bf16[104,16,128]{2,1,0:T(8,128)(2,1)S(1)} collective-permute-done((bf16[104,16,128]{2,1,0:T(8,128)(2,1)S(1)}, bf16[104,16,128]{2,1,0:T(8,128)(2,1)S(1)}, u32[]{:S(2)}, u32[]{:S(2)}) %collective-permute-start.38) | collective-permute-done | bytes 426016 | tf_op jit(solution)/shard_map/ppermute | solution.py:29
  97.8 3.0 %collective-permute-done.41.refs_5_ = bf16[104,16,128]{2,1,0:T(8,128)(2,1)S(1)} collective-permute-done((bf16[104,16,128]{2,1,0:T(8,128)(2,1)S(1)}, bf16[104,16,128]{2,1,0:T(8,128)(2,1)S(1)}, u32[]{:S(2)}, u32[]{:S(2)}) %collective-permute-start.41) | collective-permute-done | bytes 426016 | tf_op jit(solution)/shard_map/ppermute | solution.py:34
  100.9 4.6 %collective-permute-done.43.refs_7_ = bf16[104,16,128]{2,1,0:T(8,128)(2,1)S(1)} collective-permute-done((bf16[104,16,128]{2,1,0:T(8,128)(2,1)S(1)}, bf16[104,16,128]{2,1,0:T(8,128)(2,1)S(1)}, u32[]{:S(2)}, u32[]{:S(2)}) %collective-permute-start.43) | collective-permute-done | bytes 426016 | tf_op jit(solution)/shard_map/ppermute | solution.py:34
  105.5 3.3 %gather_up.1 = f32[64,8,8,128]{3,2,1,0:T(8,128)} custom-call(s32[64,8]{1,0:T(8,128)S(1)} %get-tuple-element.133.place_ref, f32[104,16,128]{2,1,0:T(8,128)S(1)} %get-tuple-element.161.refs_0_, bf16[104,16,128]{2,1,0:T(8,128)(2,1)S(1)} %collective-permute-done.38.refs_1_, bf16[104,16,128]{2,1,0:T(8,128)(2,1)S(1)} %collective-permute-done.39.refs_2_, ...), custom_call_target="tpu_custom_call" | custom-call | bytes 7340032 | tf_op jit(solution)/shard_map/gather_up/pallas_call | solution.py:439
  (64 shorter events, 20.8 us)
Async XLA Ops:
  2.4 13.0 %collective-permute-start.22 = (bf16[16,32,128]{2,1,0:T(8,128)(2,1)S(1)}, bf16[16,32,128]{2,1,0:T(8,128)(2,1)S(1)}, u32[]{:S(2)}, u32[]{:S(2)}) collective-permute-start(bf16[16,32,128]{2,1,0:T(8,128)(2,1)S(1)} %get-tuple-element.134), channel_id=1, source_target_pairs={{0,224},{16,240},{32,0},{48,16},{64,32},{80,48},{96,64},{112,80},{... | collective-permute-start | bytes 393224 | tf_op jit(solution)/shard_map/ppermute | solution.py:24
  8.4 7.1 %collective-permute-start.23 = (bf16[16,32,128]{2,1,0:T(8,128)(2,1)S(1)}, bf16[16,32,128]{2,1,0:T(8,128)(2,1)S(1)}, u32[]{:S(2)}, u32[]{:S(2)}) collective-permute-start(bf16[16,32,128]{2,1,0:T(8,128)(2,1)S(1)} %get-tuple-element.135), channel_id=1, source_target_pairs={{0,240},{16,0},{32,16},{48,32},{64,48},{80,64},{96,80},{112,96},{1... | collective-permute-start | bytes 393224 | tf_op jit(solution)/shard_map/ppermute | solution.py:24
  8.5 6.9 %collective-permute-start.24 = (bf16[16,32,128]{2,1,0:T(8,128)(2,1)S(1)}, bf16[16,32,128]{2,1,0:T(8,128)(2,1)S(1)}, u32[]{:S(2)}, u32[]{:S(2)}) collective-permute-start(bf16[16,32,128]{2,1,0:T(8,128)(2,1)S(1)} %get-tuple-element.136), channel_id=1, source_target_pairs={{0,16},{16,32},{32,48},{48,64},{64,80},{80,96},{96,112},{112,128},... | collective-permute-start | bytes 393224 | tf_op jit(solution)/shard_map/ppermute | solution.py:24
  8.9 7.6 %collective-permute-start.25 = (bf16[16,32,128]{2,1,0:T(8,128)(2,1)S(1)}, bf16[16,32,128]{2,1,0:T(8,128)(2,1)S(1)}, u32[]{:S(2)}, u32[]{:S(2)}) collective-permute-start(bf16[16,32,128]{2,1,0:T(8,128)(2,1)S(1)} %get-tuple-element.137), channel_id=1, source_target_pairs={{0,32},{16,48},{32,64},{48,80},{64,96},{80,112},{96,128},{112,144}... | collective-permute-start | bytes 393224 | tf_op jit(solution)/shard_map/ppermute | solution.py:24
  24.9 41.1 %copy-start.16 = (bf16[65,32,128]{2,1,0:T(8,128)(2,1)}, bf16[65,32,128]{2,1,0:T(8,128)(2,1)S(1)}, u32[]{:S(2)}) copy-start(bf16[65,32,128]{2,1,0:T(8,128)(2,1)S(1)} %get-tuple-element.146.own) | copy-start | bytes 1597444
  24.9 6.4 %collective-permute-start.26 = (bf16[16,32,128]{2,1,0:T(8,128)(2,1)S(1)}, bf16[16,32,128]{2,1,0:T(8,128)(2,1)S(1)}, u32[]{:S(2)}, u32[]{:S(2)}) collective-permute-start(bf16[16,32,128]{2,1,0:T(8,128)(2,1)S(1)} %get-tuple-element.138), channel_id=1, source_target_pairs={{0,224},{16,240},{32,0},{48,16},{64,32},{80,48},{96,64},{112,80},{... | collective-permute-start | bytes 393224 | tf_op jit(solution)/shard_map/ppermute | solution.py:24
  26.5 15.7 %collective-permute-start.33 = (bf16[65,32,128]{2,1,0:T(8,128)(2,1)S(1)}, bf16[65,32,128]{2,1,0:T(8,128)(2,1)S(1)}, u32[]{:S(2)}, u32[]{:S(2)}) collective-permute-start(bf16[65,32,128]{2,1,0:T(8,128)(2,1)S(1)} %get-tuple-element.146.own), channel_id=1, source_target_pairs={{0,2},{1,3},{2,0},{3,1},{4,6},{5,7},{6,4},{7,5},{8,10},{9,11},{10,... | collective-permute-start | bytes 1597448 | tf_op jit(solution)/shard_map/ppermute | solution.py:34
  27.8 15.5 %collective-permute-start.32 = (bf16[65,32,128]{2,1,0:T(8,128)(2,1)S(1)}, bf16[65,32,128]{2,1,0:T(8,128)(2,1)S(1)}, u32[]{:S(2)}, u32[]{:S(2)}) collective-permute-start(bf16[65,32,128]{2,1,0:T(8,128)(2,1)S(1)} %get-tuple-element.146.own), channel_id=1, source_target_pairs={{0,8},{1,9},{2,10},{3,11},{4,12},{5,13},{6,14},{7,15},{8,0},{9,1},... | collective-permute-start | bytes 1597448 | tf_op jit(solution)/shard_map/ppermute | solution.py:29
  30.8 2.8 %collective-permute-start.27 = (bf16[16,32,128]{2,1,0:T(8,128)(2,1)S(1)}, bf16[16,32,128]{2,1,0:T(8,128)(2,1)S(1)}, u32[]{:S(2)}, u32[]{:S(2)}) collective-permute-start(bf16[16,32,128]{2,1,0:T(8,128)(2,1)S(1)} %get-tuple-element.139), channel_id=1, source_target_pairs={{0,240},{16,0},{32,16},{48,32},{64,48},{80,64},{96,80},{112,96},{1... | collective-permute-start | bytes 393224 | tf_op jit(solution)/shard_map/ppermute | solution.py:24
  31.1 6.2 %collective-permute-start.28 = (bf16[16,32,128]{2,1,0:T(8,128)(2,1)S(1)}, bf16[16,32,128]{2,1,0:T(8,128)(2,1)S(1)}, u32[]{:S(2)}, u32[]{:S(2)}) collective-permute-start(bf16[16,32,128]{2,1,0:T(8,128)(2,1)S(1)} %get-tuple-element.140), channel_id=1, source_target_pairs={{0,16},{16,32},{32,48},{48,64},{64,80},{80,96},{96,112},{112,128},... | collective-permute-start | bytes 393224 | tf_op jit(solution)/shard_map/ppermute | solution.py:24
  31.3 7.6 %collective-permute-start.29 = (bf16[16,32,128]{2,1,0:T(8,128)(2,1)S(1)}, bf16[16,32,128]{2,1,0:T(8,128)(2,1)S(1)}, u32[]{:S(2)}, u32[]{:S(2)}) collective-permute-start(bf16[16,32,128]{2,1,0:T(8,128)(2,1)S(1)} %get-tuple-element.141), channel_id=1, source_target_pairs={{0,32},{16,48},{32,64},{48,80},{64,96},{80,112},{96,128},{112,144}... | collective-permute-start | bytes 393224 | tf_op jit(solution)/shard_map/ppermute | solution.py:24
  44.0 22.0 %collective-permute-start.35 = (bf16[97,32,128]{2,1,0:T(8,128)(2,1)}, bf16[97,32,128]{2,1,0:T(8,128)(2,1)S(1)}, u32[]{:S(2)}, u32[]{:S(2)}) collective-permute-start(bf16[97,32,128]{2,1,0:T(8,128)(2,1)} %constant_dynamic-update-slice_fusion.2), channel_id=1, source_target_pairs={{0,3},{1,0},{2,1},{3,2},{4,7},{5,4},{6,5},{7,6},{8,11},{9,8},{10,9... | collective-permute-start | bytes 2383880 | tf_op jit(solution)/shard_map/ppermute | solution.py:34
  44.6 24.7 %collective-permute-start.34 = (bf16[97,32,128]{2,1,0:T(8,128)(2,1)}, bf16[97,32,128]{2,1,0:T(8,128)(2,1)S(1)}, u32[]{:S(2)}, u32[]{:S(2)}) collective-permute-start(bf16[97,32,128]{2,1,0:T(8,128)(2,1)} %constant_dynamic-update-slice_fusion.2), channel_id=1, source_target_pairs={{0,1},{1,2},{2,3},{3,0},{4,5},{5,6},{6,7},{7,4},{8,9},{9,10},{10,1... | collective-permute-start | bytes 2383880 | tf_op jit(solution)/shard_map/ppermute | solution.py:34
  47.3 25.6 %collective-permute-start.37 = (bf16[97,32,128]{2,1,0:T(8,128)(2,1)}, bf16[97,32,128]{2,1,0:T(8,128)(2,1)S(1)}, u32[]{:S(2)}, u32[]{:S(2)}) collective-permute-start(bf16[97,32,128]{2,1,0:T(8,128)(2,1)} %constant_dynamic-update-slice_fusion), channel_id=1, source_target_pairs={{0,12},{1,13},{2,14},{3,15},{4,0},{5,1},{6,2},{7,3},{8,4},{9,5},{1... | collective-permute-start | bytes 2383880 | tf_op jit(solution)/shard_map/ppermute | solution.py:29
  50.0 25.1 %collective-permute-start.36 = (bf16[97,32,128]{2,1,0:T(8,128)(2,1)}, bf16[97,32,128]{2,1,0:T(8,128)(2,1)S(1)}, u32[]{:S(2)}, u32[]{:S(2)}) collective-permute-start(bf16[97,32,128]{2,1,0:T(8,128)(2,1)} %constant_dynamic-update-slice_fusion), channel_id=1, source_target_pairs={{0,4},{1,5},{2,6},{3,7},{4,8},{5,9},{6,10},{7,11},{8,12},{9,13},{1... | collective-permute-start | bytes 2383880 | tf_op jit(solution)/shard_map/ppermute | solution.py:29
  58.7 18.7 %collective-permute-start.30 = (bf16[32,32,128]{2,1,0:T(8,128)(2,1)S(1)}, bf16[32,32,128]{2,1,0:T(8,128)(2,1)}, u32[]{:S(2)}, u32[]{:S(2)}) collective-permute-start(bf16[32,32,128]{2,1,0:T(8,128)(2,1)S(1)} %pad_maximum_fusion.1.own), channel_id=1, source_target_pairs={{0,2},{1,3},{2,0},{3,1},{4,6},{5,7},{6,4},{7,5},{8,10},{9,11},{10,... | collective-permute-start | bytes 786440 | tf_op jit(solution)/shard_map/ppermute | solution.py:34
  66.0 11.5 %collective-permute-start.31 = (bf16[32,32,128]{2,1,0:T(8,128)(2,1)}, bf16[32,32,128]{2,1,0:T(8,128)(2,1)}, u32[]{:S(2)}, u32[]{:S(2)}) collective-permute-start(bf16[32,32,128]{2,1,0:T(8,128)(2,1)} %pad_maximum_fusion.2.own), channel_id=1, source_target_pairs={{0,8},{1,9},{2,10},{3,11},{4,12},{5,13},{6,14},{7,15},{8,0},{9,1},... | collective-permute-start | bytes 786440 | tf_op jit(solution)/shard_map/ppermute | solution.py:29
  69.0 6.0 %copy-start.7 = (bf16[65,32,128]{2,1,0:T(8,128)(2,1)S(1)}, bf16[65,32,128]{2,1,0:T(8,128)(2,1)}, u32[]{:S(2)}) copy-start(bf16[65,32,128]{2,1,0:T(8,128)(2,1)} %copy-done.6) | copy-start | bytes 1597444
  79.9 16.3 %collective-permute-start.38 = (bf16[104,16,128]{2,1,0:T(8,128)(2,1)S(1)}, bf16[104,16,128]{2,1,0:T(8,128)(2,1)S(1)}, u32[]{:S(2)}, u32[]{:S(2)}) collective-permute-start(bf16[104,16,128]{2,1,0:T(8,128)(2,1)S(1)} %get-tuple-element.162), channel_id=1, source_target_pairs={{0,4},{1,5},{2,6},{3,7},{4,8},{5,9},{6,10},{7,11},{8,12},{9,13},{1... | collective-permute-start | bytes 1277960 | tf_op jit(solution)/shard_map/ppermute | solution.py:29
  80.0 17.8 %collective-permute-start.39 = (bf16[104,16,128]{2,1,0:T(8,128)(2,1)S(1)}, bf16[104,16,128]{2,1,0:T(8,128)(2,1)S(1)}, u32[]{:S(2)}, u32[]{:S(2)}) collective-permute-start(bf16[104,16,128]{2,1,0:T(8,128)(2,1)S(1)} %get-tuple-element.163), channel_id=1, source_target_pairs={{0,8},{1,9},{2,10},{3,11},{4,12},{5,13},{6,14},{7,15},{8,0},{9,1},... | collective-permute-start | bytes 1277960 | tf_op jit(solution)/shard_map/ppermute | solution.py:29
  82.0 15.9 %collective-permute-start.40 = (bf16[104,16,128]{2,1,0:T(8,128)(2,1)S(1)}, bf16[104,16,128]{2,1,0:T(8,128)(2,1)S(1)}, u32[]{:S(2)}, u32[]{:S(2)}) collective-permute-start(bf16[104,16,128]{2,1,0:T(8,128)(2,1)S(1)} %get-tuple-element.164), channel_id=1, source_target_pairs={{0,12},{1,13},{2,14},{3,15},{4,0},{5,1},{6,2},{7,3},{8,4},{9,5},{1... | collective-permute-start | bytes 1277960 | tf_op jit(solution)/shard_map/ppermute | solution.py:29
  85.9 15.0 %collective-permute-start.41 = (bf16[104,16,128]{2,1,0:T(8,128)(2,1)S(1)}, bf16[104,16,128]{2,1,0:T(8,128)(2,1)S(1)}, u32[]{:S(2)}, u32[]{:S(2)}) collective-permute-start(bf16[104,16,128]{2,1,0:T(8,128)(2,1)S(1)} %get-tuple-element.172), channel_id=1, source_target_pairs={{0,1},{1,2},{2,3},{3,0},{4,5},{5,6},{6,7},{7,4},{8,9},{9,10},{10,1... | collective-permute-start | bytes 1277960 | tf_op jit(solution)/shard_map/ppermute | solution.py:34
  89.5 11.4 %collective-permute-start.42 = (bf16[104,16,128]{2,1,0:T(8,128)(2,1)S(1)}, bf16[104,16,128]{2,1,0:T(8,128)(2,1)S(1)}, u32[]{:S(2)}, u32[]{:S(2)}) collective-permute-start(bf16[104,16,128]{2,1,0:T(8,128)(2,1)S(1)} %get-tuple-element.173), channel_id=1, source_target_pairs={{0,2},{1,3},{2,0},{3,1},{4,6},{5,7},{6,4},{7,5},{8,10},{9,11},{10,... | collective-permute-start | bytes 1277960 | tf_op jit(solution)/shard_map/ppermute | solution.py:34
  96.2 9.3 %collective-permute-start.43 = (bf16[104,16,128]{2,1,0:T(8,128)(2,1)S(1)}, bf16[104,16,128]{2,1,0:T(8,128)(2,1)S(1)}, u32[]{:S(2)}, u32[]{:S(2)}) collective-permute-start(bf16[104,16,128]{2,1,0:T(8,128)(2,1)S(1)} %get-tuple-element.174), channel_id=1, source_target_pairs={{0,3},{1,0},{2,1},{3,2},{4,7},{5,4},{6,5},{7,6},{8,11},{9,8},{10,9... | collective-permute-start | bytes 1277960 | tf_op jit(solution)/shard_map/ppermute | solution.py:34
  (10 other events, 22.0 us)

commit v4 on v3

--- a/solution.py
+++ b/solution.py
@@ -420,14 +420,33 @@
     )(entries, weighted, *shards, *begun)
 
 
-def gather_up(parts, places):
+def total(v, parts):
+    def kernel(kept, first, second, third, out_ref):
+        value = kept[...]
+        for part in (first, second, third):
+            value = value + part[...].astype(F32)
+        out_ref[...] = value.reshape(2 * PAIRS, 8, 128)
+
+    vmem = pl.BlockSpec(memory_space=pltpu.VMEM)
+    return pl.pallas_call(
+        kernel,
+        out_shape=jax.ShapeDtypeStruct((2 * PAIRS, 8, 128), F32),
+        in_specs=[vmem] * 4,
+        out_specs=vmem,
+        compiler_params=params(16),
+        cost_estimate=cost(0, 3 * 1024 * 1024),
+        name=f"total_{v}",
+    )(*parts)
+
+
+def gather_up(total_0, parts, places):
     def kernel(place_ref, *refs):
-        ins, out_ref, sums = refs[:8], refs[8], refs[9]
-        for v in range(2):
-            value = ins[4 * v][...]
-            for t in range(1, 4):
-                value = value + ins[4 * v + t][...].astype(F32)
-            sums[2 * PAIRS * v : 2 * PAIRS * v + 2 * PAIRS] = value.reshape(2 * PAIRS, 8, 128)
+        total_ref, ins, out_ref, sums = refs[0], refs[1:5], refs[5], refs[6]
+        value = ins[0][...]
+        for part in ins[1:]:
+            value = value + part[...].astype(F32)
+        sums[0 : 2 * PAIRS] = total_ref[...]
+        sums[2 * PAIRS : 4 * PAIRS] = value.reshape(2 * PAIRS, 8, 128)
         sums[4 * PAIRS] = jnp.zeros((8, 128), F32)
         for i in range(64):
             for k in range(2):
@@ -439,13 +458,13 @@
     return pl.pallas_call(
         kernel,
         out_shape=jax.ShapeDtypeStruct((64, 8, 8, 128), F32),
-        in_specs=[smem] + [vmem] * 8,
+        in_specs=[smem] + [vmem] * 5,
         out_specs=vmem,
         scratch_shapes=[pltpu.VMEM((4 * PAIRS + 1, 8, 128), F32)],
         compiler_params=params(16),
         cost_estimate=cost(0, 7 * 1024 * 1024),
         name="gather_up",
-    )(places, *parts)
+    )(places, total_0, *parts)
 
 
 def scattered(parts_x, parts_y):
@@ -493,7 +512,8 @@
     )
     parts_x = density_list(0, entries, weighted_y, [half_y, *beside[:2], half_far_y], begun_y)
     parts_y = density_list(1, entries, weighted_x, [half_x, *beside[2:], half_far_x], begun_x)
-    density = gather_up(scattered(parts_x, parts_y), places)
+    arrived = scattered(parts_x, parts_y)
+    density = gather_up(total(0, arrived[:4]), arrived[4:], places)
 
     def again(density, coef, halo, *rest):
         return any_way(coef, halo, *rest)

time: 109 us -> 109 us (level)
  no operation moved by 1% of the time
where the time goes in v4:
time: 109 us
  Pallas kernels  33.3 us (31%)
  starting transfers between devices  31.5 us (29%)
  waiting for transfers between devices  31.5 us (29%)
  local copies, waits for them, and re-layouts  9.58 us (9%)
  other arithmetic  1.82 us (2%)
    ppermute x7, waiting for transfers between devices, along_y(): return lax.ppermute(value, 'st', pairs)  16.7 us
    ppermute x7, starting transfers between devices, along_x(): return lax.ppermute(value, 'st', pairs)  12.3 us
    ppermute x8, starting transfers between devices, along_dom(): return lax.ppermute(value, 'dom', [(i, (i + by) % 16) for i in range(16)])  10.1 us
    ppermute x7, starting transfers between devices, along_y(): return lax.ppermute(value, 'st', pairs)  9.18 us
    ppermute x7, waiting for transfers between devices, along_x(): return lax.ppermute(value, 'st', pairs)  9.09 us
    pallas_call x1, Pallas kernels, coef_all(): pl.pallas_call(kernel, grid=(64 // ROWS,), out_shape=[jax.ShapeDtypeStruc...  8.49 us
    pallas_call x1, Pallas kernels, plan(): pl.pallas_call(kernel, out_shape=[jax.ShapeDtypeStruct((2, LIST + 1), jnp...  7.93 us
    unnamed x25, local copies, waits for them, and re-layouts  6.2 us
  transfers between devices with their start and end apart: 22, of which 12 were waited for; matrix products, arithmetic and copies ran while one was open for 5% of the time, Pallas kernels for 17%

profile of v4, /device:TPU:24, one launch (start us, length us, event | category | flops | bytes accessed | tf_op | source)
XLA Modules:
  0.0 108.5 jit_solution(4022685681734331751)
XLA Ops:
  2.4 5.9 %collective-permute-start.22 = (bf16[16,32,128]{2,1,0:T(8,128)(2,1)S(1)}, bf16[16,32,128]{2,1,0:T(8,128)(2,1)S(1)}, u32[]{:S(2)}, u32[]{:S(2)}) collective-permute-start(bf16[16,32,128]{2,1,0:T(8,128)(2,1)S(1)} %get-tuple-element.134), channel_id=1, source_target_pairs={{0,224},{16,240},{32,0},{48,16},{64,32},{80,48},{96,64},{112,80},{... | collective-permute-start | bytes 393224 | tf_op jit(solution)/shard_map/ppermute | solution.py:24
  12.1 3.3 %coef_own.1.first_ref = f32[64,32,128]{2,1,0:T(8,128)S(1)} custom-call(s32[64,8]{1,0:T(8,128)S(1)} %copy.17.ref_ref, bf16[64,8,128,128]{3,2,1,0:T(8,128)(2,1)} %blocks_3.1, bf16[32,8192]{1,0:T(8,128)(2,1)S(1)} %copy-done.1), custom_call_target="tpu_custom_call" | custom-call | flops 134217728 | bytes 6291456 | tf_op jit(solution)/shard_map/coef_own/pallas_call | solution.py:78
  16.5 8.5 %coef_all.1 = (bf16[65,32,128]{2,1,0:T(8,128)(2,1)S(1)}, bf16[97,32,128]{2,1,0:T(8,128)(2,1)}, bf16[97,32,128]{2,1,0:T(8,128)(2,1)}, bf16[16,32,128]{2,1,0:T(8,1...) custom-call(s32[64,8]{1,0:T(8,128)S(1)} %copy.17.ref_ref, ...), custom_call_target="tpu_custom_call" | custom-call | flops 402653184 | bytes 14680064 | tf_op jit(solution)/shard_map/coef_all/pallas_call | solution.py:139
  24.9 1.6 %collective-permute-start.26 = (bf16[16,32,128]{2,1,0:T(8,128)(2,1)S(1)}, bf16[16,32,128]{2,1,0:T(8,128)(2,1)S(1)}, u32[]{:S(2)}, u32[]{:S(2)}) collective-permute-start(bf16[16,32,128]{2,1,0:T(8,128)(2,1)S(1)} %get-tuple-element.138), channel_id=1, source_target_pairs={{0,224},{16,240},{32,0},{48,16},{64,32},{80,48},{96,64},{112,80},{... | collective-permute-start | bytes 393224 | tf_op jit(solution)/shard_map/ppermute | solution.py:24
  27.8 3.0 %collective-permute-start.32 = (bf16[65,32,128]{2,1,0:T(8,128)(2,1)S(1)}, bf16[65,32,128]{2,1,0:T(8,128)(2,1)S(1)}, u32[]{:S(2)}, u32[]{:S(2)}) collective-permute-start(bf16[65,32,128]{2,1,0:T(8,128)(2,1)S(1)} %get-tuple-element.146.own), channel_id=1, source_target_pairs={{0,8},{1,9},{2,10},{3,11},{4,12},{5,13},{6,14},{7,15},{8,0},{9,1},... | collective-permute-start | bytes 1597448 | tf_op jit(solution)/shard_map/ppermute | solution.py:29
  34.3 3.1 %collective-permute-done.28 = bf16[16,32,128]{2,1,0:T(8,128)(2,1)S(1)} collective-permute-done((bf16[16,32,128]{2,1,0:T(8,128)(2,1)S(1)}, bf16[16,32,128]{2,1,0:T(8,128)(2,1)S(1)}, u32[]{:S(2)}, u32[]{:S(2)}) %collective-permute-start.28) | collective-permute-done | bytes 131104 | tf_op jit(solution)/shard_map/ppermute | solution.py:24
  39.5 2.7 %collective-permute-done.33.far = bf16[65,32,128]{2,1,0:T(8,128)(2,1)S(1)} collective-permute-done((bf16[65,32,128]{2,1,0:T(8,128)(2,1)S(1)}, bf16[65,32,128]{2,1,0:T(8,128)(2,1)S(1)}, u32[]{:S(2)}, u32[]{:S(2)}) %collective-permute-start.33) | collective-permute-done | bytes 532512 | tf_op jit(solution)/shard_map/ppermute | solution.py:34
  44.6 2.7 %collective-permute-start.34 = (bf16[97,32,128]{2,1,0:T(8,128)(2,1)}, bf16[97,32,128]{2,1,0:T(8,128)(2,1)S(1)}, u32[]{:S(2)}, u32[]{:S(2)}) collective-permute-start(bf16[97,32,128]{2,1,0:T(8,128)(2,1)} %constant_dynamic-update-slice_fusion.2), channel_id=1, source_target_pairs={{0,1},{1,2},{2,3},{3,0},{4,5},{5,6},{6,7},{7,4},{8,9},{9,10},{10,1... | collective-permute-start | bytes 2383880 | tf_op jit(solution)/shard_map/ppermute | solution.py:34
  47.3 2.8 %collective-permute-start.37 = (bf16[97,32,128]{2,1,0:T(8,128)(2,1)}, bf16[97,32,128]{2,1,0:T(8,128)(2,1)S(1)}, u32[]{:S(2)}, u32[]{:S(2)}) collective-permute-start(bf16[97,32,128]{2,1,0:T(8,128)(2,1)} %constant_dynamic-update-slice_fusion), channel_id=1, source_target_pairs={{0,12},{1,13},{2,14},{3,15},{4,0},{5,1},{6,2},{7,3},{8,4},{9,5},{1... | collective-permute-start | bytes 2383880 | tf_op jit(solution)/shard_map/ppermute | solution.py:29
  50.0 7.9 %plan.1 = (s32[2,145]{1,0:T(2,128)S(1)}, s32[64,8]{1,0:T(8,128)S(1)}, s32[1,1]{1,0:T(1,128)}) custom-call(s32[64,8]{1,0:T(8,128)S(1)} %copy.17.ref_ref, s32[1,64]{1,0:T(1,128)S(1)} %bitcast.9), custom_call_target="tpu_custom_call" | custom-call | bytes 25165824 | tf_op jit(solution)/shard_map/plan/pallas_call | solution.py:338
  59.8 6.2 %collective-permute-done.35.higher = bf16[97,32,128]{2,1,0:T(8,128)(2,1)S(1)} collective-permute-done((bf16[97,32,128]{2,1,0:T(8,128)(2,1)}, bf16[97,32,128]{2,1,0:T(8,128)(2,1)S(1)}, u32[]{:S(2)}, u32[]{:S(2)}) %collective-permute-start.35) | collective-permute-done | bytes 794656 | tf_op jit(solution)/shard_map/ppermute | solution.py:34
  66.0 3.0 %collective-permute-start.31 = (bf16[32,32,128]{2,1,0:T(8,128)(2,1)}, bf16[32,32,128]{2,1,0:T(8,128)(2,1)}, u32[]{:S(2)}, u32[]{:S(2)}) collective-permute-start(bf16[32,32,128]{2,1,0:T(8,128)(2,1)} %pad_maximum_fusion.2.own), channel_id=1, source_target_pairs={{0,8},{1,9},{2,10},{3,11},{4,12},{5,13},{6,14},{7,15},{8,0},{9,1},... | collective-permute-start | bytes 786440 | tf_op jit(solution)/shard_map/ppermute | solution.py:29
  70.4 2.4 %weigh_0.1 = (bf16[64,32,128]{2,1,0:T(8,128)(2,1)S(1)}, f32[32,16,128]{2,1,0:T(8,128)S(1)}, bf16[32,16,128]{2,1,0:T(8,128)(2,1)S(1)}, bf16[32,16,128]{2,1,0:T(8,128)(2,1)S(1)}, bf16[32,16,128]{2,1,0:T(8,128)(2,1)S(1)}) custom-call(s32[2]{0:T(128)S(1)} %pad_add_fusion.here_ref, s32[64,8]{1,0:T(8,128)S(1)} %copy.17.ref_ref, bf16[65,32,128]{2,1,0:T(8,128)(2,1)} %copy-done.16, ...), custom_call_target="tpu_custom_call" | custom-call | flops 67108864 | bytes 4194304 | tf_op jit(solution)/shard_map/weigh_0/pallas_call | solution.py:379
  72.8 2.3 %collective-permute-done.36.lower = bf16[97,32,128]{2,1,0:T(8,128)(2,1)S(1)} collective-permute-done((bf16[97,32,128]{2,1,0:T(8,128)(2,1)}, bf16[97,32,128]{2,1,0:T(8,128)(2,1)S(1)}, u32[]{:S(2)}, u32[]{:S(2)}) %collective-permute-start.36) | collective-permute-done | bytes 794656 | tf_op jit(solution)/shard_map/ppermute | solution.py:29
  75.1 2.4 %weigh_1.1 = (bf16[64,32,128]{2,1,0:T(8,128)(2,1)S(1)}, f32[32,16,128]{2,1,0:T(8,128)S(1)}, bf16[32,16,128]{2,1,0:T(8,128)(2,1)S(1)}, bf16[32,16,128]{2,1,0:T(8,128)(2,1)S(1)}, bf16[32,16,128]{2,1,0:T(8,128)(2,1)S(1)}) custom-call(s32[2]{0:T(128)S(1)} %pad_add_fusion.here_ref, s32[64,8]{1,0:T(8,128)S(1)} %copy.17.ref_ref, ...), custom_call_target="tpu_custom_call" | custom-call | flops 67108864 | bytes 4194304 | tf_op jit(solution)/shard_map/weigh_1/pallas_call | solution.py:379
  77.5 2.4 %density_list_0.1 = (f32[104,16,128]{2,1,0:T(8,128)S(1)}, bf16[104,16,128]{2,1,0:T(8,128)(2,1)S(1)}, bf16[104,16,128]{2,1,0:T(8,128)(2,1)S(1)}, bf16[104,16,128]{2,1,0:T(8,128)(2,1)S(1)}) custom-call(s32[2,145]{1,0:T(2,128)S(1)} %get-tuple-element.143.entry_ref, bf16[64,32,128]{2,1,0:T(8,128)(2,1)S(1)} %get-tuple-element.155.w_ref, ...), custom_call_target="tpu_custom_call" | custom-call | flops 150994944 | bytes 4194304 | tf_op jit(solution)/shard_map/density_list_0/pallas_call | solution.py:411
  80.0 2.0 %collective-permute-start.39 = (bf16[104,16,128]{2,1,0:T(8,128)(2,1)S(1)}, bf16[104,16,128]{2,1,0:T(8,128)(2,1)S(1)}, u32[]{:S(2)}, u32[]{:S(2)}) collective-permute-start(bf16[104,16,128]{2,1,0:T(8,128)(2,1)S(1)} %get-tuple-element.163), channel_id=1, source_target_pairs={{0,8},{1,9},{2,10},{3,11},{4,12},{5,13},{6,14},{7,15},{8,0},{9,1},... | collective-permute-start | bytes 1277960 | tf_op jit(solution)/shard_map/ppermute | solution.py:29
  82.0 1.4 %collective-permute-start.40 = (bf16[104,16,128]{2,1,0:T(8,128)(2,1)S(1)}, bf16[104,16,128]{2,1,0:T(8,128)(2,1)S(1)}, u32[]{:S(2)}, u32[]{:S(2)}) collective-permute-start(bf16[104,16,128]{2,1,0:T(8,128)(2,1)S(1)} %get-tuple-element.164), channel_id=1, source_target_pairs={{0,12},{1,13},{2,14},{3,15},{4,0},{5,1},{6,2},{7,3},{8,4},{9,5},{1... | collective-permute-start | bytes 1277960 | tf_op jit(solution)/shard_map/ppermute | solution.py:29
  83.4 2.5 %density_list_1.1 = (f32[104,16,128]{2,1,0:T(8,128)S(1)}, bf16[104,16,128]{2,1,0:T(8,128)(2,1)S(1)}, bf16[104,16,128]{2,1,0:T(8,128)(2,1)S(1)}, bf16[104,16,128]{2,1,0:T(8,128)(2,1)S(1)}) custom-call(s32[2,145]{1,0:T(2,128)S(1)} %get-tuple-element.143.entry_ref, bf16[64,32,128]{2,1,0:T(8,128)(2,1)S(1)} %get-tuple-element.165.w_ref, ...), custom_call_target="tpu_custom_call" | custom-call | flops 150994944 | bytes 4194304 | tf_op jit(solution)/shard_map/density_list_1/pallas_call | solution.py:411
  85.9 3.6 %collective-permute-start.41 = (bf16[104,16,128]{2,1,0:T(8,128)(2,1)S(1)}, bf16[104,16,128]{2,1,0:T(8,128)(2,1)S(1)}, u32[]{:S(2)}, u32[]{:S(2)}) collective-permute-start(bf16[104,16,128]{2,1,0:T(8,128)(2,1)S(1)} %get-tuple-element.172), channel_id=1, source_target_pairs={{0,1},{1,2},{2,3},{3,0},{4,5},{5,6},{6,7},{7,4},{8,9},{9,10},{10,1... | collective-permute-start | bytes 1277960 | tf_op jit(solution)/shard_map/ppermute | solution.py:34
  89.5 6.7 %collective-permute-done.38.first = bf16[104,16,128]{2,1,0:T(8,128)(2,1)S(1)} collective-permute-done((bf16[104,16,128]{2,1,0:T(8,128)(2,1)S(1)}, bf16[104,16,128]{2,1,0:T(8,128)(2,1)S(1)}, u32[]{:S(2)}, u32[]{:S(2)}) %collective-permute-start.38) | collective-permute-done | bytes 426016 | tf_op jit(solution)/shard_map/ppermute | solution.py:29
  98.0 2.9 %collective-permute-done.41.refs_2_ = bf16[104,16,128]{2,1,0:T(8,128)(2,1)S(1)} collective-permute-done((bf16[104,16,128]{2,1,0:T(8,128)(2,1)S(1)}, bf16[104,16,128]{2,1,0:T(8,128)(2,1)S(1)}, u32[]{:S(2)}, u32[]{:S(2)}) %collective-permute-start.41) | collective-permute-done | bytes 426016 | tf_op jit(solution)/shard_map/ppermute | solution.py:34
  100.9 4.6 %collective-permute-done.43.refs_4_ = bf16[104,16,128]{2,1,0:T(8,128)(2,1)S(1)} collective-permute-done((bf16[104,16,128]{2,1,0:T(8,128)(2,1)S(1)}, bf16[104,16,128]{2,1,0:T(8,128)(2,1)S(1)}, u32[]{:S(2)}, u32[]{:S(2)}) %collective-permute-start.43) | collective-permute-done | bytes 426016 | tf_op jit(solution)/shard_map/ppermute | solution.py:34
  105.5 3.0 %gather_up.1 = f32[64,8,8,128]{3,2,1,0:T(8,128)} custom-call(s32[64,8]{1,0:T(8,128)S(1)} %get-tuple-element.133.place_ref, f32[208,8,128]{2,1,0:T(8,128)S(1)} %total_0.1.refs_0_, f32[104,16,128]{2,1,0:T(8,128)S(1)} %get-tuple-element.171.refs_1_, bf16[104,16,128]{2,1,0:T(8,128)(2,1)S(1)} %collective-permute-done.41.refs_2_, ...), custom_call_target="tpu_custom_call" | custom-call | bytes 7340032 | tf_op jit(solution)/shard_map/gather_up/pallas_call | solution.py:458
  (65 shorter events, 20.9 us)
Async XLA Ops:
  2.4 13.0 %collective-permute-start.22 = (bf16[16,32,128]{2,1,0:T(8,128)(2,1)S(1)}, bf16[16,32,128]{2,1,0:T(8,128)(2,1)S(1)}, u32[]{:S(2)}, u32[]{:S(2)}) collective-permute-start(bf16[16,32,128]{2,1,0:T(8,128)(2,1)S(1)} %get-tuple-element.134), channel_id=1, source_target_pairs={{0,224},{16,240},{32,0},{48,16},{64,32},{80,48},{96,64},{112,80},{... | collective-permute-start | bytes 393224 | tf_op jit(solution)/shard_map/ppermute | solution.py:24
  8.4 7.1 %collective-permute-start.23 = (bf16[16,32,128]{2,1,0:T(8,128)(2,1)S(1)}, bf16[16,32,128]{2,1,0:T(8,128)(2,1)S(1)}, u32[]{:S(2)}, u32[]{:S(2)}) collective-permute-start(bf16[16,32,128]{2,1,0:T(8,128)(2,1)S(1)} %get-tuple-element.135), channel_id=1, source_target_pairs={{0,240},{16,0},{32,16},{48,32},{64,48},{80,64},{96,80},{112,96},{1... | collective-permute-start | bytes 393224 | tf_op jit(solution)/shard_map/ppermute | solution.py:24
  8.5 6.9 %collective-permute-start.24 = (bf16[16,32,128]{2,1,0:T(8,128)(2,1)S(1)}, bf16[16,32,128]{2,1,0:T(8,128)(2,1)S(1)}, u32[]{:S(2)}, u32[]{:S(2)}) collective-permute-start(bf16[16,32,128]{2,1,0:T(8,128)(2,1)S(1)} %get-tuple-element.136), channel_id=1, source_target_pairs={{0,16},{16,32},{32,48},{48,64},{64,80},{80,96},{96,112},{112,128},... | collective-permute-start | bytes 393224 | tf_op jit(solution)/shard_map/ppermute | solution.py:24
  8.9 7.6 %collective-permute-start.25 = (bf16[16,32,128]{2,1,0:T(8,128)(2,1)S(1)}, bf16[16,32,128]{2,1,0:T(8,128)(2,1)S(1)}, u32[]{:S(2)}, u32[]{:S(2)}) collective-permute-start(bf16[16,32,128]{2,1,0:T(8,128)(2,1)S(1)} %get-tuple-element.137), channel_id=1, source_target_pairs={{0,32},{16,48},{32,64},{48,80},{64,96},{80,112},{96,128},{112,144}... | collective-permute-start | bytes 393224 | tf_op jit(solution)/shard_map/ppermute | solution.py:24
  24.9 41.1 %copy-start.16 = (bf16[65,32,128]{2,1,0:T(8,128)(2,1)}, bf16[65,32,128]{2,1,0:T(8,128)(2,1)S(1)}, u32[]{:S(2)}) copy-start(bf16[65,32,128]{2,1,0:T(8,128)(2,1)S(1)} %get-tuple-element.146.own) | copy-start | bytes 1597444
  24.9 6.4 %collective-permute-start.26 = (bf16[16,32,128]{2,1,0:T(8,128)(2,1)S(1)}, bf16[16,32,128]{2,1,0:T(8,128)(2,1)S(1)}, u32[]{:S(2)}, u32[]{:S(2)}) collective-permute-start(bf16[16,32,128]{2,1,0:T(8,128)(2,1)S(1)} %get-tuple-element.138), channel_id=1, source_target_pairs={{0,224},{16,240},{32,0},{48,16},{64,32},{80,48},{96,64},{112,80},{... | collective-permute-start | bytes 393224 | tf_op jit(solution)/shard_map/ppermute | solution.py:24
  26.5 15.7 %collective-permute-start.33 = (bf16[65,32,128]{2,1,0:T(8,128)(2,1)S(1)}, bf16[65,32,128]{2,1,0:T(8,128)(2,1)S(1)}, u32[]{:S(2)}, u32[]{:S(2)}) collective-permute-start(bf16[65,32,128]{2,1,0:T(8,128)(2,1)S(1)} %get-tuple-element.146.own), channel_id=1, source_target_pairs={{0,2},{1,3},{2,0},{3,1},{4,6},{5,7},{6,4},{7,5},{8,10},{9,11},{10,... | collective-permute-start | bytes 1597448 | tf_op jit(solution)/shard_map/ppermute | solution.py:34
  27.8 15.4 %collective-permute-start.32 = (bf16[65,32,128]{2,1,0:T(8,128)(2,1)S(1)}, bf16[65,32,128]{2,1,0:T(8,128)(2,1)S(1)}, u32[]{:S(2)}, u32[]{:S(2)}) collective-permute-start(bf16[65,32,128]{2,1,0:T(8,128)(2,1)S(1)} %get-tuple-element.146.own), channel_id=1, source_target_pairs={{0,8},{1,9},{2,10},{3,11},{4,12},{5,13},{6,14},{7,15},{8,0},{9,1},... | collective-permute-start | bytes 1597448 | tf_op jit(solution)/shard_map/ppermute | solution.py:29
  30.8 2.8 %collective-permute-start.27 = (bf16[16,32,128]{2,1,0:T(8,128)(2,1)S(1)}, bf16[16,32,128]{2,1,0:T(8,128)(2,1)S(1)}, u32[]{:S(2)}, u32[]{:S(2)}) collective-permute-start(bf16[16,32,128]{2,1,0:T(8,128)(2,1)S(1)} %get-tuple-element.139), channel_id=1, source_target_pairs={{0,240},{16,0},{32,16},{48,32},{64,48},{80,64},{96,80},{112,96},{1... | collective-permute-start | bytes 393224 | tf_op jit(solution)/shard_map/ppermute | solution.py:24
  31.1 6.2 %collective-permute-start.28 = (bf16[16,32,128]{2,1,0:T(8,128)(2,1)S(1)}, bf16[16,32,128]{2,1,0:T(8,128)(2,1)S(1)}, u32[]{:S(2)}, u32[]{:S(2)}) collective-permute-start(bf16[16,32,128]{2,1,0:T(8,128)(2,1)S(1)} %get-tuple-element.140), channel_id=1, source_target_pairs={{0,16},{16,32},{32,48},{48,64},{64,80},{80,96},{96,112},{112,128},... | collective-permute-start | bytes 393224 | tf_op jit(solution)/shard_map/ppermute | solution.py:24
  31.3 7.5 %collective-permute-start.29 = (bf16[16,32,128]{2,1,0:T(8,128)(2,1)S(1)}, bf16[16,32,128]{2,1,0:T(8,128)(2,1)S(1)}, u32[]{:S(2)}, u32[]{:S(2)}) collective-permute-start(bf16[16,32,128]{2,1,0:T(8,128)(2,1)S(1)} %get-tuple-element.141), channel_id=1, source_target_pairs={{0,32},{16,48},{32,64},{48,80},{64,96},{80,112},{96,128},{112,144}... | collective-permute-start | bytes 393224 | tf_op jit(solution)/shard_map/ppermute | solution.py:24
  44.0 22.0 %collective-permute-start.35 = (bf16[97,32,128]{2,1,0:T(8,128)(2,1)}, bf16[97,32,128]{2,1,0:T(8,128)(2,1)S(1)}, u32[]{:S(2)}, u32[]{:S(2)}) collective-permute-start(bf16[97,32,128]{2,1,0:T(8,128)(2,1)} %constant_dynamic-update-slice_fusion.2), channel_id=1, source_target_pairs={{0,3},{1,0},{2,1},{3,2},{4,7},{5,4},{6,5},{7,6},{8,11},{9,8},{10,9... | collective-permute-start | bytes 2383880 | tf_op jit(solution)/shard_map/ppermute | solution.py:34
  44.6 24.7 %collective-permute-start.34 = (bf16[97,32,128]{2,1,0:T(8,128)(2,1)}, bf16[97,32,128]{2,1,0:T(8,128)(2,1)S(1)}, u32[]{:S(2)}, u32[]{:S(2)}) collective-permute-start(bf16[97,32,128]{2,1,0:T(8,128)(2,1)} %constant_dynamic-update-slice_fusion.2), channel_id=1, source_target_pairs={{0,1},{1,2},{2,3},{3,0},{4,5},{5,6},{6,7},{7,4},{8,9},{9,10},{10,1... | collective-permute-start | bytes 2383880 | tf_op jit(solution)/shard_map/ppermute | solution.py:34
  47.3 25.6 %collective-permute-start.37 = (bf16[97,32,128]{2,1,0:T(8,128)(2,1)}, bf16[97,32,128]{2,1,0:T(8,128)(2,1)S(1)}, u32[]{:S(2)}, u32[]{:S(2)}) collective-permute-start(bf16[97,32,128]{2,1,0:T(8,128)(2,1)} %constant_dynamic-update-slice_fusion), channel_id=1, source_target_pairs={{0,12},{1,13},{2,14},{3,15},{4,0},{5,1},{6,2},{7,3},{8,4},{9,5},{1... | collective-permute-start | bytes 2383880 | tf_op jit(solution)/shard_map/ppermute | solution.py:29
  50.0 25.1 %collective-permute-start.36 = (bf16[97,32,128]{2,1,0:T(8,128)(2,1)}, bf16[97,32,128]{2,1,0:T(8,128)(2,1)S(1)}, u32[]{:S(2)}, u32[]{:S(2)}) collective-permute-start(bf16[97,32,128]{2,1,0:T(8,128)(2,1)} %constant_dynamic-update-slice_fusion), channel_id=1, source_target_pairs={{0,4},{1,5},{2,6},{3,7},{4,8},{5,9},{6,10},{7,11},{8,12},{9,13},{1... | collective-permute-start | bytes 2383880 | tf_op jit(solution)/shard_map/ppermute | solution.py:29
  58.7 18.8 %collective-permute-start.30 = (bf16[32,32,128]{2,1,0:T(8,128)(2,1)S(1)}, bf16[32,32,128]{2,1,0:T(8,128)(2,1)}, u32[]{:S(2)}, u32[]{:S(2)}) collective-permute-start(bf16[32,32,128]{2,1,0:T(8,128)(2,1)S(1)} %pad_maximum_fusion.1.own), channel_id=1, source_target_pairs={{0,2},{1,3},{2,0},{3,1},{4,6},{5,7},{6,4},{7,5},{8,10},{9,11},{10,... | collective-permute-start | bytes 786440 | tf_op jit(solution)/shard_map/ppermute | solution.py:34
  66.0 11.5 %collective-permute-start.31 = (bf16[32,32,128]{2,1,0:T(8,128)(2,1)}, bf16[32,32,128]{2,1,0:T(8,128)(2,1)}, u32[]{:S(2)}, u32[]{:S(2)}) collective-permute-start(bf16[32,32,128]{2,1,0:T(8,128)(2,1)} %pad_maximum_fusion.2.own), channel_id=1, source_target_pairs={{0,8},{1,9},{2,10},{3,11},{4,12},{5,13},{6,14},{7,15},{8,0},{9,1},... | collective-permute-start | bytes 786440 | tf_op jit(solution)/shard_map/ppermute | solution.py:29
  69.0 6.1 %copy-start.7 = (bf16[65,32,128]{2,1,0:T(8,128)(2,1)S(1)}, bf16[65,32,128]{2,1,0:T(8,128)(2,1)}, u32[]{:S(2)}) copy-start(bf16[65,32,128]{2,1,0:T(8,128)(2,1)} %copy-done.6) | copy-start | bytes 1597444
  79.9 16.3 %collective-permute-start.38 = (bf16[104,16,128]{2,1,0:T(8,128)(2,1)S(1)}, bf16[104,16,128]{2,1,0:T(8,128)(2,1)S(1)}, u32[]{:S(2)}, u32[]{:S(2)}) collective-permute-start(bf16[104,16,128]{2,1,0:T(8,128)(2,1)S(1)} %get-tuple-element.162), channel_id=1, source_target_pairs={{0,4},{1,5},{2,6},{3,7},{4,8},{5,9},{6,10},{7,11},{8,12},{9,13},{1... | collective-permute-start | bytes 1277960 | tf_op jit(solution)/shard_map/ppermute | solution.py:29
  80.0 17.8 %collective-permute-start.39 = (bf16[104,16,128]{2,1,0:T(8,128)(2,1)S(1)}, bf16[104,16,128]{2,1,0:T(8,128)(2,1)S(1)}, u32[]{:S(2)}, u32[]{:S(2)}) collective-permute-start(bf16[104,16,128]{2,1,0:T(8,128)(2,1)S(1)} %get-tuple-element.163), channel_id=1, source_target_pairs={{0,8},{1,9},{2,10},{3,11},{4,12},{5,13},{6,14},{7,15},{8,0},{9,1},... | collective-permute-start | bytes 1277960 | tf_op jit(solution)/shard_map/ppermute | solution.py:29
  82.0 15.8 %collective-permute-start.40 = (bf16[104,16,128]{2,1,0:T(8,128)(2,1)S(1)}, bf16[104,16,128]{2,1,0:T(8,128)(2,1)S(1)}, u32[]{:S(2)}, u32[]{:S(2)}) collective-permute-start(bf16[104,16,128]{2,1,0:T(8,128)(2,1)S(1)} %get-tuple-element.164), channel_id=1, source_target_pairs={{0,12},{1,13},{2,14},{3,15},{4,0},{5,1},{6,2},{7,3},{8,4},{9,5},{1... | collective-permute-start | bytes 1277960 | tf_op jit(solution)/shard_map/ppermute | solution.py:29
  85.9 15.0 %collective-permute-start.41 = (bf16[104,16,128]{2,1,0:T(8,128)(2,1)S(1)}, bf16[104,16,128]{2,1,0:T(8,128)(2,1)S(1)}, u32[]{:S(2)}, u32[]{:S(2)}) collective-permute-start(bf16[104,16,128]{2,1,0:T(8,128)(2,1)S(1)} %get-tuple-element.172), channel_id=1, source_target_pairs={{0,1},{1,2},{2,3},{3,0},{4,5},{5,6},{6,7},{7,4},{8,9},{9,10},{10,1... | collective-permute-start | bytes 1277960 | tf_op jit(solution)/shard_map/ppermute | solution.py:34
  89.5 11.4 %collective-permute-start.42 = (bf16[104,16,128]{2,1,0:T(8,128)(2,1)S(1)}, bf16[104,16,128]{2,1,0:T(8,128)(2,1)S(1)}, u32[]{:S(2)}, u32[]{:S(2)}) collective-permute-start(bf16[104,16,128]{2,1,0:T(8,128)(2,1)S(1)} %get-tuple-element.173), channel_id=1, source_target_pairs={{0,2},{1,3},{2,0},{3,1},{4,6},{5,7},{6,4},{7,5},{8,10},{9,11},{10,... | collective-permute-start | bytes 1277960 | tf_op jit(solution)/shard_map/ppermute | solution.py:34
  96.2 9.3 %collective-permute-start.43 = (bf16[104,16,128]{2,1,0:T(8,128)(2,1)S(1)}, bf16[104,16,128]{2,1,0:T(8,128)(2,1)S(1)}, u32[]{:S(2)}, u32[]{:S(2)}) collective-permute-start(bf16[104,16,128]{2,1,0:T(8,128)(2,1)S(1)} %get-tuple-element.174), channel_id=1, source_target_pairs={{0,3},{1,0},{2,1},{3,2},{4,7},{5,4},{6,5},{7,6},{8,11},{9,8},{10,9... | collective-permute-start | bytes 1277960 | tf_op jit(solution)/shard_map/ppermute | solution.py:34
  (10 other events, 21.8 us)

commit v5 on v4

--- a/solution.py
+++ b/solution.py
@@ -515,14 +515,13 @@
     arrived = scattered(parts_x, parts_y)
     density = gather_up(total(0, arrived[:4]), arrived[4:], places)
 
-    def again(density, coef, halo, *rest):
-        return any_way(coef, halo, *rest)
+    def again(density, coef, low, high, *rest):
+        return any_way(coef, jnp.concatenate([low, high], axis=0), *rest)
 
     def keep(density, *rest):
         return density
 
-    halo = jnp.concatenate([half_y, half_x], axis=0)
-    return lax.cond(over[0, 0] > 0, again, keep, density, coef, halo, here, block_ref, count)
+    return lax.cond(over[0, 0] > 0, again, keep, density, coef, half_y, half_x, here, block_ref, count)
 
 
 def solution(mesh):

time: 109 us -> 109 us (level)
  no operation moved by 1% of the time
where the time goes in v5:
time: 109 us
  Pallas kernels  33.3 us (31%)
  waiting for transfers between devices  31.9 us (29%)
  starting transfers between devices  31.5 us (29%)
  local copies, waits for them, and re-layouts  9.58 us (9%)
  other arithmetic  1.52 us (1%)
    ppermute x7, waiting for transfers between devices, along_y(): return lax.ppermute(value, 'st', pairs)  17 us
    ppermute x7, starting transfers between devices, along_x(): return lax.ppermute(value, 'st', pairs)  12.3 us
    ppermute x8, starting transfers between devices, along_dom(): return lax.ppermute(value, 'dom', [(i, (i + by) % 16) for i in range(16)])  10.1 us
    ppermute x7, starting transfers between devices, along_y(): return lax.ppermute(value, 'st', pairs)  9.19 us
    ppermute x7, waiting for transfers between devices, along_x(): return lax.ppermute(value, 'st', pairs)  9.16 us
    pallas_call x1, Pallas kernels, coef_all(): pl.pallas_call(kernel, grid=(64 // ROWS,), out_shape=[jax.ShapeDtypeStruc...  8.49 us
    pallas_call x1, Pallas kernels, plan(): pl.pallas_call(kernel, out_shape=[jax.ShapeDtypeStruct((2, LIST + 1), jnp...  7.93 us
    unnamed x25, local copies, waits for them, and re-layouts  6.2 us
  transfers between devices with their start and end apart: 22, of which 12 were waited for; matrix products, arithmetic and copies ran while one was open for 5% of the time, Pallas kernels for 17%

profile of v5, /device:TPU:24, one launch (start us, length us, event | category | flops | bytes accessed | tf_op | source)
XLA Modules:
  0.0 108.6 jit_solution(12937531113751516591)
XLA Ops:
  2.4 5.9 %collective-permute-start.22 = (bf16[16,32,128]{2,1,0:T(8,128)(2,1)S(1)}, bf16[16,32,128]{2,1,0:T(8,128)(2,1)S(1)}, u32[]{:S(2)}, u32[]{:S(2)}) collective-permute-start(bf16[16,32,128]{2,1,0:T(8,128)(2,1)S(1)} %get-tuple-element.137), channel_id=1, source_target_pairs={{0,224},{16,240},{32,0},{48,16},{64,32},{80,48},{96,64},{112,80},{... | collective-permute-start | bytes 393224 | tf_op jit(solution)/shard_map/ppermute | solution.py:24
  12.1 3.3 %coef_own.1.first_ref = f32[64,32,128]{2,1,0:T(8,128)S(1)} custom-call(s32[64,8]{1,0:T(8,128)S(1)} %copy.17.ref_ref, bf16[64,8,128,128]{3,2,1,0:T(8,128)(2,1)} %blocks_3.1, bf16[32,8192]{1,0:T(8,128)(2,1)S(1)} %copy-done.1), custom_call_target="tpu_custom_call" | custom-call | flops 134217728 | bytes 6291456 | tf_op jit(solution)/shard_map/coef_own/pallas_call | solution.py:78
  16.5 8.5 %coef_all.1 = (bf16[65,32,128]{2,1,0:T(8,128)(2,1)S(1)}, bf16[97,32,128]{2,1,0:T(8,128)(2,1)}, bf16[97,32,128]{2,1,0:T(8,128)(2,1)}, bf16[16,32,128]{2,1,0:T(8,1...) custom-call(s32[64,8]{1,0:T(8,128)S(1)} %copy.17.ref_ref, ...), custom_call_target="tpu_custom_call" | custom-call | flops 402653184 | bytes 14680064 | tf_op jit(solution)/shard_map/coef_all/pallas_call | solution.py:139
  24.9 1.6 %collective-permute-start.26 = (bf16[16,32,128]{2,1,0:T(8,128)(2,1)S(1)}, bf16[16,32,128]{2,1,0:T(8,128)(2,1)S(1)}, u32[]{:S(2)}, u32[]{:S(2)}) collective-permute-start(bf16[16,32,128]{2,1,0:T(8,128)(2,1)S(1)} %get-tuple-element.141), channel_id=1, source_target_pairs={{0,224},{16,240},{32,0},{48,16},{64,32},{80,48},{96,64},{112,80},{... | collective-permute-start | bytes 393224 | tf_op jit(solution)/shard_map/ppermute | solution.py:24
  27.8 3.0 %collective-permute-start.32 = (bf16[65,32,128]{2,1,0:T(8,128)(2,1)S(1)}, bf16[65,32,128]{2,1,0:T(8,128)(2,1)S(1)}, u32[]{:S(2)}, u32[]{:S(2)}) collective-permute-start(bf16[65,32,128]{2,1,0:T(8,128)(2,1)S(1)} %get-tuple-element.149.own), channel_id=1, source_target_pairs={{0,8},{1,9},{2,10},{3,11},{4,12},{5,13},{6,14},{7,15},{8,0},{9,1},... | collective-permute-start | bytes 1597448 | tf_op jit(solution)/shard_map/ppermute | solution.py:29
  34.3 3.1 %collective-permute-done.28 = bf16[16,32,128]{2,1,0:T(8,128)(2,1)S(1)} collective-permute-done((bf16[16,32,128]{2,1,0:T(8,128)(2,1)S(1)}, bf16[16,32,128]{2,1,0:T(8,128)(2,1)S(1)}, u32[]{:S(2)}, u32[]{:S(2)}) %collective-permute-start.28) | collective-permute-done | bytes 131104 | tf_op jit(solution)/shard_map/ppermute | solution.py:24
  39.5 2.8 %collective-permute-done.33.far = bf16[65,32,128]{2,1,0:T(8,128)(2,1)S(1)} collective-permute-done((bf16[65,32,128]{2,1,0:T(8,128)(2,1)S(1)}, bf16[65,32,128]{2,1,0:T(8,128)(2,1)S(1)}, u32[]{:S(2)}, u32[]{:S(2)}) %collective-permute-start.33) | collective-permute-done | bytes 532512 | tf_op jit(solution)/shard_map/ppermute | solution.py:34
  44.6 2.7 %collective-permute-start.34 = (bf16[97,32,128]{2,1,0:T(8,128)(2,1)}, bf16[97,32,128]{2,1,0:T(8,128)(2,1)S(1)}, u32[]{:S(2)}, u32[]{:S(2)}) collective-permute-start(bf16[97,32,128]{2,1,0:T(8,128)(2,1)} %constant_dynamic-update-slice_fusion.4), channel_id=1, source_target_pairs={{0,1},{1,2},{2,3},{3,0},{4,5},{5,6},{6,7},{7,4},{8,9},{9,10},{10,1... | collective-permute-start | bytes 2383880 | tf_op jit(solution)/shard_map/ppermute | solution.py:34
  47.3 2.8 %collective-permute-start.37 = (bf16[97,32,128]{2,1,0:T(8,128)(2,1)}, bf16[97,32,128]{2,1,0:T(8,128)(2,1)S(1)}, u32[]{:S(2)}, u32[]{:S(2)}) collective-permute-start(bf16[97,32,128]{2,1,0:T(8,128)(2,1)} %constant_dynamic-update-slice_fusion.2), channel_id=1, source_target_pairs={{0,12},{1,13},{2,14},{3,15},{4,0},{5,1},{6,2},{7,3},{8,4},{9,5},{1... | collective-permute-start | bytes 2383880 | tf_op jit(solution)/shard_map/ppermute | solution.py:29
  50.0 7.9 %plan.1 = (s32[2,145]{1,0:T(2,128)S(1)}, s32[64,8]{1,0:T(8,128)S(1)}, s32[1,1]{1,0:T(1,128)}) custom-call(s32[64,8]{1,0:T(8,128)S(1)} %copy.17.ref_ref, s32[1,64]{1,0:T(1,128)S(1)} %bitcast.9), custom_call_target="tpu_custom_call" | custom-call | bytes 25165824 | tf_op jit(solution)/shard_map/plan/pallas_call | solution.py:338
  60.5 5.5 %collective-permute-done.35.higher = bf16[97,32,128]{2,1,0:T(8,128)(2,1)S(1)} collective-permute-done((bf16[97,32,128]{2,1,0:T(8,128)(2,1)}, bf16[97,32,128]{2,1,0:T(8,128)(2,1)S(1)}, u32[]{:S(2)}, u32[]{:S(2)}) %collective-permute-start.35) | collective-permute-done | bytes 794656 | tf_op jit(solution)/shard_map/ppermute | solution.py:34
  66.0 3.0 %collective-permute-start.31 = (bf16[32,32,128]{2,1,0:T(8,128)(2,1)}, bf16[32,32,128]{2,1,0:T(8,128)(2,1)S(1)}, u32[]{:S(2)}, u32[]{:S(2)}) collective-permute-start(bf16[32,32,128]{2,1,0:T(8,128)(2,1)} %pad_maximum_fusion.1.own), channel_id=1, source_target_pairs={{0,8},{1,9},{2,10},{3,11},{4,12},{5,13},{6,14},{7,15},{8,0},{9,1},... | collective-permute-start | bytes 786440 | tf_op jit(solution)/shard_map/ppermute | solution.py:29
  70.4 2.4 %weigh_0.1 = (bf16[64,32,128]{2,1,0:T(8,128)(2,1)S(1)}, f32[32,16,128]{2,1,0:T(8,128)S(1)}, bf16[32,16,128]{2,1,0:T(8,128)(2,1)S(1)}, bf16[32,16,128]{2,1,0:T(8,128)(2,1)S(1)}, bf16[32,16,128]{2,1,0:T(8,128)(2,1)S(1)}) custom-call(s32[2]{0:T(128)S(1)} %pad_add_fusion.here_ref, s32[64,8]{1,0:T(8,128)S(1)} %copy.17.ref_ref, bf16[65,32,128]{2,1,0:T(8,128)(2,1)} %copy-done.18, ...), custom_call_target="tpu_custom_call" | custom-call | flops 67108864 | bytes 4194304 | tf_op jit(solution)/shard_map/weigh_0/pallas_call | solution.py:379
  72.9 2.3 %collective-permute-done.36.lower = bf16[97,32,128]{2,1,0:T(8,128)(2,1)S(1)} collective-permute-done((bf16[97,32,128]{2,1,0:T(8,128)(2,1)}, bf16[97,32,128]{2,1,0:T(8,128)(2,1)S(1)}, u32[]{:S(2)}, u32[]{:S(2)}) %collective-permute-start.36) | collective-permute-done | bytes 794656 | tf_op jit(solution)/shard_map/ppermute | solution.py:29
  75.1 2.4 %weigh_1.1 = (bf16[64,32,128]{2,1,0:T(8,128)(2,1)S(1)}, f32[32,16,128]{2,1,0:T(8,128)S(1)}, bf16[32,16,128]{2,1,0:T(8,128)(2,1)S(1)}, bf16[32,16,128]{2,1,0:T(8,128)(2,1)S(1)}, bf16[32,16,128]{2,1,0:T(8,128)(2,1)S(1)}) custom-call(s32[2]{0:T(128)S(1)} %pad_add_fusion.here_ref, s32[64,8]{1,0:T(8,128)S(1)} %copy.17.ref_ref, ...), custom_call_target="tpu_custom_call" | custom-call | flops 67108864 | bytes 4194304 | tf_op jit(solution)/shard_map/weigh_1/pallas_call | solution.py:379
  77.5 2.5 %density_list_0.1 = (f32[104,16,128]{2,1,0:T(8,128)S(1)}, bf16[104,16,128]{2,1,0:T(8,128)(2,1)S(1)}, bf16[104,16,128]{2,1,0:T(8,128)(2,1)S(1)}, bf16[104,16,128]{2,1,0:T(8,128)(2,1)S(1)}) custom-call(s32[2,145]{1,0:T(2,128)S(1)} %get-tuple-element.146.entry_ref, bf16[64,32,128]{2,1,0:T(8,128)(2,1)S(1)} %get-tuple-element.158.w_ref, ...), custom_call_target="tpu_custom_call" | custom-call | flops 150994944 | bytes 4194304 | tf_op jit(solution)/shard_map/density_list_0/pallas_call | solution.py:411
  80.1 2.0 %collective-permute-start.39 = (bf16[104,16,128]{2,1,0:T(8,128)(2,1)S(1)}, bf16[104,16,128]{2,1,0:T(8,128)(2,1)S(1)}, u32[]{:S(2)}, u32[]{:S(2)}) collective-permute-start(bf16[104,16,128]{2,1,0:T(8,128)(2,1)S(1)} %get-tuple-element.166), channel_id=1, source_target_pairs={{0,8},{1,9},{2,10},{3,11},{4,12},{5,13},{6,14},{7,15},{8,0},{9,1},... | collective-permute-start | bytes 1277960 | tf_op jit(solution)/shard_map/ppermute | solution.py:29
  82.1 1.4 %collective-permute-start.40 = (bf16[104,16,128]{2,1,0:T(8,128)(2,1)S(1)}, bf16[104,16,128]{2,1,0:T(8,128)(2,1)S(1)}, u32[]{:S(2)}, u32[]{:S(2)}) collective-permute-start(bf16[104,16,128]{2,1,0:T(8,128)(2,1)S(1)} %get-tuple-element.167), channel_id=1, source_target_pairs={{0,12},{1,13},{2,14},{3,15},{4,0},{5,1},{6,2},{7,3},{8,4},{9,5},{1... | collective-permute-start | bytes 1277960 | tf_op jit(solution)/shard_map/ppermute | solution.py:29
  83.5 2.4 %density_list_1.1 = (f32[104,16,128]{2,1,0:T(8,128)S(1)}, bf16[104,16,128]{2,1,0:T(8,128)(2,1)S(1)}, bf16[104,16,128]{2,1,0:T(8,128)(2,1)S(1)}, bf16[104,16,128]{2,1,0:T(8,128)(2,1)S(1)}) custom-call(s32[2,145]{1,0:T(2,128)S(1)} %get-tuple-element.146.entry_ref, bf16[64,32,128]{2,1,0:T(8,128)(2,1)S(1)} %get-tuple-element.168.w_ref, ...), custom_call_target="tpu_custom_call" | custom-call | flops 150994944 | bytes 4194304 | tf_op jit(solution)/shard_map/density_list_1/pallas_call | solution.py:411
  85.9 3.6 %collective-permute-start.41 = (bf16[104,16,128]{2,1,0:T(8,128)(2,1)S(1)}, bf16[104,16,128]{2,1,0:T(8,128)(2,1)S(1)}, u32[]{:S(2)}, u32[]{:S(2)}) collective-permute-start(bf16[104,16,128]{2,1,0:T(8,128)(2,1)S(1)} %get-tuple-element.175), channel_id=1, source_target_pairs={{0,1},{1,2},{2,3},{3,0},{4,5},{5,6},{6,7},{7,4},{8,9},{9,10},{10,1... | collective-permute-start | bytes 1277960 | tf_op jit(solution)/shard_map/ppermute | solution.py:34
  89.5 6.7 %collective-permute-done.38.first = bf16[104,16,128]{2,1,0:T(8,128)(2,1)S(1)} collective-permute-done((bf16[104,16,128]{2,1,0:T(8,128)(2,1)S(1)}, bf16[104,16,128]{2,1,0:T(8,128)(2,1)S(1)}, u32[]{:S(2)}, u32[]{:S(2)}) %collective-permute-start.38) | collective-permute-done | bytes 426016 | tf_op jit(solution)/shard_map/ppermute | solution.py:29
  97.1 3.8 %collective-permute-done.41.refs_2_ = bf16[104,16,128]{2,1,0:T(8,128)(2,1)S(1)} collective-permute-done((bf16[104,16,128]{2,1,0:T(8,128)(2,1)S(1)}, bf16[104,16,128]{2,1,0:T(8,128)(2,1)S(1)}, u32[]{:S(2)}, u32[]{:S(2)}) %collective-permute-start.41) | collective-permute-done | bytes 426016 | tf_op jit(solution)/shard_map/ppermute | solution.py:34
  100.9 4.7 %collective-permute-done.43.refs_4_ = bf16[104,16,128]{2,1,0:T(8,128)(2,1)S(1)} collective-permute-done((bf16[104,16,128]{2,1,0:T(8,128)(2,1)S(1)}, bf16[104,16,128]{2,1,0:T(8,128)(2,1)S(1)}, u32[]{:S(2)}, u32[]{:S(2)}) %collective-permute-start.43) | collective-permute-done | bytes 426016 | tf_op jit(solution)/shard_map/ppermute | solution.py:34
  105.6 3.0 %gather_up.1 = f32[64,8,8,128]{3,2,1,0:T(8,128)} custom-call(s32[64,8]{1,0:T(8,128)S(1)} %get-tuple-element.136.place_ref, f32[208,8,128]{2,1,0:T(8,128)S(1)} %total_0.1.refs_0_, f32[104,16,128]{2,1,0:T(8,128)S(1)} %get-tuple-element.174.refs_1_, bf16[104,16,128]{2,1,0:T(8,128)(2,1)S(1)} %collective-permute-done.41.refs_2_, ...), custom_call_target="tpu_custom_call" | custom-call | bytes 7340032 | tf_op jit(solution)/shard_map/gather_up/pallas_call | solution.py:458
  (64 shorter events, 20.6 us)
Async XLA Ops:
  2.4 13.0 %collective-permute-start.22 = (bf16[16,32,128]{2,1,0:T(8,128)(2,1)S(1)}, bf16[16,32,128]{2,1,0:T(8,128)(2,1)S(1)}, u32[]{:S(2)}, u32[]{:S(2)}) collective-permute-start(bf16[16,32,128]{2,1,0:T(8,128)(2,1)S(1)} %get-tuple-element.137), channel_id=1, source_target_pairs={{0,224},{16,240},{32,0},{48,16},{64,32},{80,48},{96,64},{112,80},{... | collective-permute-start | bytes 393224 | tf_op jit(solution)/shard_map/ppermute | solution.py:24
  8.4 7.1 %collective-permute-start.23 = (bf16[16,32,128]{2,1,0:T(8,128)(2,1)S(1)}, bf16[16,32,128]{2,1,0:T(8,128)(2,1)S(1)}, u32[]{:S(2)}, u32[]{:S(2)}) collective-permute-start(bf16[16,32,128]{2,1,0:T(8,128)(2,1)S(1)} %get-tuple-element.138), channel_id=1, source_target_pairs={{0,240},{16,0},{32,16},{48,32},{64,48},{80,64},{96,80},{112,96},{1... | collective-permute-start | bytes 393224 | tf_op jit(solution)/shard_map/ppermute | solution.py:24
  8.5 6.9 %collective-permute-start.24 = (bf16[16,32,128]{2,1,0:T(8,128)(2,1)S(1)}, bf16[16,32,128]{2,1,0:T(8,128)(2,1)S(1)}, u32[]{:S(2)}, u32[]{:S(2)}) collective-permute-start(bf16[16,32,128]{2,1,0:T(8,128)(2,1)S(1)} %get-tuple-element.139), channel_id=1, source_target_pairs={{0,16},{16,32},{32,48},{48,64},{64,80},{80,96},{96,112},{112,128},... | collective-permute-start | bytes 393224 | tf_op jit(solution)/shard_map/ppermute | solution.py:24
  8.9 7.6 %collective-permute-start.25 = (bf16[16,32,128]{2,1,0:T(8,128)(2,1)S(1)}, bf16[16,32,128]{2,1,0:T(8,128)(2,1)S(1)}, u32[]{:S(2)}, u32[]{:S(2)}) collective-permute-start(bf16[16,32,128]{2,1,0:T(8,128)(2,1)S(1)} %get-tuple-element.140), channel_id=1, source_target_pairs={{0,32},{16,48},{32,64},{48,80},{64,96},{80,112},{96,128},{112,144}... | collective-permute-start | bytes 393224 | tf_op jit(solution)/shard_map/ppermute | solution.py:24
  24.9 41.1 %copy-start.18 = (bf16[65,32,128]{2,1,0:T(8,128)(2,1)}, bf16[65,32,128]{2,1,0:T(8,128)(2,1)S(1)}, u32[]{:S(2)}) copy-start(bf16[65,32,128]{2,1,0:T(8,128)(2,1)S(1)} %get-tuple-element.149.own) | copy-start | bytes 1597444
  24.9 6.3 %collective-permute-start.26 = (bf16[16,32,128]{2,1,0:T(8,128)(2,1)S(1)}, bf16[16,32,128]{2,1,0:T(8,128)(2,1)S(1)}, u32[]{:S(2)}, u32[]{:S(2)}) collective-permute-start(bf16[16,32,128]{2,1,0:T(8,128)(2,1)S(1)} %get-tuple-element.141), channel_id=1, source_target_pairs={{0,224},{16,240},{32,0},{48,16},{64,32},{80,48},{96,64},{112,80},{... | collective-permute-start | bytes 393224 | tf_op jit(solution)/shard_map/ppermute | solution.py:24
  26.5 15.8 %collective-permute-start.33 = (bf16[65,32,128]{2,1,0:T(8,128)(2,1)S(1)}, bf16[65,32,128]{2,1,0:T(8,128)(2,1)S(1)}, u32[]{:S(2)}, u32[]{:S(2)}) collective-permute-start(bf16[65,32,128]{2,1,0:T(8,128)(2,1)S(1)} %get-tuple-element.149.own), channel_id=1, source_target_pairs={{0,2},{1,3},{2,0},{3,1},{4,6},{5,7},{6,4},{7,5},{8,10},{9,11},{10,... | collective-permute-start | bytes 1597448 | tf_op jit(solution)/shard_map/ppermute | solution.py:34
  27.8 15.5 %collective-permute-start.32 = (bf16[65,32,128]{2,1,0:T(8,128)(2,1)S(1)}, bf16[65,32,128]{2,1,0:T(8,128)(2,1)S(1)}, u32[]{:S(2)}, u32[]{:S(2)}) collective-permute-start(bf16[65,32,128]{2,1,0:T(8,128)(2,1)S(1)} %get-tuple-element.149.own), channel_id=1, source_target_pairs={{0,8},{1,9},{2,10},{3,11},{4,12},{5,13},{6,14},{7,15},{8,0},{9,1},... | collective-permute-start | bytes 1597448 | tf_op jit(solution)/shard_map/ppermute | solution.py:29
  30.8 2.8 %collective-permute-start.27 = (bf16[16,32,128]{2,1,0:T(8,128)(2,1)S(1)}, bf16[16,32,128]{2,1,0:T(8,128)(2,1)S(1)}, u32[]{:S(2)}, u32[]{:S(2)}) collective-permute-start(bf16[16,32,128]{2,1,0:T(8,128)(2,1)S(1)} %get-tuple-element.142), channel_id=1, source_target_pairs={{0,240},{16,0},{32,16},{48,32},{64,48},{80,64},{96,80},{112,96},{1... | collective-permute-start | bytes 393224 | tf_op jit(solution)/shard_map/ppermute | solution.py:24
  31.1 6.2 %collective-permute-start.28 = (bf16[16,32,128]{2,1,0:T(8,128)(2,1)S(1)}, bf16[16,32,128]{2,1,0:T(8,128)(2,1)S(1)}, u32[]{:S(2)}, u32[]{:S(2)}) collective-permute-start(bf16[16,32,128]{2,1,0:T(8,128)(2,1)S(1)} %get-tuple-element.143), channel_id=1, source_target_pairs={{0,16},{16,32},{32,48},{48,64},{64,80},{80,96},{96,112},{112,128},... | collective-permute-start | bytes 393224 | tf_op jit(solution)/shard_map/ppermute | solution.py:24
  31.3 7.5 %collective-permute-start.29 = (bf16[16,32,128]{2,1,0:T(8,128)(2,1)S(1)}, bf16[16,32,128]{2,1,0:T(8,128)(2,1)S(1)}, u32[]{:S(2)}, u32[]{:S(2)}) collective-permute-start(bf16[16,32,128]{2,1,0:T(8,128)(2,1)S(1)} %get-tuple-element.144), channel_id=1, source_target_pairs={{0,32},{16,48},{32,64},{48,80},{64,96},{80,112},{96,128},{112,144}... | collective-permute-start | bytes 393224 | tf_op jit(solution)/shard_map/ppermute | solution.py:24
  44.0 22.0 %collective-permute-start.35 = (bf16[97,32,128]{2,1,0:T(8,128)(2,1)}, bf16[97,32,128]{2,1,0:T(8,128)(2,1)S(1)}, u32[]{:S(2)}, u32[]{:S(2)}) collective-permute-start(bf16[97,32,128]{2,1,0:T(8,128)(2,1)} %constant_dynamic-update-slice_fusion.4), channel_id=1, source_target_pairs={{0,3},{1,0},{2,1},{3,2},{4,7},{5,4},{6,5},{7,6},{8,11},{9,8},{10,9... | collective-permute-start | bytes 2383880 | tf_op jit(solution)/shard_map/ppermute | solution.py:34
  44.6 24.7 %collective-permute-start.34 = (bf16[97,32,128]{2,1,0:T(8,128)(2,1)}, bf16[97,32,128]{2,1,0:T(8,128)(2,1)S(1)}, u32[]{:S(2)}, u32[]{:S(2)}) collective-permute-start(bf16[97,32,128]{2,1,0:T(8,128)(2,1)} %constant_dynamic-update-slice_fusion.4), channel_id=1, source_target_pairs={{0,1},{1,2},{2,3},{3,0},{4,5},{5,6},{6,7},{7,4},{8,9},{9,10},{10,1... | collective-permute-start | bytes 2383880 | tf_op jit(solution)/shard_map/ppermute | solution.py:34
  47.3 25.6 %collective-permute-start.37 = (bf16[97,32,128]{2,1,0:T(8,128)(2,1)}, bf16[97,32,128]{2,1,0:T(8,128)(2,1)S(1)}, u32[]{:S(2)}, u32[]{:S(2)}) collective-permute-start(bf16[97,32,128]{2,1,0:T(8,128)(2,1)} %constant_dynamic-update-slice_fusion.2), channel_id=1, source_target_pairs={{0,12},{1,13},{2,14},{3,15},{4,0},{5,1},{6,2},{7,3},{8,4},{9,5},{1... | collective-permute-start | bytes 2383880 | tf_op jit(solution)/shard_map/ppermute | solution.py:29
  50.0 25.1 %collective-permute-start.36 = (bf16[97,32,128]{2,1,0:T(8,128)(2,1)}, bf16[97,32,128]{2,1,0:T(8,128)(2,1)S(1)}, u32[]{:S(2)}, u32[]{:S(2)}) collective-permute-start(bf16[97,32,128]{2,1,0:T(8,128)(2,1)} %constant_dynamic-update-slice_fusion.2), channel_id=1, source_target_pairs={{0,4},{1,5},{2,6},{3,7},{4,8},{5,9},{6,10},{7,11},{8,12},{9,13},{1... | collective-permute-start | bytes 2383880 | tf_op jit(solution)/shard_map/ppermute | solution.py:29
  59.4 18.1 %collective-permute-start.30 = (bf16[32,32,128]{2,1,0:T(8,128)(2,1)}, bf16[32,32,128]{2,1,0:T(8,128)(2,1)}, u32[]{:S(2)}, u32[]{:S(2)}) collective-permute-start(bf16[32,32,128]{2,1,0:T(8,128)(2,1)} %pad_maximum_fusion.own), channel_id=1, source_target_pairs={{0,2},{1,3},{2,0},{3,1},{4,6},{5,7},{6,4},{7,5},{8,10},{9,11},{10,... | collective-permute-start | bytes 786440 | tf_op jit(solution)/shard_map/ppermute | solution.py:34
  66.0 11.5 %collective-permute-start.31 = (bf16[32,32,128]{2,1,0:T(8,128)(2,1)}, bf16[32,32,128]{2,1,0:T(8,128)(2,1)S(1)}, u32[]{:S(2)}, u32[]{:S(2)}) collective-permute-start(bf16[32,32,128]{2,1,0:T(8,128)(2,1)} %pad_maximum_fusion.1.own), channel_id=1, source_target_pairs={{0,8},{1,9},{2,10},{3,11},{4,12},{5,13},{6,14},{7,15},{8,0},{9,1},... | collective-permute-start | bytes 786440 | tf_op jit(solution)/shard_map/ppermute | solution.py:29
  69.0 6.1 %copy-start.9 = (bf16[65,32,128]{2,1,0:T(8,128)(2,1)S(1)}, bf16[65,32,128]{2,1,0:T(8,128)(2,1)}, u32[]{:S(2)}) copy-start(bf16[65,32,128]{2,1,0:T(8,128)(2,1)} %copy-done.8) | copy-start | bytes 1597444
  80.0 16.3 %collective-permute-start.38 = (bf16[104,16,128]{2,1,0:T(8,128)(2,1)S(1)}, bf16[104,16,128]{2,1,0:T(8,128)(2,1)S(1)}, u32[]{:S(2)}, u32[]{:S(2)}) collective-permute-start(bf16[104,16,128]{2,1,0:T(8,128)(2,1)S(1)} %get-tuple-element.165), channel_id=1, source_target_pairs={{0,4},{1,5},{2,6},{3,7},{4,8},{5,9},{6,10},{7,11},{8,12},{9,13},{1... | collective-permute-start | bytes 1277960 | tf_op jit(solution)/shard_map/ppermute | solution.py:29
  80.1 16.8 %collective-permute-start.39 = (bf16[104,16,128]{2,1,0:T(8,128)(2,1)S(1)}, bf16[104,16,128]{2,1,0:T(8,128)(2,1)S(1)}, u32[]{:S(2)}, u32[]{:S(2)}) collective-permute-start(bf16[104,16,128]{2,1,0:T(8,128)(2,1)S(1)} %get-tuple-element.166), channel_id=1, source_target_pairs={{0,8},{1,9},{2,10},{3,11},{4,12},{5,13},{6,14},{7,15},{8,0},{9,1},... | collective-permute-start | bytes 1277960 | tf_op jit(solution)/shard_map/ppermute | solution.py:29
  82.1 14.8 %collective-permute-start.40 = (bf16[104,16,128]{2,1,0:T(8,128)(2,1)S(1)}, bf16[104,16,128]{2,1,0:T(8,128)(2,1)S(1)}, u32[]{:S(2)}, u32[]{:S(2)}) collective-permute-start(bf16[104,16,128]{2,1,0:T(8,128)(2,1)S(1)} %get-tuple-element.167), channel_id=1, source_target_pairs={{0,12},{1,13},{2,14},{3,15},{4,0},{5,1},{6,2},{7,3},{8,4},{9,5},{1... | collective-permute-start | bytes 1277960 | tf_op jit(solution)/shard_map/ppermute | solution.py:29
  85.9 15.0 %collective-permute-start.41 = (bf16[104,16,128]{2,1,0:T(8,128)(2,1)S(1)}, bf16[104,16,128]{2,1,0:T(8,128)(2,1)S(1)}, u32[]{:S(2)}, u32[]{:S(2)}) collective-permute-start(bf16[104,16,128]{2,1,0:T(8,128)(2,1)S(1)} %get-tuple-element.175), channel_id=1, source_target_pairs={{0,1},{1,2},{2,3},{3,0},{4,5},{5,6},{6,7},{7,4},{8,9},{9,10},{10,1... | collective-permute-start | bytes 1277960 | tf_op jit(solution)/shard_map/ppermute | solution.py:34
  89.5 11.4 %collective-permute-start.42 = (bf16[104,16,128]{2,1,0:T(8,128)(2,1)S(1)}, bf16[104,16,128]{2,1,0:T(8,128)(2,1)S(1)}, u32[]{:S(2)}, u32[]{:S(2)}) collective-permute-start(bf16[104,16,128]{2,1,0:T(8,128)(2,1)S(1)} %get-tuple-element.176), channel_id=1, source_target_pairs={{0,2},{1,3},{2,0},{3,1},{4,6},{5,7},{6,4},{7,5},{8,10},{9,11},{10,... | collective-permute-start | bytes 1277960 | tf_op jit(solution)/shard_map/ppermute | solution.py:34
  96.3 9.3 %collective-permute-start.43 = (bf16[104,16,128]{2,1,0:T(8,128)(2,1)S(1)}, bf16[104,16,128]{2,1,0:T(8,128)(2,1)S(1)}, u32[]{:S(2)}, u32[]{:S(2)}) collective-permute-start(bf16[104,16,128]{2,1,0:T(8,128)(2,1)S(1)} %get-tuple-element.177), channel_id=1, source_target_pairs={{0,3},{1,0},{2,1},{3,2},{4,7},{5,4},{6,5},{7,6},{8,11},{9,8},{10,9... | collective-permute-start | bytes 1277960 | tf_op jit(solution)/shard_map/ppermute | solution.py:34
  (10 other events, 21.8 us)
